TPU v7x, 32 devices: a whole 2x2x4 slice. The times are simulated.
32 devices in a mesh: replica: 2 (over y), fsdp: 16 (over z, x, core).
Axes of the slice: x: 2, y: 2, z: 4, core: 2. Of those that a mesh axis runs over, the one named last changes fastest.
Arguments:
- hidden_states: bfloat16 [8192, 8192], P(('replica', 'fsdp')), may hold values from -6 to 6
- key_weight: bfloat16 [8192, 1024], P('fsdp'), may hold values from -0.13258252 to 0.13258252
- previous_peak: float32 [1], replicated, may hold values from 0.088388346 to 0.12705825
- key_cotangent: bfloat16 [8192, 1024], P(('replica', 'fsdp')), may hold values from -6 to 6
Outputs:
- projected_keys: bfloat16 [8192, 1024], P(('replica', 'fsdp'))
- input_gradient: bfloat16 [8192, 8192], P(('replica', 'fsdp'))
- weight_gradient: bfloat16 [8192, 1024], P('fsdp')
- peak_ratio: float32 [1], replicated
All inputs are finite; a program needn't handle non-finite values.
Results may differ from a plain program's by a relative error of at most 0.025.
Values may be sent and summed in bfloat16 or wider, within the bound.
No kernel may reach another device: no remote copies, remote signals or barrier semaphores. Data moves between devices by JAX's collectives and lax.ppermute only.
A program may use at most 128 MiB of HBM per device.

v0:
```python
import jax
import jax.numpy as jnp
from jax import lax
from jax.sharding import PartitionSpec as P


def quantize(weight, limit):
    return jnp.clip(weight.astype(jnp.float32) * (448.0 / limit), -448.0, 448.0).astype(
        jnp.bfloat16
    )


def body(hidden_states, key_weight, previous_peak, key_cotangent):
    limit = previous_peak[0]
    unscale = limit / 448.0
    tok_rows = hidden_states.shape[0]
    source = quantize(key_weight, limit)
    local_peak = jnp.max(jnp.abs(key_weight.astype(jnp.float32)))
    peak = lax.pmax(local_peak, "fsdp")
    gathered = lax.all_gather(source, "fsdp", axis=0, tiled=True)
    keys_sum = jnp.dot(hidden_states, gathered, preferred_element_type=jnp.float32)
    grad_sum = lax.dot_general(
        key_cotangent, gathered, (((1,), (1,)), ((), ())), preferred_element_type=jnp.float32
    )
    projected_keys = (keys_sum * unscale).astype(jnp.bfloat16)
    input_gradient = (grad_sum * unscale).astype(jnp.bfloat16)
    group = lax.psum_scatter(
        lax.dot_general(
            hidden_states,
            key_cotangent,
            (((0,), (0,)), ((), ())),
            preferred_element_type=jnp.float32,
        ).astype(jnp.bfloat16),
        "fsdp",
        scatter_dimension=0,
        tiled=True,
    ).astype(jnp.float32)
    group = group.astype(jnp.bfloat16)
    total = lax.psum(group, "replica").astype(jnp.float32)
    token_count = tok_rows * lax.axis_size("replica") * lax.axis_size("fsdp")
    weight_gradient = (total * token_count ** (-0.5)).astype(jnp.bfloat16)
    peak_ratio = (peak / limit).reshape(1)
    return (projected_keys, input_gradient, weight_gradient, peak_ratio)


def solution(mesh):
    in_specs = (P(("replica", "fsdp"), None), P("fsdp", None), P(), P(("replica", "fsdp"), None))
    out_specs = (P(("replica", "fsdp"), None), P(("replica", "fsdp"), None), P("fsdp", None), P())
    return jax.shard_map(body, mesh=mesh, in_specs=in_specs, out_specs=out_specs, check_vma=False)
```

profile of v0, /device:TPU:0, one launch (start us, length us, event | category | flops | bytes accessed | tf_op | source)
XLA Modules:
  0.0 410.2 jit_solution(6583380183339231205)
XLA Ops:
  7.2 0.0 copy-start
  7.2 0.0 reduce-scatter.2.cloned.1.call-start
  7.2 1.0 copy-done
  8.2 10.5 %convolution_convert_fusion = bf16[8192,1024]{1,0:T(8,128)(2,1)} fusion(bf16[256,8192]{1,0:T(8,128)(2,1)} %param.4, bf16[256,1024]{1,0:T(8,128)(2,1)S(1)} %copy-done), kind=kOutput, calls=%fused_computation | convolution fusion | flops 4303355904 | bytes 21495808 | tf_op jit(solution)/shard_map/dot_general | solution.py:28
  18.7 0.0 copy-start.1
  18.7 0.0 reduce-scatter.2.cloned.1.call-update
  18.7 0.0 all-reduce.2.cloned.1.call-start
  18.8 181.3 %reduce-scatter.2.cloned.1.call-done = bf16[512,1024]{1,0:T(8,128)(2,1)} async-done(((bf16[8192,1024]{1,0:T(8,128)(2,1)}), bf16[512,1024]{1,0:T(8,128)(2,1)}) %reduce-scatter.2.cloned.1.call-update) | async-done | bytes 1048592 | tf_op jit(solution)/shard_map/reduce_scatter | solution.py:27
  200.1 0.0 all-reduce.2.cloned.1.call-update
  200.1 0.0 all-gather.2.cloned.1.call-start
  200.9 0.0 copy-done.1
  200.9 1.9 fusion.4
  202.7 0.0 all-gather.2.cloned.1.call-update
  202.8 32.3 %pmax.7 = f32[]{:T(128)} all-reduce(f32[]{:T(128)} %get-tuple-element.8), channel_id=1, replica_groups=mesh['replica'=2,'fsdp'=16] {'fsdp'}, use_global_device_ids=true, to_apply=%region_3.4 | all-reduce | flops 1 | bytes 8 | tf_op jit(solution)/shard_map/pmax | solution.py:19
  235.8 5.7 %all-reduce.2.cloned.1.call-done = bf16[512,1024]{1,0:T(8,128)(2,1)} async-done(((bf16[512,1024]{1,0:T(8,128)(2,1)}), bf16[512,1024]{1,0:T(8,128)(2,1)}) %all-reduce.2.cloned.1.call-update) | async-done | bytes 1048592 | tf_op jit(solution)/shard_map/psum | solution.py:39
  241.5 2.4 multiply_convert_fusion
  243.9 127.5 %all-gather.2.cloned.1.call-done = bf16[8192,1024]{1,0:T(8,128)(2,1)} async-done(((bf16[512,1024]{1,0:T(8,128)(2,1)}), bf16[8192,1024]{1,0:T(8,128)(2,1)}) %all-gather.2.cloned.1.call-update) | async-done | bytes 16777232 | tf_op jit(solution)/shard_map/all_gather | solution.py:20
  371.4 12.3 %fusion.1 = bf16[256,8192]{0,1:T(8,128)(2,1)} fusion(bf16[8192,1024]{1,0:T(8,128)(2,1)} %all-gather.2.cloned.1.call-done, bf16[256,1024]{1,0:T(8,128)(2,1)S(1)} %copy-done, f32[]{:T(128)S(6)} %div.10), kind=kOutput, calls=%fused_computation.3 | convolution fusion | flops 4299161600 | bytes 21495812 | tf_op jit(solution)/shard_map/dot_general | solution.py:22
  383.7 6.3 %copy.9 = bf16[256,8192]{1,0:T(8,128)(2,1)} copy(bf16[256,8192]{0,1:T(8,128)(2,1)} %fusion.1) | data formatting | bytes 8388608
  390.0 11.5 %fusion.6 = bf16[256,1024]{0,1:T(8,128)(2,1)S(1)} fusion(bf16[8192,1024]{1,0:T(8,128)(2,1)} %all-gather.2.cloned.1.call-done, bf16[256,8192]{1,0:T(8,128)(2,1)} %param.4, f32[]{:T(128)S(6)} %div.10), kind=kOutput, calls=%fused_computation.12 | convolution fusion | flops 4295491584 | bytes 21495812 | tf_op jit(solution)/shard_map/dot_general | solution.py:21
  401.5 1.0 copy.8
Async XLA Ops:
  7.2 1.0 copy-start
  7.2 192.9 %reduce-scatter.2.cloned.1.call-start = ((), (), s32[]{:S(2)}) async-start(), calls=%async_computation.2 | async-start | bytes 17825792 | tf_op jit(solution)/shard_map/reduce_scatter | solution.py:27
  18.7 182.2 %copy-start.1 = (bf16[512,1024]{1,0:T(8,128)(2,1)S(1)}, bf16[512,1024]{1,0:T(8,128)(2,1)}, u32[]{:S(2)}) copy-start(bf16[512,1024]{1,0:T(8,128)(2,1)} %param.5) | copy-start | bytes 3145732
  18.7 222.8 %all-reduce.2.cloned.1.call-start = ((), (), s32[]{:S(2)}) async-start(), calls=%async_computation.3 | async-start | bytes 2097152 | tf_op jit(solution)/shard_map/psum | solution.py:39
  200.1 171.2 %all-gather.2.cloned.1.call-start = ((), (), s32[]{:S(2)}) async-start(), calls=%async_computation.1 | async-start | bytes 17825792 | tf_op jit(solution)/shard_map/all_gather | solution.py:20
Sparse Core Ops, SparseCore 0:
  18.8 181.2 reduce-scatter.1
  202.4 39.0 all-reduce.1
  244.5 126.8 all-gather.1
where the time goes:
time: 411 us; the launch traced here: 410 us
  waiting for transfers between devices  315 us (77%)
  matrix products  34.3 us (8%)
  blocking collectives  32.3 us (8%)
  between operations  16.2 us (4%)
  local copies, waits for them, and re-layouts  8.31 us (2%)
  other arithmetic  4.27 us (1%)
    reduce_scatter x1, waiting for transfers between devices, body(): lax.psum_scatter(lax.dot_general(hidden_states, key_cotangent, (((0,), (0...  181 us
    all_gather x1, waiting for transfers between devices, body(): gathered = lax.all_gather(source, 'fsdp', axis=0, tiled=True)  127 us
    pmax x1, blocking collectives, body(): peak = lax.pmax(local_peak, 'fsdp')  32.3 us
    dot_general x1, matrix products, body(): lax.dot_general(key_cotangent, gathered, (((1,), (1,)), ((), ())), prefer...  12.3 us
    dot_general x1, matrix products, body(): jnp.dot(hidden_states, gathered, preferred_element_type=jnp.float32)  11.5 us
    dot_general x1, matrix products, body(): lax.dot_general(hidden_states, key_cotangent, (((0,), (0,)), ((), ())), p...  10.5 us
    unnamed x6, local copies, waits for them, and re-layouts  8.31 us
  transfers between devices with their start and end apart: 3, of which 3 were waited for; matrix products, arithmetic and copies ran while one was open for 1% of the time, Pallas kernels for 0%

commit v1 on v0

v1 whole, which is shorter than its diff:
```python
import functools

import jax
import jax.numpy as jnp
from jax import lax
from jax.experimental import pallas as pl
from jax.experimental.pallas import tpu as pltpu
from jax.sharding import Mesh
from jax.sharding import PartitionSpec as P

ANY = pl.BlockSpec(memory_space=pl.ANY)
SMEM = pl.BlockSpec(memory_space=pltpu.SMEM)
VMEM = pl.BlockSpec(memory_space=pltpu.VMEM)
PARAMS = pltpu.CompilerParams(vmem_limit_bytes=63 * 2**20)
CHEAP = pl.CostEstimate(flops=1, bytes_accessed=1, transcendentals=0)
F32, BF16 = jnp.float32, jnp.bfloat16


def quantize(weight, limit):
    return jnp.clip(weight.astype(F32) * (448.0 / limit), -448.0, 448.0).astype(BF16)


def swap(block, axis, mask=1):
    size = lax.axis_size(axis)
    return lax.ppermute(block, axis, [(i, i ^ mask) for i in range(size)])


def run(copies):
    for copy in copies:
        copy.start()
    for copy in copies:
        copy.wait()


def pack(core, hidden, rows, nz):
    tokens = hidden.shape[0]
    half = rows // 2
    group, blocks = 8, nz * 2

    def kernel(core_ref, hidden_ref, group_ref, other_ref, sem):
        copies = []
        for d in range(group):
            for k in range(nz):
                start = (k * 4 + d % 4) * rows + (d // 4) * half
                copies.append(
                    pltpu.make_async_copy(
                        hidden_ref.at[:, pl.ds(start, half)],
                        group_ref.at[d, :, pl.ds(k * half, half)],
                        sem.at[len(copies)],
                    )
                )
        for b in range(blocks):
            start = pl.multiple_of((b * 2 + 1 - core_ref[0]) * rows, rows)
            copies.append(
                pltpu.make_async_copy(
                    hidden_ref.at[:, pl.ds(start, rows)], other_ref.at[b], sem.at[len(copies)]
                )
            )
        run(copies)

    return pl.pallas_call(
        kernel,
        out_shape=[
            jax.ShapeDtypeStruct((group, tokens, nz * half), BF16),
            jax.ShapeDtypeStruct((blocks, tokens, rows), BF16),
        ],
        in_specs=[SMEM, ANY],
        out_specs=[VMEM, VMEM],
        scratch_shapes=[pltpu.SemaphoreType.DMA((group * nz + blocks,))],
        compiler_params=PARAMS,
        name="pack",
    )(core, hidden)


def weight_terms(slots, swapped, cotangents, tiles, state):
    sources, tokens, width = swapped.shape
    features = cotangents[0].shape[1]
    count = len(tiles)
    tile = width // 4

    def kernel(slots_ref, swapped_ref, *refs):
        cots_ref, refs = refs[:2], refs[2 + len(state) :]
        out_ref, lhs, rhs, out, sem, out_sem = refs
        copies = []
        for s in range(sources):
            place = pl.ds(pl.multiple_of(slots_ref[s] * tokens, tokens), tokens)
            source = cots_ref[s // 4].at[pl.ds(s % 4 * tokens, tokens)]
            copies.append(pltpu.make_async_copy(source, rhs.at[place], sem.at[count, s]))
        for i, t in enumerate(tiles):
            at = pl.ds(t * tile, tile)
            for s in range(sources):
                place = pl.ds(s * tokens, tokens)
                copies.append(
                    pltpu.make_async_copy(swapped_ref.at[s, :, at], lhs.at[i, place], sem.at[i, s])
                )
        for copy in copies:
            copy.start()
        stores = []
        for i, t in enumerate(tiles):
            for copy in copies[(i + 1 if i else 0) * sources : (i + 2) * sources]:
                copy.wait()
            out[i] = lax.dot_general(
                lhs[i], rhs[...], (((0,), (0,)), ((), ())), preferred_element_type=F32
            ).astype(BF16)
            target = out_ref.at[pl.ds(t * tile, tile)]
            stores.append(pltpu.make_async_copy(out.at[i], target, out_sem.at[i]))
            stores[-1].start()
        for copy in stores:
            copy.wait()

    return pl.pallas_call(
        kernel,
        out_shape=jax.ShapeDtypeStruct((width, features), BF16),
        in_specs=[SMEM] + [ANY] * (3 + len(state)),
        out_specs=ANY,
        input_output_aliases={4: 0} if state else {},
        scratch_shapes=[
            pltpu.VMEM((count, sources * tokens, tile), BF16),
            pltpu.VMEM((sources * tokens, features), BF16),
            pltpu.VMEM((count, tile, features), BF16),
            pltpu.SemaphoreType.DMA((count + 1, sources)),
            pltpu.SemaphoreType.DMA((count,)),
        ],
        cost_estimate=CHEAP,
        compiler_params=PARAMS,
        name="weight_terms",
    )(slots, swapped, *cotangents, *state)


def consume(where, scale, hidden, other, cotangents, units, state, arrived, last=False):
    tokens, width = hidden.shape
    rows, features = other.shape[2], cotangents[0].shape[1]
    half = rows // 2
    count = len(units)
    extra = len(arrived[1]) if arrived else 0
    chunks = [min(4, count - i) for i in range(0, count, 4)]
    arrays = []
    for array, _, _ in units:
        if not any(array is known for known in arrays):
            arrays.append(array)

    def kernel(where_ref, scale_ref, hidden_ref, other_ref, *refs):
        cots_ref, refs = refs[:2], refs[2:]
        array_refs, refs = refs[: len(arrays)], refs[len(arrays) :]
        if state:
            totals_ref, refs = refs[:2], refs[3:]
        arrived_refs, refs = refs[: (extra + 3) // 4], refs[(extra + 3) // 4 :]
        total_refs, gradient_ref, away_refs, refs = refs[:2], refs[2], refs[3 : 3 + len(chunks)], refs[3 + len(chunks) :]
        hid, cot, wgt, acc, prior, near, far, held, sent, sem, cot_sem, out_sem, near_sem, far_sem = refs
        place = functools.partial(unit_columns, where_ref, rows)
        early = []
        for s in range(2):
            span = pl.ds(s * tokens, tokens)
            source = cots_ref[s].at[pl.ds(0, tokens)]
            early.append(pltpu.make_async_copy(source, cot.at[span], cot_sem.at[s]))
        for copy in early:
            copy.start()
        loads = []
        for b, (array, row, (k, side, part)) in enumerate(units):
            ref = [r for r, known in zip(array_refs, arrays) if known is array][0]
            at = pl.multiple_of((1 - where_ref[2] if part else where_ref[2]) * half, half)
            if len(array.shape) == 3:
                source = ref.at[where_ref[3] ^ k]
            else:
                source = ref.at[pl.ds(at if row is None else row, half)]
            block = (where_ref[3] ^ k) * 2 + (1 - where_ref[1] if side else where_ref[1])
            pairs = [
                (source, wgt.at[b]),
                (hidden_ref.at[:, place((k, side, part), 0)], hid.at[b, pl.ds(0, tokens)]),
                (other_ref.at[block, :, pl.ds(at, half)], hid.at[b, pl.ds(tokens, tokens)]),
            ]
            loads.append([pltpu.make_async_copy(f, t, sem.at[i, b]) for i, (f, t) in enumerate(pairs)])
            for copy in loads[-1]:
                copy.start()
        before = []
        for i, ref in enumerate(arrived_refs):
            size = min(4, extra - 4 * i)
            before.append(pltpu.make_async_copy(ref, held.at[pl.ds(4 * i, size)], cot_sem.at[4 + i]))
        if state:
            for s in range(2):
                span = pl.ds(s * tokens, tokens)
                before.append(pltpu.make_async_copy(totals_ref[s], prior.at[span], cot_sem.at[2 + s]))
        for copy in before:
            copy.start()
        for copy in early:
            copy.wait()
        acc[...] = jnp.zeros_like(acc)

        def step(b, carry):
            for i, ref in enumerate((wgt.at[b], hid.at[b, pl.ds(0, tokens)], hid.at[b, pl.ds(0, tokens)])):
                pltpu.make_async_copy(ref, ref, sem.at[i, b]).wait()
            weight = wgt[b]
            acc[...] += jnp.dot(hid[b], weight, preferred_element_type=F32)
            product = (
                lax.dot_general(
                    cot[...], weight, (((1,), (1,)), ((), ())), preferred_element_type=F32
                )
                * scale_ref[0]
            ).astype(BF16)
            near[b] = product[:tokens]
            far[b] = product[tokens:]
            return carry

        lax.fori_loop(0, count, step, 0)
        late = [
            pltpu.make_async_copy(far.at[pl.ds(4 * i, size)], away_refs[i], far_sem.at[i])
            for i, size in enumerate(chunks)
        ]
        for b, (_, _, unit) in enumerate(units):
            late.append(
                pltpu.make_async_copy(near.at[b], gradient_ref.at[:, place(unit, 0)], near_sem.at[b])
            )
        for copy in late:
            copy.start()
        for copy in before:
            copy.wait()
        if state:
            acc[...] += prior[...]
        sums = [acc.at[pl.ds(s * tokens, tokens)] for s in range(2)]
        if last:
            sent[...] = acc[pl.ds(tokens, tokens)].astype(BF16)
            sums[1] = sent
        end = [pltpu.make_async_copy(sums[s], total_refs[s], out_sem.at[s]) for s in range(2)]
        for e in range(extra):
            columns = place(arrived[1][e], 1)
            end.append(
                pltpu.make_async_copy(held.at[e], gradient_ref.at[:, columns], out_sem.at[2 + e])
            )
        for copy in end:
            copy.start()
        for copy in late + end:
            copy.wait()

    sums = jax.ShapeDtypeStruct((tokens, features), F32)
    operands = [where, scale, hidden, other, *cotangents, *arrays, *state]
    if arrived:
        operands += arrived[0]
    return pl.pallas_call(
        kernel,
        out_shape=[
            sums,
            jax.ShapeDtypeStruct(sums.shape, BF16) if last else sums,
            jax.ShapeDtypeStruct((tokens, width), BF16),
            *[jax.ShapeDtypeStruct((size, tokens, half), BF16) for size in chunks],
        ],
        in_specs=[SMEM, SMEM] + [ANY] * (len(operands) - 2),
        out_specs=[ANY] * (3 + len(chunks)),
        input_output_aliases=(
            {6 + len(arrays) + i: i for i in (0, 2) + (() if last else (1,))} if state else {}
        ),
        scratch_shapes=[
            pltpu.VMEM((count, 2 * tokens, half), BF16),
            pltpu.VMEM((2 * tokens, features), BF16),
            pltpu.VMEM((count, half, features), BF16),
            pltpu.VMEM((2 * tokens, features), F32),
            pltpu.VMEM((2 * tokens, features) if state else (8, 128), F32),
            pltpu.VMEM((count, tokens, half), BF16),
            pltpu.VMEM((count, tokens, half), BF16),
            pltpu.VMEM((max(extra, 1), tokens, half), BF16),
            pltpu.VMEM((tokens, features) if last else (16, 128), BF16),
            pltpu.SemaphoreType.DMA((3, count)),
            pltpu.SemaphoreType.DMA((4 + (extra + 3) // 4,)),
            pltpu.SemaphoreType.DMA((2 + extra,)),
            pltpu.SemaphoreType.DMA((count,)),
            pltpu.SemaphoreType.DMA((len(chunks),)),
        ],
        cost_estimate=CHEAP,
        compiler_params=PARAMS,
        name="consume",
    )(*operands)


def unit_columns(where_ref, rows, unit, core):
    k, side, part = unit
    half = rows // 2
    x = 1 - where_ref[1] if side else where_ref[1]
    c = 1 - where_ref[0] if core else where_ref[0]
    r = 1 - where_ref[2] if part else where_ref[2]
    at = (((where_ref[3] ^ k) * 2 + x) * 2 + c) * rows + r * half
    return pl.ds(pl.multiple_of(at, half), half)


def finish(where, scale, gradient, arrived, units, sums, shares):
    half, features = shares[0].shape
    counts = [len(some) for some in units]

    def kernel(where_ref, scale_ref, *refs):
        arrived_refs, refs = refs[: len(units)], refs[len(units) :]
        a_ref, b_ref, mine_ref, theirs_ref, _, gradient_ref, keys_ref, weight_ref, sem = refs
        copies = []
        for ref, some in zip(arrived_refs, units):
            for e, unit in enumerate(some):
                columns = unit_columns(where_ref, 2 * half, unit, 1)
                copies.append(
                    pltpu.make_async_copy(ref.at[e], gradient_ref.at[:, columns], sem.at[len(copies)])
                )
        for copy in copies:
            copy.start()
        at = pl.multiple_of(where_ref[2] * half, half)
        weight_ref[pl.ds(at, half), :] = mine_ref[...]
        weight_ref[pl.ds(half - at, half), :] = theirs_ref[pl.ds(0, half), :]
        keys_ref[...] = ((a_ref[...] + b_ref[...].astype(F32)) * scale_ref[0]).astype(BF16)
        for copy in copies:
            copy.wait()

    return pl.pallas_call(
        kernel,
        out_shape=[
            jax.ShapeDtypeStruct(gradient.shape, BF16),
            jax.ShapeDtypeStruct(sums[0].shape, BF16),
            jax.ShapeDtypeStruct((2 * half, features), BF16),
        ],
        in_specs=[SMEM, SMEM] + [VMEM] * (len(units) + 4) + [ANY],
        out_specs=[ANY, VMEM, VMEM],
        input_output_aliases={len(units) + 6: 0},
        scratch_shapes=[pltpu.SemaphoreType.DMA((sum(counts),))],
        compiler_params=PARAMS,
        name="finish",
    )(where, scale, *arrived, *sums, *shares, gradient)


def body(hidden, key_weight, previous_peak, cotangent):
    limit = previous_peak[0]
    unscale = limit / 448.0
    scale = unscale.reshape(1)
    tokens = hidden.shape[0]
    rows = key_weight.shape[0]
    r, z, x, c = (lax.axis_index(name) for name in ("replica", "z", "x", "core"))
    where = jnp.stack([c, x, r, z]).astype(jnp.int32)
    nz = lax.axis_size("z")
    token_count = tokens * lax.axis_size(("replica", "z", "x", "core"))

    codes = quantize(key_weight, limit)
    half = rows // 2
    own = lax.dynamic_slice_in_dim(codes, r * half, half, 0)
    rest = lax.dynamic_slice_in_dim(codes, (1 - r) * half, half, 0)
    hidden, own, rest = lax.optimization_barrier((hidden, own, rest))
    mine = lax.all_gather(own, "z", axis=0)
    rest, mine = lax.optimization_barrier((rest, mine))
    theirs = lax.all_gather(rest, "z", axis=0)

    cots = [swap(cotangent, "x"), swap(cotangent, "replica"), swap(cotangent, ("replica", "x"), 3)]
    for_group, for_other = pack(where, hidden, rows, nz)
    for_group, *cots = lax.optimization_barrier((for_group, *cots))
    swapped = lax.all_to_all(for_group, ("replica", "x", "core"), 0, 0, tiled=True)
    peaks = jnp.max(jnp.abs(key_weight), axis=0, keepdims=True)
    peaks = jnp.broadcast_to(peaks, (16, peaks.shape[1]))
    for k in (1, 2):
        peaks = jnp.maximum(peaks, swap(peaks, "z", k))
    cots = jnp.concatenate([cotangent, *cots], axis=0)
    cots, peaks = lax.optimization_barrier((cots, peaks))
    cots = [cots, swap(cots, "core")]
    slots = [
        ((r ^ dr) * 2 + (x ^ dx)) * 2 + (c ^ dc) for dc in (0, 1) for dr in (0, 1) for dx in (0, 1)
    ]
    slots = jnp.stack(slots).astype(jnp.int32)
    other = swap(for_other, "core")

    parts = [own] + [lax.dynamic_index_in_dim(mine, z ^ k, keepdims=False) for k in (1, 2, 3)]
    parts[3] = jnp.concatenate([parts[3], peaks])
    swapped, other = lax.optimization_barrier((swapped, other))
    stage = functools.partial(consume, where, scale, hidden, other, [cotangent, cots[1]])

    cots[1], *parts = lax.optimization_barrier((cots[1], *parts))
    side0 = swap(parts[0], "x")
    term = weight_terms(slots, swapped, cots, (0, 1, 2, 3), [])

    term, side0, theirs, *parts = lax.optimization_barrier((term, side0, theirs, *parts))
    total = lax.psum_scatter(term, "z", scatter_dimension=0, tiled=True).astype(F32)
    side1, other0 = swap(parts[1], "x"), swap(side0, "replica")
    units = [(codes, None, (0, 0, part)) for part in (0, 1)]
    units += [(block, None, (k, 0, part)) for part, block in enumerate((mine, theirs)) for k in (1, 2, 3)]
    *state, away0, away1 = stage(units, [], None)
    arrived = ([swap(away0, "core"), swap(away1, "core")], [unit for _, _, unit in units])

    side1, other0, *rest = lax.optimization_barrier((side1, other0, *state, *parts))
    state, parts = rest[:3], rest[3:]
    side2, other1 = swap(parts[2], "x"), swap(side1, "replica")
    units = [(side0, 0, (0, 1, 0)), (other0, 0, (0, 1, 1)), (side1, 0, (1, 1, 0))]
    *state, away = stage(units, state, None)
    late = [swap(away, "core")]
    late_units = [[unit for _, _, unit in units]]

    side2, other1, *rest = lax.optimization_barrier((side2, other1, *state, *parts))
    state, parts = rest[:3], rest[3:]
    side3, other2 = swap(parts[3], "x"), swap(side2, "replica")

    side3, other2, *state = lax.optimization_barrier((side3, other2, *state))
    other3 = swap(side3, "replica")
    units = [(other1, 0, (1, 1, 1)), (side2, 0, (2, 1, 0)), (other2, 0, (2, 1, 1)), (side3, 0, (3, 1, 0))]
    *state, away = stage(units, state, arrived)
    late.append(swap(away, "core"))
    late_units.append([unit for _, _, unit in units])

    peak = jnp.maximum(jnp.max(peaks), jnp.max(side3[half:]))
    peak = jnp.full((8, 128), peak.astype(F32))
    peak = jnp.maximum(peak, swap(peak, "core"))
    peak_ratio = (peak[0, 0] / limit).reshape(1)

    share = (total * token_count ** (-0.5)).astype(BF16)
    other_share = swap(jnp.pad(share, ((0, 16), (0, 0))), "replica")
    other3, peak_ratio, *state = lax.optimization_barrier((other3, peak_ratio, *state))
    *state, away = stage([(other3, 0, (3, 1, 1))], state, None, last=True)
    late.append(swap(away, "core"))
    late_units.append([(3, 1, 1)])
    sums = [state[0], swap(state[1], "core")]
    input_gradient, projected_keys, weight_gradient = finish(
        where, scale, state[2], late, late_units, sums, [share, other_share]
    )
    return (projected_keys, input_gradient, weight_gradient, peak_ratio)


def plain(hidden_states, key_weight, previous_peak, key_cotangent):
    names = ("replica", "x", "core")
    limit = previous_peak[0]
    unscale = limit / 448.0
    tokens, width = hidden_states.shape
    rows, features = key_weight.shape
    replicas = lax.axis_size("replica")
    nz, nx, nc = lax.axis_size("z"), lax.axis_size("x"), lax.axis_size("core")
    part = rows // replicas
    group = replicas * nx * nc
    split = hidden_states.reshape(tokens, nz, nx, nc, replicas, part)
    split = split.transpose(4, 2, 3, 0, 1, 5).reshape(group, tokens, nz * part)
    swapped = lax.all_to_all(split, names, 0, 0, tiled=True)
    cotangents = lax.all_gather(key_cotangent, names, axis=0, tiled=True)
    peak = lax.pmax(jnp.max(jnp.abs(key_weight.astype(F32))), ("z", "x", "core"))
    half = lax.dynamic_slice_in_dim(key_weight, lax.axis_index("replica") * part, part, 0)
    gathered = lax.all_gather(
        quantize(half, limit), ("z", "x", "core", "replica"), axis=0, tiled=True
    )
    keys_sum = jnp.dot(hidden_states, gathered, preferred_element_type=F32)
    grad_sum = lax.dot_general(
        key_cotangent, gathered, (((1,), (1,)), ((), ())), preferred_element_type=F32
    )
    term = lax.dot_general(
        swapped.reshape(group * tokens, nz * part),
        cotangents,
        (((0,), (0,)), ((), ())),
        preferred_element_type=F32,
    ).astype(BF16)
    total = lax.psum_scatter(term, "z", scatter_dimension=0, tiled=True).astype(F32)
    token_count = tokens * replicas * nz * nx * nc
    share = (total * token_count ** (-0.5)).astype(BF16)
    weight_gradient = lax.all_gather(share, "replica", axis=0, tiled=True)
    return (
        (keys_sum * unscale).astype(BF16),
        (grad_sum * unscale).astype(BF16),
        weight_gradient,
        (peak / limit).reshape(1),
    )


def solution(mesh):
    replicas, shards = mesh.shape["replica"], mesh.shape["fsdp"]
    grid = Mesh(mesh.devices.reshape(replicas, shards // 4, 2, 2), ("replica", "z", "x", "core"))
    fsdp = ("z", "x", "core")
    every = ("replica",) + fsdp
    in_specs = (P(every, None), P(fsdp, None), P(), P(every, None))
    out_specs = (P(every, None), P(every, None), P(fsdp, None), P())
    run = body if replicas == 2 and shards == 16 else plain
    return jax.shard_map(run, mesh=grid, in_specs=in_specs, out_specs=out_specs, check_vma=False)
```

time: 411 us -> 192 us (0.47)
  waiting for transfers between devices: 315 us -> 80.5 us
  Pallas kernels: 0 us -> 51.1 us
  matrix products: 34.3 us -> 0 us
  blocking collectives: 32.3 us -> 0 us
  starting transfers between devices: 0.12 us -> 25.5 us
    reduce_scatter x1, waiting for transfers between devices: 181 us -> 0.01 us  [body(): lax.psum_scatter(term, 'z', scatter_dimension=0, tiled=True).astype(F32)]
    all_gather x1 -> x2, waiting for transfers between devices: 127 us -> 19.3 us  [the longest x1 14.7 us: body(): mine = lax.all_gather(own, 'z', axis=0)]
    pallas_call x0 -> x7, Pallas kernels: none -> 51.1 us  [the longest x4 30.8 us: consume(): pl.pallas_call(kernel, out_shape=[sums, jax.ShapeDtypeStruct(sums.shape,...]
    ppermute x0 -> x23, waiting for transfers between devices: none -> 43.6 us  [swap(): return lax.ppermute(block, axis, [(i, i ^ mask) for i in range(size)])]
    dot_general x3 -> x0, matrix products: 34.3 us -> none  [the longest x1 12.3 us: body(): lax.dot_general(key_cotangent, gathered, (((1,), (1,)), ((), ())), prefer...]
    pmax x1 -> x0, blocking collectives: 32.3 us -> none  [body(): peak = lax.pmax(local_peak, 'fsdp')]
    ppermute x0 -> x23, starting transfers between devices: none -> 20.7 us  [swap(): return lax.ppermute(block, axis, [(i, i ^ mask) for i in range(size)])]
    all_to_all x0 -> x1, waiting for transfers between devices: none -> 17.5 us  [body(): lax.all_to_all(for_group, ('replica', 'x', 'core'), 0, 0, tiled=True)]
  transfers between devices with their start and end apart: 3 -> 27, of which waited for: 3 -> 17; matrix products, arithmetic and copies ran while one was open for 1% -> 6% of each run, Pallas kernels for 0% -> 24%
where the time goes in v1:
time: 192 us
  waiting for transfers between devices  80.5 us (42%)
  Pallas kernels  51.1 us (27%)
  starting transfers between devices  25.5 us (13%)
  between operations  17.8 us (9%)
  local copies, waits for them, and re-layouts  8.86 us (5%)
  other arithmetic  7.87 us (4%)
    ppermute x23, waiting for transfers between devices, swap(): return lax.ppermute(block, axis, [(i, i ^ mask) for i in range(size)])  43.6 us
    pallas_call x4, Pallas kernels, consume(): pl.pallas_call(kernel, out_shape=[sums, jax.ShapeDtypeStruct(sums.shape,...  30.8 us
    ppermute x23, starting transfers between devices, swap(): return lax.ppermute(block, axis, [(i, i ^ mask) for i in range(size)])  20.7 us
    all_to_all x1, waiting for transfers between devices, body(): lax.all_to_all(for_group, ('replica', 'x', 'core'), 0, 0, tiled=True)  17.5 us
    all_gather x1, waiting for transfers between devices, body(): mine = lax.all_gather(own, 'z', axis=0)  14.7 us
    pallas_call x1, Pallas kernels, weight_terms(): pl.pallas_call(kernel, out_shape=jax.ShapeDtypeStruct((width, features),...  9.49 us
    pallas_call x1, Pallas kernels, pack(): pl.pallas_call(kernel, out_shape=[jax.ShapeDtypeStruct((group, tokens, nz...  6.64 us
    all_to_all x1, starting transfers between devices, body(): lax.all_to_all(for_group, ('replica', 'x', 'core'), 0, 0, tiled=True)  4.67 us
  transfers between devices with their start and end apart: 27, of which 17 were waited for; matrix products, arithmetic and copies ran while one was open for 6% of the time, Pallas kernels for 24%

profile of v1, /device:TPU:0, one launch (start us, length us, event | category | flops | bytes accessed | tf_op | source)
XLA Modules:
  0.0 191.7 jit_solution(4254636614977099246)
XLA Ops:
  7.9 1.5 clamp_convert_fusion.refs_2_
  9.5 1.0 copy-done.1
  10.4 1.0 constant_dynamic-slice_fusion
  11.5 4.0 %collective-permute-start.2 = (bf16[256,1024]{1,0:T(8,128)(2,1)S(1)}, bf16[256,1024]{1,0:T(8,128)(2,1)}, u32[]{:S(2)}, u32[]{:S(2)}) collective-permute-start(bf16[256,1024]{1,0:T(8,128)(2,1)S(1)} %copy-done), channel_id=1, source_target_pairs={{0,18},{2,16},{16,2},{18,0},{1,19},{3,17},{17,3},{19,1},{4,22},{6,... | collective-permute-start | bytes 1572872 | tf_op jit(solution)/shard_map/ppermute | solution.py:25
  15.5 0.5 collective-permute-start.1
  16.0 0.1 collective-permute-start
  16.1 0.6 pad_add_fusion.core_ref.where_ref
  16.7 6.6 %pack.1 = (bf16[8,256,1024]{2,1,0:T(8,128)(2,1)}, bf16[8,256,512]{2,1,0:T(8,128)(2,1)}) custom-call(s32[4]{0:T(128)} %pad_add_fusion.core_ref.where_ref, bf16[256,8192]{1,0:T(8,128)(2,1)} %hidden_ref.4), custom_call_target="tpu_custom_call" | custom-call | tf_op jit(solution)/shard_map/pack/pallas_call | solution.py:61
  23.4 5.0 %collective-permute-done.2 = bf16[256,1024]{1,0:T(8,128)(2,1)} collective-permute-done((bf16[256,1024]{1,0:T(8,128)(2,1)S(1)}, bf16[256,1024]{1,0:T(8,128)(2,1)}, u32[]{:S(2)}, u32[]{:S(2)}) %collective-permute-start.2) | collective-permute-done | bytes 524320 | tf_op jit(solution)/shard_map/ppermute | solution.py:25
  28.4 10.4 %collective-permute-done.1 = bf16[256,1024]{1,0:T(8,128)(2,1)} collective-permute-done((bf16[256,1024]{1,0:T(8,128)(2,1)S(1)}, bf16[256,1024]{1,0:T(8,128)(2,1)}, u32[]{:S(2)}, u32[]{:S(2)}) %collective-permute-start.1) | collective-permute-done | bytes 524320 | tf_op jit(solution)/shard_map/ppermute | solution.py:25
  38.7 0.3 collective-permute-done
  39.0 4.7 %all-to-all-start = ((bf16[8,256,1024]{2,1,0:T(8,128)(2,1)}), bf16[8,256,1024]{2,1,0:T(8,128)(2,1)}, u32[]{:S(2)}, u32[]{:S(2)}) async-start(bf16[8,256,1024]{2,1,0:T(8,128)(2,1)} %get-tuple-element.75), calls=%async_computation | async-start | bytes 8388608 | tf_op jit(solution)/shard_map/all_to_all | solution.py:345
  43.8 0.1 abs_reduce_fusion
  43.9 1.6 collective-permute-start.4
  45.5 14.7 %all-gather.5.cloned.1.call-done = bf16[1024,1024]{1,0:T(8,128)(2,1)} async-done(((bf16[256,1024]{1,0:T(8,128)(2,1)}), bf16[1024,1024]{1,0:T(8,128)(2,1)}) %all-gather.5.cloned.1.call-update) | async-done | bytes 2097168 | tf_op jit(solution)/shard_map/all_gather | solution.py:338
  60.4 1.8 collective-permute-start.5
  62.2 3.4 %collective-permute-done.5 = bf16[16,1024]{1,0:T(8,128)(2,1)S(1)} collective-permute-done((bf16[16,1024]{1,0:T(8,128)(2,1)S(1)}, bf16[16,1024]{1,0:T(8,128)(2,1)S(1)}, u32[]{:S(2)}, u32[]{:S(2)}) %collective-permute-start.5) | collective-permute-done | bytes 32800 | tf_op jit(solution)/shard_map/ppermute | solution.py:25
  65.6 1.5 pad_maximum_fusion.refs_0_
  67.2 0.1 collective-permute-start.6
  67.3 0.5 collective-permute-start.3
  67.7 2.8 %dynamic-slice_bitcast_fusion = (bf16[256,1024]{1,0:T(8,128)(2,1)S(1)}, bf16[256,1024]{1,0:T(8,128)(2,1)}, bf16[256,1024]{1,0:T(8,128)(2,1)}) fusion(bf16[4,256,1024]{2,1,0:T(8,128)(2,1)} %bitcast.27, s32[]{:T(128)S(6)} %select_n.20, s32[]{:T(128)S(6)} %select_n.19, s32[]{:T(128)S(6)} %select_n.18), kind=kLoop, calls=%fused_computation.5 | loop fusion | bytes 3145740 | tf_op jit(solution)/shard_map/jit(dynamic_index_in_dim)/squeeze | solution.py:359
  70.6 0.9 pad_maximum_fusion.1
  71.4 2.3 %collective-permute-done.6.refs_1_ = bf16[1024,1024]{1,0:T(8,128)(2,1)} collective-permute-done((bf16[1024,1024]{1,0:T(8,128)(2,1)S(1)}, bf16[1024,1024]{1,0:T(8,128)(2,1)}, u32[]{:S(2)}, u32[]{:S(2)}) %collective-permute-start.6) | collective-permute-done | bytes 2097184 | tf_op jit(solution)/shard_map/ppermute | solution.py:25
  73.7 1.5 collective-permute-start.7
  75.2 0.6 stack.55.slots_ref
  75.8 17.5 %all-to-all-done.swapped_ref = bf16[8,256,1024]{2,1,0:T(8,128)(2,1)} async-done(((bf16[8,256,1024]{2,1,0:T(8,128)(2,1)}), bf16[8,256,1024]{2,1,0:T(8,128)(2,1)}, u32[]{:S(2)}, u32[]{:S(2)}) %all-to-all-start) | async-done | bytes 4194336 | tf_op jit(solution)/shard_map/all_to_all | solution.py:345
  93.3 9.5 %weight_terms.1 = bf16[1024,1024]{1,0:T(8,128)(2,1)} custom-call(s32[8]{0:T(128)} %stack.55.slots_ref, bf16[8,256,1024]{2,1,0:T(8,128)(2,1)} %all-to-all-done.swapped_ref, bf16[1024,1024]{1,0:T(8,128)(2,1)} %copy-done.2, bf16[1024,1024]{1,0:T(8,128)(2,1)} %collective-permute-done.6.refs_1_), custom_call_target="tpu_custom_call" | custom-call | flops 1 | bytes 1 | tf_op jit(solution)/shard_map/weight_terms/pallas_call | solution.py:111
  102.8 0.3 collective-permute-done.7.refs_2_
  103.1 4.6 %all-gather.7.cloned.1.call-done = bf16[1024,1024]{1,0:T(8,128)(2,1)} async-done(((bf16[256,1024]{1,0:T(8,128)(2,1)}), bf16[1024,1024]{1,0:T(8,128)(2,1)}) %all-gather.7.cloned.1.call-update) | async-done | bytes 2097168 | tf_op jit(solution)/shard_map/all_gather | solution.py:340
  107.7 1.5 collective-permute-start.9
  109.3 1.4 collective-permute-start.8
  110.7 12.0 %consume.4 = (f32[256,1024]{1,0:T(8,128)}, f32[256,1024]{1,0:T(8,128)}, bf16[256,8192]{1,0:T(8,128)(2,1)}, bf16[4,256,256]{2,1,0:T(8,128)(2,1)}, bf16[4,256,256]{2,1,0:T(8,128)(2,1)}) custom-call(s32[4]{0:T(128)} %pad_add_fusion.core_ref.where_ref, f32[1]{0:T(128)} %bitcast.5.scale_ref, bf16[256,8192]{1,0:T(8,128)(2,1)} %hidden_ref.4, ...), custom_call_target="tpu_custom_call" | custom-call | flops 1 | bytes 1 | tf_op jit(solution)/shard_map/consume/pallas_call | solution.py:238
  122.8 0.2 collective-permute-done.8.refs_4_
  123.0 0.6 copy-done.9
  123.6 0.6 collective-permute-start.12
  124.2 1.2 collective-permute-start.11
  125.4 6.4 %consume.5 = (f32[256,1024]{1,0:T(8,128)}, f32[256,1024]{1,0:T(8,128)}, bf16[256,8192]{1,0:T(8,128)(2,1)}, bf16[3,256,256]{2,1,0:T(8,128)(2,1)}) custom-call(s32[4]{0:T(128)} %pad_add_fusion.core_ref.where_ref, f32[1]{0:T(128)} %bitcast.5.scale_ref, bf16[256,8192]{1,0:T(8,128)(2,1)} %hidden_ref.4, ...), custom_call_target="tpu_custom_call", output_to_operand_aliasing={{0}: (9, {}), {2}: (11, {}), {1}: (10, {})} | custom-call | flops 1 | bytes 1 | tf_op jit(solution)/shard_map/consume/pallas_call | solution.py:238
  131.8 5.2 %collective-permute-done.12.refs_2_ = bf16[256,1024]{1,0:T(8,128)(2,1)} collective-permute-done((bf16[256,1024]{1,0:T(8,128)(2,1)}, bf16[256,1024]{1,0:T(8,128)(2,1)}, u32[]{:S(2)}, u32[]{:S(2)}) %collective-permute-start.12) | collective-permute-done | bytes 524320 | tf_op jit(solution)/shard_map/ppermute | solution.py:25
  137.0 0.3 collective-permute-done.11.refs_3_
  137.3 1.0 collective-permute-start.13
  138.3 1.0 collective-permute-start.14
  139.3 0.5 collective-permute-start.16
  139.9 0.6 reduce_max.28
  140.5 9.5 %collective-permute-done.14.refs_4_ = bf16[256,1024]{1,0:T(8,128)(2,1)S(1)} collective-permute-done((bf16[256,1024]{1,0:T(8,128)(2,1)}, bf16[256,1024]{1,0:T(8,128)(2,1)S(1)}, u32[]{:S(2)}, u32[]{:S(2)}) %collective-permute-start.14) | collective-permute-done | bytes 524320 | tf_op jit(solution)/shard_map/ppermute | solution.py:25
  150.0 0.1 collective-permute-done.13.refs_5_
  150.0 0.7 copy-done.7
  150.8 0.9 collective-permute-start.18
  151.7 1.4 slice_reduce_fusion
  154.4 0.1 collective-permute-start.19
  154.5 7.8 %consume.6 = (f32[256,1024]{1,0:T(8,128)}, f32[256,1024]{1,0:T(8,128)}, bf16[256,8192]{1,0:T(8,128)(2,1)}, bf16[4,256,256]{2,1,0:T(8,128)(2,1)}) custom-call(s32[4]{0:T(128)} %pad_add_fusion.core_ref.where_ref, f32[1]{0:T(128)} %bitcast.5.scale_ref, bf16[256,8192]{1,0:T(8,128)(2,1)} %hidden_ref.4, ...), custom_call_target="tpu_custom_call", output_to_operand_aliasing={{0}: (10, {}), {2}: (12, {}), {1}: (11, {})} | custom-call | flops 1 | bytes 1 | tf_op jit(solution)/shard_map/consume/pallas_call | solution.py:238
  162.4 0.5 collective-permute-start.17
  162.9 1.1 multiply_convert_fusion.refs_5_
  164.1 0.9 pad.4
  165.0 1.1 collective-permute-start.22
  166.1 0.5 slice.7
  167.3 4.6 %consume.7 = (f32[256,1024]{1,0:T(8,128)}, bf16[256,1024]{1,0:T(8,128)(2,1)}, bf16[256,8192]{1,0:T(8,128)(2,1)}, bf16[1,256,256]{2,1,0:T(8,128)(2,1)}) custom-call(s32[4]{0:T(128)} %pad_add_fusion.core_ref.where_ref, f32[1]{0:T(128)} %bitcast.5.scale_ref, bf16[256,8192]{1,0:T(8,128)(2,1)} %hidden_ref.4, ...), custom_call_target="tpu_custom_call", output_to_operand_aliasing={{0}: (7, {}), {2}: (9, {})} | custom-call | flops 1 | bytes 1 | tf_op jit(solution)/shard_map/consume/pallas_call | solution.py:238
  171.9 0.1 collective-permute-start.21
  171.9 0.5 collective-permute-start.10
  172.4 0.1 collective-permute-start.20
  172.5 2.1 %collective-permute-done.10.refs_0_ = bf16[3,256,256]{2,1,0:T(8,128)(2,1)S(1)} collective-permute-done((bf16[3,256,256]{2,1,0:T(8,128)(2,1)}, bf16[3,256,256]{2,1,0:T(8,128)(2,1)S(1)}, u32[]{:S(2)}, u32[]{:S(2)}) %collective-permute-start.10) | collective-permute-done | bytes 393248 | tf_op jit(solution)/shard_map/ppermute | solution.py:25
  174.6 0.2 collective-permute-done.20.refs_2_
  174.8 0.7 copy-done.11
  175.5 4.4 %collective-permute-done.22.refs_6_ = bf16[272,1024]{1,0:T(8,128)(2,1)} collective-permute-done((bf16[272,1024]{1,0:T(8,128)(2,1)}, bf16[272,1024]{1,0:T(8,128)(2,1)}, u32[]{:S(2)}, u32[]{:S(2)}) %collective-permute-start.22) | collective-permute-done | bytes 557088 | tf_op jit(solution)/shard_map/ppermute | solution.py:25
  179.9 4.2 %finish.1 = (bf16[256,8192]{1,0:T(8,128)(2,1)}, bf16[256,1024]{1,0:T(8,128)(2,1)}, bf16[512,1024]{1,0:T(8,128)(2,1)}) custom-call(s32[4]{0:T(128)} %pad_add_fusion.core_ref.where_ref, f32[1]{0:T(128)} %bitcast.5.scale_ref, bf16[3,256,256]{2,1,0:T(8,128)(2,1)} %copy-done.10, ...), custom_call_target="tpu_custom_call", output_to_operand_aliasing={{0}: (9, {})} | custom-call | tf_op jit(solution)/shard_map/finish/pallas_call | solution.py:306
  (42 shorter events, 0.3 us)
Async XLA Ops:
  7.2 53.1 %all-gather.5.cloned.1.call-start = ((), (), s32[]{:S(2)}) async-start(), calls=%async_computation.3 | async-start | bytes 2621440 | tf_op jit(solution)/shard_map/all_gather | solution.py:338
  7.9 3.6 %copy-start = (bf16[256,1024]{1,0:T(8,128)(2,1)S(1)}, bf16[256,1024]{1,0:T(8,128)(2,1)}, u32[]{:S(2)}) copy-start(bf16[256,1024]{1,0:T(8,128)(2,1)} %refs_0_.7) | copy-start | bytes 1572868
  9.5 1.0 copy-start.1
  11.5 16.9 %collective-permute-start.2 = (bf16[256,1024]{1,0:T(8,128)(2,1)S(1)}, bf16[256,1024]{1,0:T(8,128)(2,1)}, u32[]{:S(2)}, u32[]{:S(2)}) collective-permute-start(bf16[256,1024]{1,0:T(8,128)(2,1)S(1)} %copy-done), channel_id=1, source_target_pairs={{0,18},{2,16},{16,2},{18,0},{1,19},{3,17},{17,3},{19,1},{4,22},{6,... | collective-permute-start | bytes 1572872 | tf_op jit(solution)/shard_map/ppermute | solution.py:25
  15.5 23.3 %collective-permute-start.1 = (bf16[256,1024]{1,0:T(8,128)(2,1)S(1)}, bf16[256,1024]{1,0:T(8,128)(2,1)}, u32[]{:S(2)}, u32[]{:S(2)}) collective-permute-start(bf16[256,1024]{1,0:T(8,128)(2,1)S(1)} %copy-done), channel_id=1, source_target_pairs={{0,16},{16,0},{1,17},{17,1},{2,18},{18,2},{3,19},{19,3},{4,20},{20... | collective-permute-start | bytes 1572872 | tf_op jit(solution)/shard_map/ppermute | solution.py:25
  16.0 23.0 %collective-permute-start = (bf16[256,1024]{1,0:T(8,128)(2,1)S(1)}, bf16[256,1024]{1,0:T(8,128)(2,1)}, u32[]{:S(2)}, u32[]{:S(2)}) collective-permute-start(bf16[256,1024]{1,0:T(8,128)(2,1)S(1)} %copy-done), channel_id=1, source_target_pairs={{0,2},{2,0},{1,3},{3,1},{4,6},{6,4},{5,7},{7,5},{8,10},{10,8},{9,1... | collective-permute-start | bytes 1572872 | tf_op jit(solution)/shard_map/ppermute | solution.py:25
  39.0 4.7 %copy-start.4 = (bf16[512,1024]{1,0:T(8,128)(2,1)S(1)}, bf16[512,1024]{1,0:T(8,128)(2,1)}, u32[]{:S(2)}) copy-start(bf16[512,1024]{1,0:T(8,128)(2,1)} %param.5) | copy-start | bytes 3145732
  39.0 54.3 %all-to-all-start = ((bf16[8,256,1024]{2,1,0:T(8,128)(2,1)}), bf16[8,256,1024]{2,1,0:T(8,128)(2,1)}, u32[]{:S(2)}, u32[]{:S(2)}) async-start(bf16[8,256,1024]{2,1,0:T(8,128)(2,1)} %get-tuple-element.75), calls=%async_computation | async-start | bytes 8388608 | tf_op jit(solution)/shard_map/all_to_all | solution.py:345
  43.7 64.0 %all-gather.7.cloned.1.call-start = ((), (), s32[]{:S(2)}) async-start(), calls=%async_computation.4 | async-start | bytes 2621440 | tf_op jit(solution)/shard_map/all_gather | solution.py:340
  43.9 16.5 %collective-permute-start.4 = (bf16[16,1024]{1,0:T(8,128)(2,1)S(1)}, bf16[16,1024]{1,0:T(8,128)(2,1)S(1)}, u32[]{:S(2)}, u32[]{:S(2)}) collective-permute-start(bf16[16,1024]{1,0:T(8,128)(2,1)S(1)} %broadcast_in_dim.4), channel_id=1, source_target_pairs={{0,4},{4,0},{8,12},{12,8},{1,5},{5,1},{9,13},{13,9},{2,6},{6,2},{1... | collective-permute-start | bytes 98312 | tf_op jit(solution)/shard_map/ppermute | solution.py:25
  60.3 102.6 %reduce-scatter.2.cloned.1.call-start = ((), (), s32[]{:S(2)}) async-start(), calls=%async_computation.2 | async-start | bytes 2621440 | tf_op jit(solution)/shard_map/reduce_scatter | solution.py:369
  60.4 5.2 %collective-permute-start.5 = (bf16[16,1024]{1,0:T(8,128)(2,1)S(1)}, bf16[16,1024]{1,0:T(8,128)(2,1)S(1)}, u32[]{:S(2)}, u32[]{:S(2)}) collective-permute-start(bf16[16,1024]{1,0:T(8,128)(2,1)S(1)} %broadcast_maximum_fusion), channel_id=1, source_target_pairs={{0,8},{4,12},{8,0},{12,4},{1,9},{5,13},{9,1},{13,5},{2,10},{6,14},... | collective-permute-start | bytes 98312 | tf_op jit(solution)/shard_map/ppermute | solution.py:25
  67.2 4.2 %copy-start.2 = (bf16[1024,1024]{1,0:T(8,128)(2,1)}, bf16[1024,1024]{1,0:T(8,128)(2,1)S(1)}, u32[]{:S(2)}) copy-start(bf16[1024,1024]{1,0:T(8,128)(2,1)S(1)} %pad_maximum_fusion.refs_0_) | copy-start | bytes 6291460
  67.2 6.6 %collective-permute-start.6 = (bf16[1024,1024]{1,0:T(8,128)(2,1)S(1)}, bf16[1024,1024]{1,0:T(8,128)(2,1)}, u32[]{:S(2)}, u32[]{:S(2)}) collective-permute-start(bf16[1024,1024]{1,0:T(8,128)(2,1)S(1)} %pad_maximum_fusion.refs_0_), channel_id=1, source_target_pairs={{0,1},{1,0},{2,3},{3,2},{4,5},{5,4},{6,7},{7,6},{8,9},{9,8},{10,11... | collective-permute-start | bytes 6291464 | tf_op jit(solution)/shard_map/ppermute | solution.py:25
  67.3 8.5 %collective-permute-start.3 = (bf16[8,256,512]{2,1,0:T(8,128)(2,1)}, bf16[8,256,512]{2,1,0:T(8,128)(2,1)}, u32[]{:S(2)}, u32[]{:S(2)}) collective-permute-start(bf16[8,256,512]{2,1,0:T(8,128)(2,1)} %get-tuple-element.76), channel_id=1, source_target_pairs={{0,1},{1,0},{2,3},{3,2},{4,5},{5,4},{6,7},{7,6},{8,9},{9,8},{10,11... | collective-permute-start | bytes 6291464 | tf_op jit(solution)/shard_map/ppermute | solution.py:25
  67.7 6.0 %copy-start.5 = (bf16[256,1024]{1,0:T(8,128)(2,1)S(1)}, bf16[256,1024]{1,0:T(8,128)(2,1)}, u32[]{:S(2)}) copy-start(bf16[256,1024]{1,0:T(8,128)(2,1)} %get-tuple-element.88) | copy-start | bytes 1572868
  73.7 29.4 %collective-permute-start.7 = (bf16[256,1024]{1,0:T(8,128)(2,1)S(1)}, bf16[256,1024]{1,0:T(8,128)(2,1)}, u32[]{:S(2)}, u32[]{:S(2)}) collective-permute-start(bf16[256,1024]{1,0:T(8,128)(2,1)S(1)} %copy-done.5), channel_id=1, source_target_pairs={{0,2},{2,0},{1,3},{3,1},{4,6},{6,4},{5,7},{7,5},{8,10},{10,8},{9,1... | collective-permute-start | bytes 1572872 | tf_op jit(solution)/shard_map/ppermute | solution.py:25
  107.7 15.0 %collective-permute-start.9 = (bf16[256,1024]{1,0:T(8,128)(2,1)}, bf16[256,1024]{1,0:T(8,128)(2,1)S(1)}, u32[]{:S(2)}, u32[]{:S(2)}) collective-permute-start(bf16[256,1024]{1,0:T(8,128)(2,1)} %collective-permute-done.7.refs_2_), channel_id=1, source_target_pairs={{0,16},{16,0},{1,17},{17,1},{2,18},{18,2},{3,19},{19,3},{4,20},{20... | collective-permute-start | bytes 1572872 | tf_op jit(solution)/shard_map/ppermute | solution.py:25
  109.3 13.7 %collective-permute-start.8 = (bf16[256,1024]{1,0:T(8,128)(2,1)}, bf16[256,1024]{1,0:T(8,128)(2,1)}, u32[]{:S(2)}, u32[]{:S(2)}) collective-permute-start(bf16[256,1024]{1,0:T(8,128)(2,1)} %get-tuple-element.94), channel_id=1, source_target_pairs={{0,2},{2,0},{1,3},{3,1},{4,6},{6,4},{5,7},{7,5},{8,10},{10,8},{9,1... | collective-permute-start | bytes 1572872 | tf_op jit(solution)/shard_map/ppermute | solution.py:25
  122.8 0.8 copy-start.9
  123.6 13.7 %copy-start.6 = (bf16[272,1024]{1,0:T(8,128)(2,1)S(1)}, bf16[272,1024]{1,0:T(8,128)(2,1)}, u32[]{:S(2)}) copy-start(bf16[272,1024]{1,0:T(8,128)(2,1)} %pad_maximum_fusion.1) | copy-start | bytes 1671172
  123.6 13.4 %collective-permute-start.12 = (bf16[256,1024]{1,0:T(8,128)(2,1)}, bf16[256,1024]{1,0:T(8,128)(2,1)}, u32[]{:S(2)}, u32[]{:S(2)}) collective-permute-start(bf16[256,1024]{1,0:T(8,128)(2,1)} %collective-permute-done.8.refs_4_), channel_id=1, source_target_pairs={{0,16},{16,0},{1,17},{17,1},{2,18},{18,2},{3,19},{19,3},{4,20},{20... | collective-permute-start | bytes 1572872 | tf_op jit(solution)/shard_map/ppermute | solution.py:25
  124.2 13.1 %collective-permute-start.11 = (bf16[256,1024]{1,0:T(8,128)(2,1)}, bf16[256,1024]{1,0:T(8,128)(2,1)}, u32[]{:S(2)}, u32[]{:S(2)}) collective-permute-start(bf16[256,1024]{1,0:T(8,128)(2,1)} %get-tuple-element.107), channel_id=1, source_target_pairs={{0,2},{2,0},{1,3},{3,1},{4,6},{6,4},{5,7},{7,5},{8,10},{10,8},{9,1... | collective-permute-start | bytes 1572872 | tf_op jit(solution)/shard_map/ppermute | solution.py:25
  137.3 12.7 %collective-permute-start.13 = (bf16[272,1024]{1,0:T(8,128)(2,1)S(1)}, bf16[272,1024]{1,0:T(8,128)(2,1)}, u32[]{:S(2)}, u32[]{:S(2)}) collective-permute-start(bf16[272,1024]{1,0:T(8,128)(2,1)S(1)} %copy-done.6), channel_id=1, source_target_pairs={{0,2},{2,0},{1,3},{3,1},{4,6},{6,4},{5,7},{7,5},{8,10},{10,8},{9,1... | collective-permute-start | bytes 1671176 | tf_op jit(solution)/shard_map/ppermute | solution.py:25
  138.3 11.6 %collective-permute-start.14 = (bf16[256,1024]{1,0:T(8,128)(2,1)}, bf16[256,1024]{1,0:T(8,128)(2,1)S(1)}, u32[]{:S(2)}, u32[]{:S(2)}) collective-permute-start(bf16[256,1024]{1,0:T(8,128)(2,1)} %collective-permute-done.11.refs_3_), channel_id=1, source_target_pairs={{0,16},{16,0},{1,17},{17,1},{2,18},{18,2},{3,19},{19,3},{4,20},{20... | collective-permute-start | bytes 1572872 | tf_op jit(solution)/shard_map/ppermute | solution.py:25
  139.3 15.2 %collective-permute-start.15 = (bf16[4,256,256]{2,1,0:T(8,128)(2,1)}, bf16[4,256,256]{2,1,0:T(8,128)(2,1)}, u32[]{:S(2)}, u32[]{:S(2)}) collective-permute-start(bf16[4,256,256]{2,1,0:T(8,128)(2,1)} %get-tuple-element.123), channel_id=1, source_target_pairs={{0,1},{1,0},{2,3},{3,2},{4,5},{5,4},{6,7},{7,6},{8,9},{9,8},{10,11... | collective-permute-start | bytes 1572872 | tf_op jit(solution)/shard_map/ppermute | solution.py:25
  139.3 15.2 %collective-permute-start.16 = (bf16[4,256,256]{2,1,0:T(8,128)(2,1)}, bf16[4,256,256]{2,1,0:T(8,128)(2,1)}, u32[]{:S(2)}, u32[]{:S(2)}) collective-permute-start(bf16[4,256,256]{2,1,0:T(8,128)(2,1)} %get-tuple-element.124), channel_id=1, source_target_pairs={{0,1},{1,0},{2,3},{3,2},{4,5},{5,4},{6,7},{7,6},{8,9},{9,8},{10,11... | collective-permute-start | bytes 1572872 | tf_op jit(solution)/shard_map/ppermute | solution.py:25
  150.0 0.8 copy-start.7
  150.8 16.5 %collective-permute-start.18 = (bf16[272,1024]{1,0:T(8,128)(2,1)}, bf16[272,1024]{1,0:T(8,128)(2,1)}, u32[]{:S(2)}, u32[]{:S(2)}) collective-permute-start(bf16[272,1024]{1,0:T(8,128)(2,1)} %collective-permute-done.13.refs_5_), channel_id=1, source_target_pairs={{0,16},{16,0},{1,17},{17,1},{2,18},{18,2},{3,19},{19,3},{4,20},{20... | collective-permute-start | bytes 1671176 | tf_op jit(solution)/shard_map/ppermute | solution.py:25
  154.4 11.6 %collective-permute-start.19 = (f32[8,128]{1,0:T(8,128)S(1)}, f32[8,128]{1,0:T(8,128)S(1)}, u32[]{:S(2)}, u32[]{:S(2)}) collective-permute-start(f32[8,128]{1,0:T(8,128)S(1)} %broadcast_in_dim.10), channel_id=1, source_target_pairs={{0,1},{1,0},{2,3},{3,2},{4,5},{5,4},{6,7},{7,6},{8,9},{9,8},{10,11... | collective-permute-start | bytes 12296 | tf_op jit(solution)/shard_map/ppermute | solution.py:25
  162.4 12.3 %collective-permute-start.17 = (bf16[4,256,256]{2,1,0:T(8,128)(2,1)}, bf16[4,256,256]{2,1,0:T(8,128)(2,1)}, u32[]{:S(2)}, u32[]{:S(2)}) collective-permute-start(bf16[4,256,256]{2,1,0:T(8,128)(2,1)} %get-tuple-element.125), channel_id=1, source_target_pairs={{0,1},{1,0},{2,3},{3,2},{4,5},{5,4},{6,7},{7,6},{8,9},{9,8},{10,11... | collective-permute-start | bytes 1572872 | tf_op jit(solution)/shard_map/ppermute | solution.py:25
  164.0 7.8 %copy-start.3 = (bf16[256,1024]{1,0:T(8,128)(2,1)}, bf16[256,1024]{1,0:T(8,128)(2,1)S(1)}, u32[]{:S(2)}) copy-start(bf16[256,1024]{1,0:T(8,128)(2,1)S(1)} %multiply_convert_fusion.refs_5_) | copy-start | bytes 1572868
  165.0 14.9 %collective-permute-start.22 = (bf16[272,1024]{1,0:T(8,128)(2,1)}, bf16[272,1024]{1,0:T(8,128)(2,1)}, u32[]{:S(2)}, u32[]{:S(2)}) collective-permute-start(bf16[272,1024]{1,0:T(8,128)(2,1)} %pad.4), channel_id=1, source_target_pairs={{0,16},{16,0},{1,17},{17,1},{2,18},{18,2},{3,19},{19,3},{4,20},{20... | collective-permute-start | bytes 1671176 | tf_op jit(solution)/shard_map/ppermute | solution.py:25
  171.9 2.9 %collective-permute-start.21 = (bf16[256,1024]{1,0:T(8,128)(2,1)}, bf16[256,1024]{1,0:T(8,128)(2,1)S(1)}, u32[]{:S(2)}, u32[]{:S(2)}) collective-permute-start(bf16[256,1024]{1,0:T(8,128)(2,1)} %get-tuple-element.135), channel_id=1, source_target_pairs={{0,1},{1,0},{2,3},{3,2},{4,5},{5,4},{6,7},{7,6},{8,9},{9,8},{10,11... | collective-permute-start | bytes 1572872 | tf_op jit(solution)/shard_map/ppermute | solution.py:25
  171.9 2.7 %collective-permute-start.10 = (bf16[3,256,256]{2,1,0:T(8,128)(2,1)}, bf16[3,256,256]{2,1,0:T(8,128)(2,1)S(1)}, u32[]{:S(2)}, u32[]{:S(2)}) collective-permute-start(bf16[3,256,256]{2,1,0:T(8,128)(2,1)} %get-tuple-element.106), channel_id=1, source_target_pairs={{0,1},{1,0},{2,3},{3,2},{4,5},{5,4},{6,7},{7,6},{8,9},{9,8},{10,11... | collective-permute-start | bytes 1179656 | tf_op jit(solution)/shard_map/ppermute | solution.py:25
  172.4 2.4 %collective-permute-start.20 = (bf16[1,256,256]{2,1,0:T(8,128)(2,1)}, bf16[1,256,256]{2,1,0:T(8,128)(2,1)S(1)}, u32[]{:S(2)}, u32[]{:S(2)}) collective-permute-start(bf16[1,256,256]{2,1,0:T(8,128)(2,1)} %get-tuple-element.133), channel_id=1, source_target_pairs={{0,1},{1,0},{2,3},{3,2},{4,5},{5,4},{6,7},{7,6},{8,9},{9,8},{10,11... | collective-permute-start | bytes 393224 | tf_op jit(solution)/shard_map/ppermute | solution.py:25
  174.6 5.3 %copy-start.10 = (bf16[3,256,256]{2,1,0:T(8,128)(2,1)}, bf16[3,256,256]{2,1,0:T(8,128)(2,1)S(1)}, u32[]{:S(2)}) copy-start(bf16[3,256,256]{2,1,0:T(8,128)(2,1)S(1)} %collective-permute-done.10.refs_0_) | copy-start | bytes 1179652
  174.8 0.7 copy-start.11
  175.5 4.4 %copy-start.8 = (bf16[256,1024]{1,0:T(8,128)(2,1)}, bf16[256,1024]{1,0:T(8,128)(2,1)S(1)}, u32[]{:S(2)}) copy-start(bf16[256,1024]{1,0:T(8,128)(2,1)S(1)} %collective-permute-done.21.refs_4_) | copy-start | bytes 1572868
Sparse Core Ops, SparseCore 0:
  11.6 48.6 all-gather.4
  62.4 45.2 all-gather.6
  110.0 42.5 reduce-scatter.1

commit v2 on v1

--- a/solution.py
+++ b/solution.py
@@ -339,7 +339,9 @@
     rest, mine = lax.optimization_barrier((rest, mine))
     theirs = lax.all_gather(rest, "z", axis=0)
 
-    cots = [swap(cotangent, "x"), swap(cotangent, "replica"), swap(cotangent, ("replica", "x"), 3)]
+    cots = [swap(cotangent, "x"), swap(cotangent, "replica")]
+    cut = tokens // 2
+    cots += [swap(cots[1][:cut], "x"), swap(cots[0][cut:], "replica")]
     for_group, for_other = pack(where, hidden, rows, nz)
     for_group, *cots = lax.optimization_barrier((for_group, *cots))
     swapped = lax.all_to_all(for_group, ("replica", "x", "core"), 0, 0, tiled=True)
@@ -365,11 +367,11 @@
     side0 = swap(parts[0], "x")
     term = weight_terms(slots, swapped, cots, (0, 1, 2, 3), [])
 
-    term, side0, theirs, *parts = lax.optimization_barrier((term, side0, theirs, *parts))
+    term, side0, *parts = lax.optimization_barrier((term, side0, *parts))
     total = lax.psum_scatter(term, "z", scatter_dimension=0, tiled=True).astype(F32)
     side1, other0 = swap(parts[1], "x"), swap(side0, "replica")
     units = [(codes, None, (0, 0, part)) for part in (0, 1)]
-    units += [(block, None, (k, 0, part)) for part, block in enumerate((mine, theirs)) for k in (1, 2, 3)]
+    units += [(mine, None, (k, 0, 0)) for k in (1, 2, 3)]
     *state, away0, away1 = stage(units, [], None)
     arrived = ([swap(away0, "core"), swap(away1, "core")], [unit for _, _, unit in units])
 
@@ -384,6 +386,9 @@
     side2, other1, *rest = lax.optimization_barrier((side2, other1, *state, *parts))
     state, parts = rest[:3], rest[3:]
     side3, other2 = swap(parts[3], "x"), swap(side2, "replica")
+    units = [(theirs, None, (k, 0, 1)) for k in (1, 2, 3)]
+    *state, away = stage(units, state, arrived)
+    arrived = ([swap(away, "core")], [unit for _, _, unit in units])
 
     side3, other2, *state = lax.optimization_barrier((side3, other2, *state))
     other3 = swap(side3, "replica")

time: 192 us -> 188 us (0.979)
  waiting for transfers between devices: 80.5 us -> 64.6 us
  local copies, waits for them, and re-layouts: 8.86 us -> 16.1 us
  Pallas kernels: 51.1 us -> 54.1 us
  starting transfers between devices: 25.5 us -> 28 us
    ppermute x23 -> x25, waiting for transfers between devices: 43.6 us -> 31.8 us  [swap(): return lax.ppermute(block, axis, [(i, i ^ mask) for i in range(size)])]
    unnamed x24 -> x36, local copies, waits for them, and re-layouts: 3 us -> 8.66 us
    all_gather x1, waiting for transfers between devices: 4.59 us -> 0.01 us  [body(): theirs = lax.all_gather(rest, 'z', axis=0)]
    pallas_call x4 -> x5, Pallas kernels: 30.8 us -> 33.8 us  [consume(): pl.pallas_call(kernel, out_shape=[sums, jax.ShapeDtypeStruct(sums.shape,...]
    ppermute x23 -> x25, starting transfers between devices: 20.7 us -> 23.3 us  [swap(): return lax.ppermute(block, axis, [(i, i ^ mask) for i in range(size)])]
  transfers between devices with their start and end apart: 27 -> 29, of which waited for: 17 -> 16; matrix products, arithmetic and copies ran while one was open for 6% -> 9% of each run, Pallas kernels for 24% -> 27%
where the time goes in v2:
time: 188 us; the launch traced here: 187 us
  waiting for transfers between devices  64.6 us (34%)
  Pallas kernels  54.1 us (29%)
  starting transfers between devices  28 us (15%)
  between operations  17.8 us (9%)
  local copies, waits for them, and re-layouts  16.1 us (9%)
  other arithmetic  6.34 us (3%)
    pallas_call x5, Pallas kernels, consume(): pl.pallas_call(kernel, out_shape=[sums, jax.ShapeDtypeStruct(sums.shape,...  33.8 us
    ppermute x25, waiting for transfers between devices, swap(): return lax.ppermute(block, axis, [(i, i ^ mask) for i in range(size)])  31.8 us
    ppermute x25, starting transfers between devices, swap(): return lax.ppermute(block, axis, [(i, i ^ mask) for i in range(size)])  23.3 us
    all_to_all x1, waiting for transfers between devices, body(): lax.all_to_all(for_group, ('replica', 'x', 'core'), 0, 0, tiled=True)  19 us
    all_gather x1, waiting for transfers between devices, body(): mine = lax.all_gather(own, 'z', axis=0)  13.1 us
    pallas_call x1, Pallas kernels, weight_terms(): pl.pallas_call(kernel, out_shape=jax.ShapeDtypeStruct((width, features),...  9.46 us
    unnamed x36, local copies, waits for them, and re-layouts  8.66 us
    pallas_call x1, Pallas kernels, pack(): pl.pallas_call(kernel, out_shape=[jax.ShapeDtypeStruct((group, tokens, nz...  6.67 us
  transfers between devices with their start and end apart: 29, of which 16 were waited for; matrix products, arithmetic and copies ran while one was open for 9% of the time, Pallas kernels for 27%

profile of v2, /device:TPU:0, one launch (start us, length us, event | category | flops | bytes accessed | tf_op | source)
XLA Modules:
  0.0 186.9 jit_solution(830274138772864054)
XLA Ops:
  7.9 1.5 clamp_convert_fusion.refs_2_
  9.5 1.0 copy-done.1
  10.4 1.0 constant_dynamic-slice_fusion
  11.5 3.0 %collective-permute-start.1 = (bf16[256,1024]{1,0:T(8,128)(2,1)S(1)}, bf16[256,1024]{1,0:T(8,128)(2,1)S(1)}, u32[]{:S(2)}, u32[]{:S(2)}) collective-permute-start(bf16[256,1024]{1,0:T(8,128)(2,1)S(1)} %copy-done), channel_id=1, source_target_pairs={{0,16},{16,0},{1,17},{17,1},{2,18},{18,2},{3,19},{19,3},{4,20},{20... | collective-permute-start | bytes 1572872 | tf_op jit(solution)/shard_map/ppermute | solution.py:25
  14.5 1.5 collective-permute-start
  16.0 10.4 %collective-permute-done.1 = bf16[256,1024]{1,0:T(8,128)(2,1)S(1)} collective-permute-done((bf16[256,1024]{1,0:T(8,128)(2,1)S(1)}, bf16[256,1024]{1,0:T(8,128)(2,1)S(1)}, u32[]{:S(2)}, u32[]{:S(2)}) %collective-permute-start.1) | collective-permute-done | bytes 524320 | tf_op jit(solution)/shard_map/ppermute | solution.py:25
  26.5 0.8 slice.16
  27.2 1.7 collective-permute-start.2
  29.0 0.8 slice.17
  29.7 1.5 collective-permute-start.3
  31.4 1.6 collective-permute-start.5
  33.0 0.7 pad_add_fusion.core_ref.where_ref
  33.7 6.7 %pack.1 = (bf16[8,256,1024]{2,1,0:T(8,128)(2,1)}, bf16[8,256,512]{2,1,0:T(8,128)(2,1)}) custom-call(s32[4]{0:T(128)} %pad_add_fusion.core_ref.where_ref, bf16[256,8192]{1,0:T(8,128)(2,1)} %hidden_ref.5), custom_call_target="tpu_custom_call" | custom-call | tf_op jit(solution)/shard_map/pack/pallas_call | solution.py:61
  40.4 4.6 %all-to-all-start = ((bf16[8,256,1024]{2,1,0:T(8,128)(2,1)}), bf16[8,256,1024]{2,1,0:T(8,128)(2,1)}, u32[]{:S(2)}, u32[]{:S(2)}) async-start(bf16[8,256,1024]{2,1,0:T(8,128)(2,1)} %get-tuple-element.79), calls=%async_computation | async-start | bytes 8388608 | tf_op jit(solution)/shard_map/all_to_all | solution.py:347
  45.1 2.7 %collective-permute-start.6 = (bf16[16,1024]{1,0:T(8,128)(2,1)S(1)}, bf16[16,1024]{1,0:T(8,128)(2,1)S(1)}, u32[]{:S(2)}, u32[]{:S(2)}) collective-permute-start(bf16[16,1024]{1,0:T(8,128)(2,1)S(1)} %broadcast_maximum_fusion), channel_id=1, source_target_pairs={{0,8},{4,12},{8,0},{12,4},{1,9},{5,13},{9,1},{13,5},{2,10},{6,14},... | collective-permute-start | bytes 98312 | tf_op jit(solution)/shard_map/ppermute | solution.py:25
  47.7 0.9 constant_dynamic-update-slice_fusion.4
  48.6 13.1 %all-gather.5.cloned.1.call-done = bf16[1024,1024]{1,0:T(8,128)(2,1)} async-done(((bf16[256,1024]{1,0:T(8,128)(2,1)}), bf16[1024,1024]{1,0:T(8,128)(2,1)}) %all-gather.5.cloned.1.call-update) | async-done | bytes 2097168 | tf_op jit(solution)/shard_map/all_gather | solution.py:338
  61.8 2.0 %constant_dynamic-update-slice_fusion.3 = bf16[1024,1024]{1,0:T(8,128)(2,1)} fusion(bf16[1024,1024]{1,0:T(8,128)(2,1)} %constant_dynamic-update-slice_fusion.4, bf16[256,1024]{1,0:T(8,128)(2,1)} %copy-done.7), kind=kLoop, calls=%fused_computation.12 | loop fusion | bytes 1048576
  63.8 1.9 %constant_dynamic-update-slice_fusion.2 = bf16[1024,1024]{1,0:T(8,128)(2,1)} fusion(bf16[1024,1024]{1,0:T(8,128)(2,1)} %constant_dynamic-update-slice_fusion.3, bf16[256,1024]{1,0:T(8,128)(2,1)} %copy-done.6), kind=kLoop, calls=%fused_computation.11 | loop fusion | bytes 1048576
  65.7 0.7 constant_dynamic-update-slice_fusion.1
  66.4 1.7 constant_dynamic-update-slice_fusion.refs_0_
  68.1 0.5 collective-permute-start.4
  68.6 1.1 dynamic-slice_bitcast_fusion
  69.7 0.8 pad_maximum_fusion
  70.5 2.0 %collective-permute-done.7.refs_1_ = bf16[1024,1024]{1,0:T(8,128)(2,1)} collective-permute-done((bf16[1024,1024]{1,0:T(8,128)(2,1)}, bf16[1024,1024]{1,0:T(8,128)(2,1)}, u32[]{:S(2)}, u32[]{:S(2)}) %collective-permute-start.7) | collective-permute-done | bytes 2097184 | tf_op jit(solution)/shard_map/ppermute | solution.py:25
  72.6 1.4 collective-permute-start.8
  74.0 0.6 stack.55.slots_ref
  74.6 0.9 collective-permute-done.4.other_ref
  75.6 19.0 %all-to-all-done.swapped_ref = bf16[8,256,1024]{2,1,0:T(8,128)(2,1)} async-done(((bf16[8,256,1024]{2,1,0:T(8,128)(2,1)}), bf16[8,256,1024]{2,1,0:T(8,128)(2,1)}, u32[]{:S(2)}, u32[]{:S(2)}) %all-to-all-start) | async-done | bytes 4194336 | tf_op jit(solution)/shard_map/all_to_all | solution.py:347
  94.6 9.5 %weight_terms.1 = bf16[1024,1024]{1,0:T(8,128)(2,1)} custom-call(s32[8]{0:T(128)} %stack.55.slots_ref, bf16[8,256,1024]{2,1,0:T(8,128)(2,1)} %all-to-all-done.swapped_ref, bf16[1024,1024]{1,0:T(8,128)(2,1)} %constant_dynamic-update-slice_fusion.refs_0_, bf16[1024,1024]{1,0:T(8,128)(2,1)} %collective-permute-done.7.refs_1_), custom_call_target="tpu_custom_call" | custom-call | flops 1 | bytes 1 | tf_op jit(solution)/shard_map/weight_terms/pallas_call | solution.py:111
  104.0 0.4 collective-permute-done.8.refs_2_
  104.4 1.6 collective-permute-start.10
  106.0 0.6 collective-permute-start.9
  106.6 8.8 %consume.5 = (f32[256,1024]{1,0:T(8,128)}, f32[256,1024]{1,0:T(8,128)}, bf16[256,8192]{1,0:T(8,128)(2,1)}, bf16[4,256,256]{2,1,0:T(8,128)(2,1)}, bf16[1,256,256]{2,1,0:T(8,128)(2,1)}) custom-call(s32[4]{0:T(128)} %pad_add_fusion.core_ref.where_ref, f32[1]{0:T(128)} %bitcast.5.scale_ref, bf16[256,8192]{1,0:T(8,128)(2,1)} %hidden_ref.5, ...), custom_call_target="tpu_custom_call" | custom-call | flops 1 | bytes 1 | tf_op jit(solution)/shard_map/consume/pallas_call | solution.py:238
  115.4 2.8 %collective-permute-done.10.refs_3_ = bf16[256,1024]{1,0:T(8,128)(2,1)S(1)} collective-permute-done((bf16[256,1024]{1,0:T(8,128)(2,1)}, bf16[256,1024]{1,0:T(8,128)(2,1)S(1)}, u32[]{:S(2)}, u32[]{:S(2)}) %collective-permute-start.10) | collective-permute-done | bytes 524320 | tf_op jit(solution)/shard_map/ppermute | solution.py:25
  118.2 1.3 collective-permute-done.9.refs_4_
  119.5 1.0 collective-permute-start.13
  120.5 0.6 collective-permute-start.12
  121.1 6.4 %consume.6 = (f32[256,1024]{1,0:T(8,128)}, f32[256,1024]{1,0:T(8,128)}, bf16[256,8192]{1,0:T(8,128)(2,1)}, bf16[3,256,256]{2,1,0:T(8,128)(2,1)}) custom-call(s32[4]{0:T(128)} %pad_add_fusion.core_ref.where_ref, f32[1]{0:T(128)} %bitcast.5.scale_ref, bf16[256,8192]{1,0:T(8,128)(2,1)} %hidden_ref.5, ...), custom_call_target="tpu_custom_call", output_to_operand_aliasing={{0}: (9, {}), {2}: (11, {}), {1}: (10, {})} | custom-call | flops 1 | bytes 1 | tf_op jit(solution)/shard_map/consume/pallas_call | solution.py:238
  127.4 4.7 %collective-permute-done.13.refs_2_ = bf16[256,1024]{1,0:T(8,128)(2,1)} collective-permute-done((bf16[256,1024]{1,0:T(8,128)(2,1)}, bf16[256,1024]{1,0:T(8,128)(2,1)}, u32[]{:S(2)}, u32[]{:S(2)}) %collective-permute-start.13) | collective-permute-done | bytes 524320 | tf_op jit(solution)/shard_map/ppermute | solution.py:25
  132.1 1.1 collective-permute-done.12.refs_3_
  133.2 0.6 collective-permute-start.14
  133.8 0.9 collective-permute-start.15
  134.9 0.6 reduce_max.28
  135.5 0.5 collective-permute-done.17.refs_7_
  136.0 0.6 copy-done.14
  136.6 6.5 %consume.7 = (f32[256,1024]{1,0:T(8,128)}, f32[256,1024]{1,0:T(8,128)}, bf16[256,8192]{1,0:T(8,128)(2,1)}, bf16[3,256,256]{2,1,0:T(8,128)(2,1)}) custom-call(s32[4]{0:T(128)} %pad_add_fusion.core_ref.where_ref, f32[1]{0:T(128)} %bitcast.5.scale_ref, bf16[256,8192]{1,0:T(8,128)(2,1)} %hidden_ref.5, ...), custom_call_target="tpu_custom_call", output_to_operand_aliasing={{0}: (7, {}), {2}: (9, {}), {1}: (8, {})} | custom-call | flops 1 | bytes 1 | tf_op jit(solution)/shard_map/consume/pallas_call | solution.py:238
  143.5 4.9 %collective-permute-done.15.refs_4_ = bf16[256,1024]{1,0:T(8,128)(2,1)} collective-permute-done((bf16[256,1024]{1,0:T(8,128)(2,1)}, bf16[256,1024]{1,0:T(8,128)(2,1)}, u32[]{:S(2)}, u32[]{:S(2)}) %collective-permute-start.15) | collective-permute-done | bytes 524320 | tf_op jit(solution)/shard_map/ppermute | solution.py:25
  148.4 0.9 collective-permute-start.20
  149.3 1.4 slice_reduce_fusion
  152.1 0.6 reduce-scatter.2.cloned.1.call-done
  152.7 1.1 multiply_convert_fusion.refs_5_
  153.9 0.9 pad.4
  154.8 1.6 collective-permute-start.24
  156.4 0.5 slice.15
  157.6 0.8 copy-done.12
  158.3 7.5 %consume.8 = (f32[256,1024]{1,0:T(8,128)}, f32[256,1024]{1,0:T(8,128)}, bf16[256,8192]{1,0:T(8,128)(2,1)}, bf16[4,256,256]{2,1,0:T(8,128)(2,1)}) custom-call(s32[4]{0:T(128)} %pad_add_fusion.core_ref.where_ref, f32[1]{0:T(128)} %bitcast.5.scale_ref, bf16[256,8192]{1,0:T(8,128)(2,1)} %hidden_ref.5, ...), custom_call_target="tpu_custom_call", output_to_operand_aliasing={{0}: (10, {}), {2}: (12, {}), {1}: (11, {})} | custom-call | flops 1 | bytes 1 | tf_op jit(solution)/shard_map/consume/pallas_call | solution.py:238
  166.0 4.6 %consume.9 = (f32[256,1024]{1,0:T(8,128)}, bf16[256,1024]{1,0:T(8,128)(2,1)}, bf16[256,8192]{1,0:T(8,128)(2,1)}, bf16[1,256,256]{2,1,0:T(8,128)(2,1)}) custom-call(s32[4]{0:T(128)} %pad_add_fusion.core_ref.where_ref, f32[1]{0:T(128)} %bitcast.5.scale_ref, bf16[256,8192]{1,0:T(8,128)(2,1)} %hidden_ref.5, ...), custom_call_target="tpu_custom_call", output_to_operand_aliasing={{0}: (7, {}), {2}: (9, {})} | custom-call | flops 1 | bytes 1 | tf_op jit(solution)/shard_map/consume/pallas_call | solution.py:238
  170.6 0.5 collective-permute-start.23
  171.2 0.4 collective-permute-start.22
  171.6 1.8 collective-permute-done.11.refs_0_
  173.6 0.6 copy-done.13
  174.3 0.7 collective-permute-done.24.refs_6_
  175.1 4.2 %finish.1 = (bf16[256,8192]{1,0:T(8,128)(2,1)}, bf16[256,1024]{1,0:T(8,128)(2,1)}, bf16[512,1024]{1,0:T(8,128)(2,1)}) custom-call(s32[4]{0:T(128)} %pad_add_fusion.core_ref.where_ref, f32[1]{0:T(128)} %bitcast.5.scale_ref, bf16[3,256,256]{2,1,0:T(8,128)(2,1)} %copy-done.11, bf16[4,256,256]{2,1,0:T(8,128)(2,1)} %copy-done.9, ...), custom_call_target="tpu_custom_call", output_to_operand_aliasing={{0}: (9, {})} | custom-call | tf_op jit(solution)/shard_map/finish/pallas_call | solution.py:306
  (61 shorter events, 1.5 us)
Async XLA Ops:
  7.2 54.5 %all-gather.5.cloned.1.call-start = ((), (), s32[]{:S(2)}) async-start(), calls=%async_computation.3 | async-start | bytes 2621440 | tf_op jit(solution)/shard_map/all_gather | solution.py:338
  7.9 3.6 %copy-start = (bf16[256,1024]{1,0:T(8,128)(2,1)S(1)}, bf16[256,1024]{1,0:T(8,128)(2,1)}, u32[]{:S(2)}) copy-start(bf16[256,1024]{1,0:T(8,128)(2,1)} %refs_0_.9) | copy-start | bytes 1572868
  9.5 1.0 copy-start.1
  10.4 20.8 %copy-start.4 = (bf16[512,1024]{1,0:T(8,128)(2,1)S(1)}, bf16[512,1024]{1,0:T(8,128)(2,1)}, u32[]{:S(2)}) copy-start(bf16[512,1024]{1,0:T(8,128)(2,1)} %param.5) | copy-start | bytes 3145732
  11.5 15.0 %collective-permute-start.1 = (bf16[256,1024]{1,0:T(8,128)(2,1)S(1)}, bf16[256,1024]{1,0:T(8,128)(2,1)S(1)}, u32[]{:S(2)}, u32[]{:S(2)}) collective-permute-start(bf16[256,1024]{1,0:T(8,128)(2,1)S(1)} %copy-done), channel_id=1, source_target_pairs={{0,16},{16,0},{1,17},{17,1},{2,18},{18,2},{3,19},{19,3},{4,20},{20... | collective-permute-start | bytes 1572872 | tf_op jit(solution)/shard_map/ppermute | solution.py:25
  14.5 14.4 %collective-permute-start = (bf16[256,1024]{1,0:T(8,128)(2,1)S(1)}, bf16[256,1024]{1,0:T(8,128)(2,1)S(1)}, u32[]{:S(2)}, u32[]{:S(2)}) collective-permute-start(bf16[256,1024]{1,0:T(8,128)(2,1)S(1)} %copy-done), channel_id=1, source_target_pairs={{0,2},{2,0},{1,3},{3,1},{4,6},{6,4},{5,7},{7,5},{8,10},{10,8},{9,1... | collective-permute-start | bytes 1572872 | tf_op jit(solution)/shard_map/ppermute | solution.py:25
  26.5 4.9 %copy-start.6 = (bf16[256,1024]{1,0:T(8,128)(2,1)}, bf16[256,1024]{1,0:T(8,128)(2,1)S(1)}, u32[]{:S(2)}) copy-start(bf16[256,1024]{1,0:T(8,128)(2,1)S(1)} %collective-permute-done.1) | copy-start | bytes 1572868
  27.2 13.1 %collective-permute-start.2 = (bf16[128,1024]{1,0:T(8,128)(2,1)}, bf16[128,1024]{1,0:T(8,128)(2,1)S(1)}, u32[]{:S(2)}, u32[]{:S(2)}) collective-permute-start(bf16[128,1024]{1,0:T(8,128)(2,1)} %slice.16), channel_id=1, source_target_pairs={{0,2},{2,0},{1,3},{3,1},{4,6},{6,4},{5,7},{7,5},{8,10},{10,8},{9,1... | collective-permute-start | bytes 786440 | tf_op jit(solution)/shard_map/ppermute | solution.py:25
  29.0 2.4 %copy-start.7 = (bf16[256,1024]{1,0:T(8,128)(2,1)}, bf16[256,1024]{1,0:T(8,128)(2,1)S(1)}, u32[]{:S(2)}) copy-start(bf16[256,1024]{1,0:T(8,128)(2,1)S(1)} %collective-permute-done) | copy-start | bytes 1572868
  29.7 10.7 %collective-permute-start.3 = (bf16[128,1024]{1,0:T(8,128)(2,1)}, bf16[128,1024]{1,0:T(8,128)(2,1)}, u32[]{:S(2)}, u32[]{:S(2)}) collective-permute-start(bf16[128,1024]{1,0:T(8,128)(2,1)} %slice.17), channel_id=1, source_target_pairs={{0,16},{16,0},{1,17},{17,1},{2,18},{18,2},{3,19},{19,3},{4,20},{20... | collective-permute-start | bytes 786440 | tf_op jit(solution)/shard_map/ppermute | solution.py:25
  31.4 13.6 %collective-permute-start.5 = (bf16[16,1024]{1,0:T(8,128)(2,1)S(1)}, bf16[16,1024]{1,0:T(8,128)(2,1)S(1)}, u32[]{:S(2)}, u32[]{:S(2)}) collective-permute-start(bf16[16,1024]{1,0:T(8,128)(2,1)S(1)} %broadcast_in_dim.4), channel_id=1, source_target_pairs={{0,4},{4,0},{8,12},{12,8},{1,5},{5,1},{9,13},{13,9},{2,6},{6,2},{1... | collective-permute-start | bytes 98312 | tf_op jit(solution)/shard_map/ppermute | solution.py:25
  40.4 54.2 %all-to-all-start = ((bf16[8,256,1024]{2,1,0:T(8,128)(2,1)}), bf16[8,256,1024]{2,1,0:T(8,128)(2,1)}, u32[]{:S(2)}, u32[]{:S(2)}) async-start(bf16[8,256,1024]{2,1,0:T(8,128)(2,1)} %get-tuple-element.79), calls=%async_computation | async-start | bytes 8388608 | tf_op jit(solution)/shard_map/all_to_all | solution.py:347
  45.0 91.0 %all-gather.7.cloned.1.call-start = ((), (), s32[]{:S(2)}) async-start(), calls=%async_computation.4 | async-start | bytes 2621440 | tf_op jit(solution)/shard_map/all_gather | solution.py:340
  45.1 16.7 %collective-permute-start.6 = (bf16[16,1024]{1,0:T(8,128)(2,1)S(1)}, bf16[16,1024]{1,0:T(8,128)(2,1)S(1)}, u32[]{:S(2)}, u32[]{:S(2)}) collective-permute-start(bf16[16,1024]{1,0:T(8,128)(2,1)S(1)} %broadcast_maximum_fusion), channel_id=1, source_target_pairs={{0,8},{4,12},{8,0},{12,4},{1,9},{5,13},{9,1},{13,5},{2,10},{6,14},... | collective-permute-start | bytes 98312 | tf_op jit(solution)/shard_map/ppermute | solution.py:25
  61.7 6.9 %copy-start.2 = (bf16[1024,1024]{1,0:T(8,128)(2,1)S(1)}, bf16[1024,1024]{1,0:T(8,128)(2,1)}, u32[]{:S(2)}) copy-start(bf16[1024,1024]{1,0:T(8,128)(2,1)} %all-gather.5.cloned.1.call-done) | copy-start | bytes 6291460
  61.7 91.0 %reduce-scatter.2.cloned.1.call-start = ((), (), s32[]{:S(2)}) async-start(), calls=%async_computation.2 | async-start | bytes 2621440 | tf_op jit(solution)/shard_map/reduce_scatter | solution.py:371
  68.1 4.5 %collective-permute-start.7 = (bf16[1024,1024]{1,0:T(8,128)(2,1)}, bf16[1024,1024]{1,0:T(8,128)(2,1)}, u32[]{:S(2)}, u32[]{:S(2)}) collective-permute-start(bf16[1024,1024]{1,0:T(8,128)(2,1)} %constant_dynamic-update-slice_fusion.refs_0_), channel_id=1, source_target_pairs={{0,1},{1,0},{2,3},{3,2},{4,5},{5,4},{6,7},{7,6},{8,9},{9,8},{10,11... | collective-permute-start | bytes 6291464 | tf_op jit(solution)/shard_map/ppermute | solution.py:25
  68.1 7.5 %collective-permute-start.4 = (bf16[8,256,512]{2,1,0:T(8,128)(2,1)}, bf16[8,256,512]{2,1,0:T(8,128)(2,1)}, u32[]{:S(2)}, u32[]{:S(2)}) collective-permute-start(bf16[8,256,512]{2,1,0:T(8,128)(2,1)} %get-tuple-element.80), channel_id=1, source_target_pairs={{0,1},{1,0},{2,3},{3,2},{4,5},{5,4},{6,7},{7,6},{8,9},{9,8},{10,11... | collective-permute-start | bytes 6291464 | tf_op jit(solution)/shard_map/ppermute | solution.py:25
  68.6 4.0 %copy-start.5 = (bf16[256,1024]{1,0:T(8,128)(2,1)S(1)}, bf16[256,1024]{1,0:T(8,128)(2,1)}, u32[]{:S(2)}) copy-start(bf16[256,1024]{1,0:T(8,128)(2,1)} %get-tuple-element.93) | copy-start | bytes 1572868
  72.6 31.8 %collective-permute-start.8 = (bf16[256,1024]{1,0:T(8,128)(2,1)S(1)}, bf16[256,1024]{1,0:T(8,128)(2,1)}, u32[]{:S(2)}, u32[]{:S(2)}) collective-permute-start(bf16[256,1024]{1,0:T(8,128)(2,1)S(1)} %copy-done.5), channel_id=1, source_target_pairs={{0,2},{2,0},{1,3},{3,1},{4,6},{6,4},{5,7},{7,5},{8,10},{10,8},{9,1... | collective-permute-start | bytes 1572872 | tf_op jit(solution)/shard_map/ppermute | solution.py:25
  104.4 13.7 %collective-permute-start.10 = (bf16[256,1024]{1,0:T(8,128)(2,1)}, bf16[256,1024]{1,0:T(8,128)(2,1)S(1)}, u32[]{:S(2)}, u32[]{:S(2)}) collective-permute-start(bf16[256,1024]{1,0:T(8,128)(2,1)} %collective-permute-done.8.refs_2_), channel_id=1, source_target_pairs={{0,16},{16,0},{1,17},{17,1},{2,18},{18,2},{3,19},{19,3},{4,20},{20... | collective-permute-start | bytes 1572872 | tf_op jit(solution)/shard_map/ppermute | solution.py:25
  106.0 13.5 %collective-permute-start.9 = (bf16[256,1024]{1,0:T(8,128)(2,1)}, bf16[256,1024]{1,0:T(8,128)(2,1)}, u32[]{:S(2)}, u32[]{:S(2)}) collective-permute-start(bf16[256,1024]{1,0:T(8,128)(2,1)} %get-tuple-element.98), channel_id=1, source_target_pairs={{0,2},{2,0},{1,3},{3,1},{4,6},{6,4},{5,7},{7,5},{8,10},{10,8},{9,1... | collective-permute-start | bytes 1572872 | tf_op jit(solution)/shard_map/ppermute | solution.py:25
  118.2 1.3 copy-start.10
  119.5 13.7 %copy-start.8 = (bf16[272,1024]{1,0:T(8,128)(2,1)S(1)}, bf16[272,1024]{1,0:T(8,128)(2,1)}, u32[]{:S(2)}) copy-start(bf16[272,1024]{1,0:T(8,128)(2,1)} %pad_maximum_fusion) | copy-start | bytes 1671172
  119.5 15.1 %copy-start.15 = (bf16[1,256,256]{2,1,0:T(8,128)(2,1)S(1)}, bf16[1,256,256]{2,1,0:T(8,128)(2,1)}, u32[]{:S(2)}) copy-start(bf16[1,256,256]{2,1,0:T(8,128)(2,1)} %get-tuple-element.123) | copy-start | bytes 393220
  119.5 12.6 %collective-permute-start.13 = (bf16[256,1024]{1,0:T(8,128)(2,1)}, bf16[256,1024]{1,0:T(8,128)(2,1)}, u32[]{:S(2)}, u32[]{:S(2)}) collective-permute-start(bf16[256,1024]{1,0:T(8,128)(2,1)} %collective-permute-done.9.refs_4_), channel_id=1, source_target_pairs={{0,16},{16,0},{1,17},{17,1},{2,18},{18,2},{3,19},{19,3},{4,20},{20... | collective-permute-start | bytes 1572872 | tf_op jit(solution)/shard_map/ppermute | solution.py:25
  120.5 12.7 %collective-permute-start.12 = (bf16[256,1024]{1,0:T(8,128)(2,1)}, bf16[256,1024]{1,0:T(8,128)(2,1)}, u32[]{:S(2)}, u32[]{:S(2)}) collective-permute-start(bf16[256,1024]{1,0:T(8,128)(2,1)} %get-tuple-element.110), channel_id=1, source_target_pairs={{0,2},{2,0},{1,3},{3,1},{4,6},{6,4},{5,7},{7,5},{8,10},{10,8},{9,1... | collective-permute-start | bytes 1572872 | tf_op jit(solution)/shard_map/ppermute | solution.py:25
  133.2 15.2 %collective-permute-start.14 = (bf16[272,1024]{1,0:T(8,128)(2,1)S(1)}, bf16[272,1024]{1,0:T(8,128)(2,1)}, u32[]{:S(2)}, u32[]{:S(2)}) collective-permute-start(bf16[272,1024]{1,0:T(8,128)(2,1)S(1)} %copy-done.8), channel_id=1, source_target_pairs={{0,2},{2,0},{1,3},{3,1},{4,6},{6,4},{5,7},{7,5},{8,10},{10,8},{9,1... | collective-permute-start | bytes 1671176 | tf_op jit(solution)/shard_map/ppermute | solution.py:25
  133.8 2.3 %collective-permute-start.16 = (bf16[4,256,256]{2,1,0:T(8,128)(2,1)}, bf16[4,256,256]{2,1,0:T(8,128)(2,1)}, u32[]{:S(2)}, u32[]{:S(2)}) collective-permute-start(bf16[4,256,256]{2,1,0:T(8,128)(2,1)} %get-tuple-element.122), channel_id=1, source_target_pairs={{0,1},{1,0},{2,3},{3,2},{4,5},{5,4},{6,7},{7,6},{8,9},{9,8},{10,11... | collective-permute-start | bytes 1572872 | tf_op jit(solution)/shard_map/ppermute | solution.py:25
  133.8 14.7 %collective-permute-start.15 = (bf16[256,1024]{1,0:T(8,128)(2,1)}, bf16[256,1024]{1,0:T(8,128)(2,1)}, u32[]{:S(2)}, u32[]{:S(2)}) collective-permute-start(bf16[256,1024]{1,0:T(8,128)(2,1)} %collective-permute-done.12.refs_3_), channel_id=1, source_target_pairs={{0,16},{16,0},{1,17},{17,1},{2,18},{18,2},{3,19},{19,3},{4,20},{20... | collective-permute-start | bytes 1572872 | tf_op jit(solution)/shard_map/ppermute | solution.py:25
  134.6 1.3 collective-permute-start.17
  136.0 0.7 copy-start.14
  143.2 14.4 %collective-permute-start.18 = (bf16[3,256,256]{2,1,0:T(8,128)(2,1)}, bf16[3,256,256]{2,1,0:T(8,128)(2,1)S(1)}, u32[]{:S(2)}, u32[]{:S(2)}) collective-permute-start(bf16[3,256,256]{2,1,0:T(8,128)(2,1)} %get-tuple-element.132), channel_id=1, source_target_pairs={{0,1},{1,0},{2,3},{3,2},{4,5},{5,4},{6,7},{7,6},{8,9},{9,8},{10,11... | collective-permute-start | bytes 1179656 | tf_op jit(solution)/shard_map/ppermute | solution.py:25
  148.4 17.5 %collective-permute-start.20 = (bf16[272,1024]{1,0:T(8,128)(2,1)}, bf16[272,1024]{1,0:T(8,128)(2,1)}, u32[]{:S(2)}, u32[]{:S(2)}) collective-permute-start(bf16[272,1024]{1,0:T(8,128)(2,1)} %collective-permute-done.14.refs_5_), channel_id=1, source_target_pairs={{0,16},{16,0},{1,17},{17,1},{2,18},{18,2},{3,19},{19,3},{4,20},{20... | collective-permute-start | bytes 1671176 | tf_op jit(solution)/shard_map/ppermute | solution.py:25
  152.0 4.3 %collective-permute-start.21 = (f32[8,128]{1,0:T(8,128)S(1)}, f32[8,128]{1,0:T(8,128)S(1)}, u32[]{:S(2)}, u32[]{:S(2)}) collective-permute-start(f32[8,128]{1,0:T(8,128)S(1)} %broadcast_in_dim.10), channel_id=1, source_target_pairs={{0,1},{1,0},{2,3},{3,2},{4,5},{5,4},{6,7},{7,6},{8,9},{9,8},{10,11... | collective-permute-start | bytes 12296 | tf_op jit(solution)/shard_map/ppermute | solution.py:25
  153.8 12.0 %copy-start.3 = (bf16[256,1024]{1,0:T(8,128)(2,1)}, bf16[256,1024]{1,0:T(8,128)(2,1)S(1)}, u32[]{:S(2)}) copy-start(bf16[256,1024]{1,0:T(8,128)(2,1)S(1)} %multiply_convert_fusion.refs_5_) | copy-start | bytes 1572868
  154.8 20.2 %collective-permute-start.24 = (bf16[272,1024]{1,0:T(8,128)(2,1)}, bf16[272,1024]{1,0:T(8,128)(2,1)}, u32[]{:S(2)}, u32[]{:S(2)}) collective-permute-start(bf16[272,1024]{1,0:T(8,128)(2,1)} %pad.4), channel_id=1, source_target_pairs={{0,16},{16,0},{1,17},{17,1},{2,18},{18,2},{3,19},{19,3},{4,20},{20... | collective-permute-start | bytes 1671176 | tf_op jit(solution)/shard_map/ppermute | solution.py:25
  157.6 0.8 copy-start.12
  165.9 7.7 %collective-permute-start.19 = (bf16[4,256,256]{2,1,0:T(8,128)(2,1)}, bf16[4,256,256]{2,1,0:T(8,128)(2,1)S(1)}, u32[]{:S(2)}, u32[]{:S(2)}) collective-permute-start(bf16[4,256,256]{2,1,0:T(8,128)(2,1)} %get-tuple-element.133), channel_id=1, source_target_pairs={{0,1},{1,0},{2,3},{3,2},{4,5},{5,4},{6,7},{7,6},{8,9},{9,8},{10,11... | collective-permute-start | bytes 1572872 | tf_op jit(solution)/shard_map/ppermute | solution.py:25
  170.6 3.7 %collective-permute-start.23 = (bf16[256,1024]{1,0:T(8,128)(2,1)}, bf16[256,1024]{1,0:T(8,128)(2,1)}, u32[]{:S(2)}, u32[]{:S(2)}) collective-permute-start(bf16[256,1024]{1,0:T(8,128)(2,1)} %get-tuple-element.143), channel_id=1, source_target_pairs={{0,1},{1,0},{2,3},{3,2},{4,5},{5,4},{6,7},{7,6},{8,9},{9,8},{10,11... | collective-permute-start | bytes 1572872 | tf_op jit(solution)/shard_map/ppermute | solution.py:25
  171.1 2.3 %collective-permute-start.11 = (bf16[3,256,256]{2,1,0:T(8,128)(2,1)}, bf16[3,256,256]{2,1,0:T(8,128)(2,1)S(1)}, u32[]{:S(2)}, u32[]{:S(2)}) collective-permute-start(bf16[3,256,256]{2,1,0:T(8,128)(2,1)} %get-tuple-element.109), channel_id=1, source_target_pairs={{0,1},{1,0},{2,3},{3,2},{4,5},{5,4},{6,7},{7,6},{8,9},{9,8},{10,11... | collective-permute-start | bytes 1179656 | tf_op jit(solution)/shard_map/ppermute | solution.py:25
  171.2 2.4 %collective-permute-start.22 = (bf16[1,256,256]{2,1,0:T(8,128)(2,1)}, bf16[1,256,256]{2,1,0:T(8,128)(2,1)S(1)}, u32[]{:S(2)}, u32[]{:S(2)}) collective-permute-start(bf16[1,256,256]{2,1,0:T(8,128)(2,1)} %get-tuple-element.141), channel_id=1, source_target_pairs={{0,1},{1,0},{2,3},{3,2},{4,5},{5,4},{6,7},{7,6},{8,9},{9,8},{10,11... | collective-permute-start | bytes 393224 | tf_op jit(solution)/shard_map/ppermute | solution.py:25
  173.4 1.5 copy-start.11
  173.6 0.7 copy-start.13
  174.3 0.8 copy-start.9
Sparse Core Ops, SparseCore 0:
  11.6 49.9 all-gather.4
  63.2 44.5 all-gather.6
  110.2 42.4 reduce-scatter.1

commit v3 on v2

--- a/solution.py
+++ b/solution.py
@@ -280,13 +280,13 @@
     return pl.ds(pl.multiple_of(at, half), half)
 
 
-def finish(where, scale, gradient, arrived, units, sums, shares):
-    half, features = shares[0].shape
+def finish(where, scale, gradient, arrived, units, sums):
+    half = arrived[0].shape[2]
     counts = [len(some) for some in units]
 
     def kernel(where_ref, scale_ref, *refs):
         arrived_refs, refs = refs[: len(units)], refs[len(units) :]
-        a_ref, b_ref, mine_ref, theirs_ref, _, gradient_ref, keys_ref, weight_ref, sem = refs
+        a_ref, b_ref, _, gradient_ref, keys_ref, sem = refs
         copies = []
         for ref, some in zip(arrived_refs, units):
             for e, unit in enumerate(some):
@@ -296,9 +296,6 @@
                 )
         for copy in copies:
             copy.start()
-        at = pl.multiple_of(where_ref[2] * half, half)
-        weight_ref[pl.ds(at, half), :] = mine_ref[...]
-        weight_ref[pl.ds(half - at, half), :] = theirs_ref[pl.ds(0, half), :]
         keys_ref[...] = ((a_ref[...] + b_ref[...].astype(F32)) * scale_ref[0]).astype(BF16)
         for copy in copies:
             copy.wait()
@@ -308,15 +305,32 @@
         out_shape=[
             jax.ShapeDtypeStruct(gradient.shape, BF16),
             jax.ShapeDtypeStruct(sums[0].shape, BF16),
-            jax.ShapeDtypeStruct((2 * half, features), BF16),
         ],
-        in_specs=[SMEM, SMEM] + [VMEM] * (len(units) + 4) + [ANY],
-        out_specs=[ANY, VMEM, VMEM],
-        input_output_aliases={len(units) + 6: 0},
+        in_specs=[SMEM, SMEM] + [VMEM] * (len(units) + 2) + [ANY],
+        out_specs=[ANY, VMEM],
+        input_output_aliases={len(units) + 4: 0},
         scratch_shapes=[pltpu.SemaphoreType.DMA((sum(counts),))],
         compiler_params=PARAMS,
         name="finish",
-    )(where, scale, *arrived, *sums, *shares, gradient)
+    )(where, scale, *arrived, *sums, gradient)
+
+
+def join(where, mine, theirs):
+    half, features = mine.shape
+
+    def kernel(where_ref, mine_ref, theirs_ref, out_ref):
+        at = pl.multiple_of(where_ref[2] * half, half)
+        out_ref[pl.ds(at, half), :] = mine_ref[...]
+        out_ref[pl.ds(half - at, half), :] = theirs_ref[pl.ds(0, half), :]
+
+    return pl.pallas_call(
+        kernel,
+        out_shape=jax.ShapeDtypeStruct((2 * half, features), BF16),
+        in_specs=[SMEM, VMEM, VMEM],
+        out_specs=VMEM,
+        compiler_params=PARAMS,
+        name="join",
+    )(where, mine, theirs)
 
 
 def body(hidden, key_weight, previous_peak, cotangent):
@@ -340,9 +354,10 @@
     theirs = lax.all_gather(rest, "z", axis=0)
 
     cots = [swap(cotangent, "x"), swap(cotangent, "replica")]
+    for_group, for_other = pack(where, hidden, rows, nz)
+    for_group, *cots = lax.optimization_barrier((for_group, *cots))
     cut = tokens // 2
     cots += [swap(cots[1][:cut], "x"), swap(cots[0][cut:], "replica")]
-    for_group, for_other = pack(where, hidden, rows, nz)
     for_group, *cots = lax.optimization_barrier((for_group, *cots))
     swapped = lax.all_to_all(for_group, ("replica", "x", "core"), 0, 0, tiled=True)
     peaks = jnp.max(jnp.abs(key_weight), axis=0, keepdims=True)
@@ -358,46 +373,47 @@
     slots = jnp.stack(slots).astype(jnp.int32)
     other = swap(for_other, "core")
 
-    parts = [own] + [lax.dynamic_index_in_dim(mine, z ^ k, keepdims=False) for k in (1, 2, 3)]
-    parts[3] = jnp.concatenate([parts[3], peaks])
-    swapped, other = lax.optimization_barrier((swapped, other))
-    stage = functools.partial(consume, where, scale, hidden, other, [cotangent, cots[1]])
-
+    parts = [jnp.concatenate([own, peaks])]
+    parts += [lax.dynamic_index_in_dim(mine, z ^ k, keepdims=False) for k in (1, 2, 3)]
     cots[1], *parts = lax.optimization_barrier((cots[1], *parts))
     side0 = swap(parts[0], "x")
+    swapped, other = lax.optimization_barrier((swapped, other))
     term = weight_terms(slots, swapped, cots, (0, 1, 2, 3), [])
+    stage = functools.partial(consume, where, scale, hidden, other, [cotangent, cots[1]])
+
+    def codes_of(units):
+        return [unit for _, _, unit in units]
 
     term, side0, *parts = lax.optimization_barrier((term, side0, *parts))
     total = lax.psum_scatter(term, "z", scatter_dimension=0, tiled=True).astype(F32)
-    side1, other0 = swap(parts[1], "x"), swap(side0, "replica")
-    units = [(codes, None, (0, 0, part)) for part in (0, 1)]
-    units += [(mine, None, (k, 0, 0)) for k in (1, 2, 3)]
+    side1, other0 = swap(parts[1], "x"), swap(side0[:half], "replica")
+    units = [(codes, None, (0, 0, part)) for part in (0, 1)] + [(mine, None, (k, 0, 0)) for k in (1, 2, 3)]
     *state, away0, away1 = stage(units, [], None)
-    arrived = ([swap(away0, "core"), swap(away1, "core")], [unit for _, _, unit in units])
+    first = ([swap(away0, "core"), swap(away1, "core")], codes_of(units))
 
     side1, other0, *rest = lax.optimization_barrier((side1, other0, *state, *parts))
     state, parts = rest[:3], rest[3:]
     side2, other1 = swap(parts[2], "x"), swap(side1, "replica")
-    units = [(side0, 0, (0, 1, 0)), (other0, 0, (0, 1, 1)), (side1, 0, (1, 1, 0))]
+    units = [(side0, 0, (0, 1, 0)), (other0, 0, (0, 1, 1)), (side1, 0, (1, 1, 0)), (theirs, None, (1, 0, 1))]
     *state, away = stage(units, state, None)
-    late = [swap(away, "core")]
-    late_units = [[unit for _, _, unit in units]]
+    second = ([swap(away, "core")], codes_of(units))
 
     side2, other1, *rest = lax.optimization_barrier((side2, other1, *state, *parts))
     state, parts = rest[:3], rest[3:]
     side3, other2 = swap(parts[3], "x"), swap(side2, "replica")
-    units = [(theirs, None, (k, 0, 1)) for k in (1, 2, 3)]
-    *state, away = stage(units, state, arrived)
-    arrived = ([swap(away, "core")], [unit for _, _, unit in units])
-
-    side3, other2, *state = lax.optimization_barrier((side3, other2, *state))
-    other3 = swap(side3, "replica")
-    units = [(other1, 0, (1, 1, 1)), (side2, 0, (2, 1, 0)), (other2, 0, (2, 1, 1)), (side3, 0, (3, 1, 0))]
-    *state, away = stage(units, state, arrived)
+    units = [(theirs, None, (2, 0, 1)), (theirs, None, (3, 0, 1)), (other1, 0, (1, 1, 1)), (side2, 0, (2, 1, 0))]
+    *state, away = stage(units, state, first)
+    late, late_units = [swap(away, "core")], [codes_of(units)]
+
+    rest = lax.dynamic_index_in_dim(theirs, z ^ 3, keepdims=False)
+    side3, other2, rest, *state = lax.optimization_barrier((side3, other2, rest, *state))
+    other3 = swap(rest, "x")
+    units = [(other2, 0, (2, 1, 1)), (side3, 0, (3, 1, 0))]
+    *state, away = stage(units, state, second)
     late.append(swap(away, "core"))
-    late_units.append([unit for _, _, unit in units])
-
-    peak = jnp.maximum(jnp.max(peaks), jnp.max(side3[half:]))
+    late_units.append(codes_of(units))
+
+    peak = jnp.maximum(jnp.max(peaks), jnp.max(side0[half:]))
     peak = jnp.full((8, 128), peak.astype(F32))
     peak = jnp.maximum(peak, swap(peak, "core"))
     peak_ratio = (peak[0, 0] / limit).reshape(1)
@@ -409,9 +425,8 @@
     late.append(swap(away, "core"))
     late_units.append([(3, 1, 1)])
     sums = [state[0], swap(state[1], "core")]
-    input_gradient, projected_keys, weight_gradient = finish(
-        where, scale, state[2], late, late_units, sums, [share, other_share]
-    )
+    input_gradient, projected_keys = finish(where, scale, state[2], late, late_units, sums)
+    weight_gradient = join(where, share, other_share)
     return (projected_keys, input_gradient, weight_gradient, peak_ratio)
 
 

time: 188 us -> 186 us (0.989)
  waiting for transfers between devices: 64.6 us -> 58.9 us
  local copies, waits for them, and re-layouts: 16.1 us -> 18.7 us
    ppermute x25, waiting for transfers between devices: 31.8 us -> 22.4 us  [swap(): return lax.ppermute(block, axis, [(i, i ^ mask) for i in range(size)])]
    reduce_scatter x1, waiting for transfers between devices: 0.61 us -> 4.33 us  [body(): lax.psum_scatter(term, 'z', scatter_dimension=0, tiled=True).astype(F32)]
    pallas_call x0 -> x1, Pallas kernels: none -> 2.26 us  [join(): pl.pallas_call(kernel, out_shape=jax.ShapeDtypeStruct((2 * half, features...]
    all_gather x1, waiting for transfers between devices: 13.1 us -> 15.3 us  [body(): mine = lax.all_gather(own, 'z', axis=0)]
    all_to_all x1, waiting for transfers between devices: 19 us -> 16.9 us  [body(): lax.all_to_all(for_group, ('replica', 'x', 'core'), 0, 0, tiled=True)]
    squeeze x0 -> x1, local copies, waits for them, and re-layouts: none -> 1.9 us  [body(): rest = lax.dynamic_index_in_dim(theirs, z ^ 3, keepdims=False)]
    unnamed x36 -> x28, local copies, waits for them, and re-layouts: 8.66 us -> 7.98 us
  transfers between devices with their start and end apart: 29 -> 29, of which waited for: 16 -> 17; matrix products, arithmetic and copies ran while one was open for 9% -> 11% of each run, Pallas kernels for 27% -> 29%
where the time goes in v3:
time: 186 us; the launch traced here: 185 us
  waiting for transfers between devices  58.9 us (32%)
  Pallas kernels  55.8 us (30%)
  starting transfers between devices  26.8 us (14%)
  local copies, waits for them, and re-layouts  18.7 us (10%)
  between operations  17.8 us (10%)
  other arithmetic  7.46 us (4%)
    pallas_call x5, Pallas kernels, consume(): pl.pallas_call(kernel, out_shape=[sums, jax.ShapeDtypeStruct(sums.shape,...  34 us
    ppermute x25, waiting for transfers between devices, swap(): return lax.ppermute(block, axis, [(i, i ^ mask) for i in range(size)])  22.4 us
    ppermute x25, starting transfers between devices, swap(): return lax.ppermute(block, axis, [(i, i ^ mask) for i in range(size)])  22.1 us
    all_to_all x1, waiting for transfers between devices, body(): lax.all_to_all(for_group, ('replica', 'x', 'core'), 0, 0, tiled=True)  16.9 us
    all_gather x1, waiting for transfers between devices, body(): mine = lax.all_gather(own, 'z', axis=0)  15.3 us
    pallas_call x1, Pallas kernels, weight_terms(): pl.pallas_call(kernel, out_shape=jax.ShapeDtypeStruct((width, features),...  9.44 us
    unnamed x28, local copies, waits for them, and re-layouts  7.98 us
    pallas_call x1, Pallas kernels, pack(): pl.pallas_call(kernel, out_shape=[jax.ShapeDtypeStruct((group, tokens, nz...  6.63 us
  transfers between devices with their start and end apart: 29, of which 17 were waited for; matrix products, arithmetic and copies ran while one was open for 11% of the time, Pallas kernels for 29%

profile of v3, /device:TPU:0, one launch (start us, length us, event | category | flops | bytes accessed | tf_op | source)
XLA Modules:
  0.0 185.5 jit_solution(18131335811031447382)
XLA Ops:
  7.9 1.5 clamp_convert_fusion.refs_2_
  9.5 1.0 copy-done.1
  10.4 1.0 constant_dynamic-slice_fusion
  11.5 3.0 %collective-permute-start.1 = (bf16[256,1024]{1,0:T(8,128)(2,1)S(1)}, bf16[256,1024]{1,0:T(8,128)(2,1)}, u32[]{:S(2)}, u32[]{:S(2)}) collective-permute-start(bf16[256,1024]{1,0:T(8,128)(2,1)S(1)} %copy-done), channel_id=1, source_target_pairs={{0,16},{16,0},{1,17},{17,1},{2,18},{18,2},{3,19},{19,3},{4,20},{20... | collective-permute-start | bytes 1572872 | tf_op jit(solution)/shard_map/ppermute | solution.py:25
  14.5 1.5 collective-permute-start
  16.0 0.6 pad_add_fusion.core_ref.where_ref
  16.6 6.6 %pack.1 = (bf16[8,256,1024]{2,1,0:T(8,128)(2,1)}, bf16[8,256,512]{2,1,0:T(8,128)(2,1)}) custom-call(s32[4]{0:T(128)} %pad_add_fusion.core_ref.where_ref, bf16[256,8192]{1,0:T(8,128)(2,1)} %hidden_ref.5), custom_call_target="tpu_custom_call" | custom-call | tf_op jit(solution)/shard_map/pack/pallas_call | solution.py:61
  23.2 3.3 %collective-permute-done.1 = bf16[256,1024]{1,0:T(8,128)(2,1)} collective-permute-done((bf16[256,1024]{1,0:T(8,128)(2,1)S(1)}, bf16[256,1024]{1,0:T(8,128)(2,1)}, u32[]{:S(2)}, u32[]{:S(2)}) %collective-permute-start.1) | collective-permute-done | bytes 524320 | tf_op jit(solution)/shard_map/ppermute | solution.py:25
  26.6 1.5 collective-permute-done
  28.0 1.0 slice.16
  29.0 1.0 slice.15
  30.0 1.6 collective-permute-start.2
  32.0 1.3 abs_reduce_fusion
  33.4 1.6 collective-permute-start.5
  35.0 1.9 collective-permute-done.2
  36.9 1.4 collective-permute-done.3
  38.2 4.6 %all-to-all-start = ((bf16[8,256,1024]{2,1,0:T(8,128)(2,1)}), bf16[8,256,1024]{2,1,0:T(8,128)(2,1)}, u32[]{:S(2)}, u32[]{:S(2)}) async-start(bf16[8,256,1024]{2,1,0:T(8,128)(2,1)} %get-tuple-element.85), calls=%async_computation | async-start | bytes 8388608 | tf_op jit(solution)/shard_map/all_to_all | solution.py:362
  42.9 2.6 %collective-permute-start.6 = (bf16[16,1024]{1,0:T(8,128)(2,1)S(1)}, bf16[16,1024]{1,0:T(8,128)(2,1)S(1)}, u32[]{:S(2)}, u32[]{:S(2)}) collective-permute-start(bf16[16,1024]{1,0:T(8,128)(2,1)S(1)} %broadcast_maximum_fusion), channel_id=1, source_target_pairs={{0,8},{4,12},{8,0},{12,4},{1,9},{5,13},{9,1},{13,5},{2,10},{6,14},... | collective-permute-start | bytes 98312 | tf_op jit(solution)/shard_map/ppermute | solution.py:25
  45.5 0.8 constant_dynamic-update-slice_fusion.4
  46.3 15.3 %all-gather.5.cloned.1.call-done = bf16[1024,1024]{1,0:T(8,128)(2,1)} async-done(((bf16[256,1024]{1,0:T(8,128)(2,1)}), bf16[1024,1024]{1,0:T(8,128)(2,1)}) %all-gather.5.cloned.1.call-update) | async-done | bytes 2097168 | tf_op jit(solution)/shard_map/all_gather | solution.py:352
  61.7 2.1 %constant_dynamic-update-slice_fusion.3 = bf16[1024,1024]{1,0:T(8,128)(2,1)} fusion(bf16[1024,1024]{1,0:T(8,128)(2,1)} %constant_dynamic-update-slice_fusion.4, bf16[256,1024]{1,0:T(8,128)(2,1)} %collective-permute-done), kind=kLoop, calls=%fused_computation.13 | loop fusion | bytes 1048576
  63.8 1.9 %constant_dynamic-update-slice_fusion.2 = bf16[1024,1024]{1,0:T(8,128)(2,1)} fusion(bf16[1024,1024]{1,0:T(8,128)(2,1)} %constant_dynamic-update-slice_fusion.3, bf16[256,1024]{1,0:T(8,128)(2,1)} %collective-permute-done.1), kind=kLoop, calls=%fused_computation.12 | loop fusion | bytes 1048576
  65.7 0.7 constant_dynamic-update-slice_fusion.1
  66.4 1.7 constant_dynamic-update-slice_fusion.refs_0_
  68.0 0.5 collective-permute-start.4
  68.6 0.8 pad_maximum_fusion
  69.4 1.2 dynamic-slice_bitcast_fusion.1
  70.6 1.9 %collective-permute-done.7.refs_1_ = bf16[1024,1024]{1,0:T(8,128)(2,1)} collective-permute-done((bf16[1024,1024]{1,0:T(8,128)(2,1)}, bf16[1024,1024]{1,0:T(8,128)(2,1)}, u32[]{:S(2)}, u32[]{:S(2)}) %collective-permute-start.7) | collective-permute-done | bytes 2097184 | tf_op jit(solution)/shard_map/ppermute | solution.py:25
  72.5 1.4 collective-permute-start.8
  74.0 0.6 stack.55.slots_ref
  74.6 1.0 collective-permute-done.4.other_ref
  75.5 16.9 %all-to-all-done.swapped_ref = bf16[8,256,1024]{2,1,0:T(8,128)(2,1)} async-done(((bf16[8,256,1024]{2,1,0:T(8,128)(2,1)}), bf16[8,256,1024]{2,1,0:T(8,128)(2,1)}, u32[]{:S(2)}, u32[]{:S(2)}) %all-to-all-start) | async-done | bytes 4194336 | tf_op jit(solution)/shard_map/all_to_all | solution.py:362
  92.4 9.4 %weight_terms.1 = bf16[1024,1024]{1,0:T(8,128)(2,1)} custom-call(s32[8]{0:T(128)} %stack.55.slots_ref, bf16[8,256,1024]{2,1,0:T(8,128)(2,1)} %all-to-all-done.swapped_ref, bf16[1024,1024]{1,0:T(8,128)(2,1)} %constant_dynamic-update-slice_fusion.refs_0_, bf16[1024,1024]{1,0:T(8,128)(2,1)} %collective-permute-done.7.refs_1_), custom_call_target="tpu_custom_call" | custom-call | flops 1 | bytes 1 | tf_op jit(solution)/shard_map/weight_terms/pallas_call | solution.py:111
  101.9 1.0 collective-permute-done.8.refs_2_
  102.9 0.9 slice.17
  103.8 1.5 collective-permute-start.10
  105.2 0.6 collective-permute-start.9
  105.8 8.7 %consume.5 = (f32[256,1024]{1,0:T(8,128)}, f32[256,1024]{1,0:T(8,128)}, bf16[256,8192]{1,0:T(8,128)(2,1)}, bf16[4,256,256]{2,1,0:T(8,128)(2,1)}, bf16[1,256,256]{2,1,0:T(8,128)(2,1)}) custom-call(s32[4]{0:T(128)} %pad_add_fusion.core_ref.where_ref, f32[1]{0:T(128)} %bitcast.5.scale_ref, bf16[256,8192]{1,0:T(8,128)(2,1)} %hidden_ref.5, ...), custom_call_target="tpu_custom_call" | custom-call | flops 1 | bytes 1 | tf_op jit(solution)/shard_map/consume/pallas_call | solution.py:238
  114.6 3.0 %collective-permute-done.10.refs_3_ = bf16[256,1024]{1,0:T(8,128)(2,1)} collective-permute-done((bf16[256,1024]{1,0:T(8,128)(2,1)}, bf16[256,1024]{1,0:T(8,128)(2,1)}, u32[]{:S(2)}, u32[]{:S(2)}) %collective-permute-start.10) | collective-permute-done | bytes 524320 | tf_op jit(solution)/shard_map/ppermute | solution.py:25
  117.6 1.2 collective-permute-done.9.refs_4_
  118.9 0.6 collective-permute-start.11
  119.4 0.6 collective-permute-start.12
  120.0 7.6 %consume.6 = (f32[256,1024]{1,0:T(8,128)}, f32[256,1024]{1,0:T(8,128)}, bf16[256,8192]{1,0:T(8,128)(2,1)}, bf16[4,256,256]{2,1,0:T(8,128)(2,1)}) custom-call(s32[4]{0:T(128)} %pad_add_fusion.core_ref.where_ref, f32[1]{0:T(128)} %bitcast.5.scale_ref, bf16[256,8192]{1,0:T(8,128)(2,1)} %hidden_ref.5, ...), custom_call_target="tpu_custom_call", output_to_operand_aliasing={{0}: (10, {}), {2}: (12, {}), {1}: (11, {})} | custom-call | flops 1 | bytes 1 | tf_op jit(solution)/shard_map/consume/pallas_call | solution.py:238
  127.6 3.9 %collective-permute-done.11.refs_4_ = bf16[256,1024]{1,0:T(8,128)(2,1)} collective-permute-done((bf16[256,1024]{1,0:T(8,128)(2,1)}, bf16[256,1024]{1,0:T(8,128)(2,1)}, u32[]{:S(2)}, u32[]{:S(2)}) %collective-permute-start.11) | collective-permute-done | bytes 524320 | tf_op jit(solution)/shard_map/ppermute | solution.py:25
  131.9 1.4 collective-permute-start.16
  133.3 0.6 collective-permute-start.17
  133.9 0.6 reduce_max.28
  134.5 0.5 collective-permute-start.18
  135.2 0.7 copy-done.9
  135.9 7.6 %consume.7 = (f32[256,1024]{1,0:T(8,128)}, f32[256,1024]{1,0:T(8,128)}, bf16[256,8192]{1,0:T(8,128)(2,1)}, bf16[4,256,256]{2,1,0:T(8,128)(2,1)}) custom-call(s32[4]{0:T(128)} %pad_add_fusion.core_ref.where_ref, f32[1]{0:T(128)} %bitcast.5.scale_ref, bf16[256,8192]{1,0:T(8,128)(2,1)} %hidden_ref.5, ...), custom_call_target="tpu_custom_call", output_to_operand_aliasing={{0}: (9, {}), {2}: (11, {}), {1}: (10, {})} | custom-call | flops 1 | bytes 1 | tf_op jit(solution)/shard_map/consume/pallas_call | solution.py:238
  143.5 1.9 %dynamic-slice_bitcast_fusion = bf16[256,1024]{1,0:T(8,128)(2,1)} fusion(bf16[4,256,1024]{2,1,0:T(8,128)(2,1)} %bitcast.31, s32[]{:T(128)S(6)} %select_n.21), kind=kLoop, calls=%fused_computation.4 | loop fusion | bytes 1048580 | tf_op jit(solution)/shard_map/jit(dynamic_index_in_dim)/squeeze | solution.py:408
  145.4 0.9 collective-permute-start.20
  146.3 1.4 slice_reduce_fusion
  149.1 4.3 %reduce-scatter.2.cloned.1.call-done = bf16[256,1024]{1,0:T(8,128)(2,1)} async-done(((bf16[1024,1024]{1,0:T(8,128)(2,1)}), bf16[256,1024]{1,0:T(8,128)(2,1)}) %reduce-scatter.2.cloned.1.call-update) | async-done | bytes 524304 | tf_op jit(solution)/shard_map/reduce_scatter | solution.py:388
  153.4 1.1 multiply_convert_fusion.mine_ref
  154.6 0.9 pad.4
  155.5 1.5 collective-permute-start.24
  157.0 0.5 slice.19
  158.2 5.5 %consume.8 = (f32[256,1024]{1,0:T(8,128)}, f32[256,1024]{1,0:T(8,128)}, bf16[256,8192]{1,0:T(8,128)(2,1)}, bf16[2,256,256]{2,1,0:T(8,128)(2,1)}) custom-call(s32[4]{0:T(128)} %pad_add_fusion.core_ref.where_ref, f32[1]{0:T(128)} %bitcast.5.scale_ref, bf16[256,8192]{1,0:T(8,128)(2,1)} %hidden_ref.5, ...), custom_call_target="tpu_custom_call", output_to_operand_aliasing={{0}: (8, {}), {2}: (10, {}), {1}: (9, {})} | custom-call | flops 1 | bytes 1 | tf_op jit(solution)/shard_map/consume/pallas_call | solution.py:238
  163.8 4.6 %consume.9 = (f32[256,1024]{1,0:T(8,128)}, bf16[256,1024]{1,0:T(8,128)(2,1)}, bf16[256,8192]{1,0:T(8,128)(2,1)}, bf16[1,256,256]{2,1,0:T(8,128)(2,1)}) custom-call(s32[4]{0:T(128)} %pad_add_fusion.core_ref.where_ref, f32[1]{0:T(128)} %bitcast.5.scale_ref, bf16[256,8192]{1,0:T(8,128)(2,1)} %hidden_ref.5, ...), custom_call_target="tpu_custom_call", output_to_operand_aliasing={{0}: (7, {}), {2}: (9, {})} | custom-call | flops 1 | bytes 1 | tf_op jit(solution)/shard_map/consume/pallas_call | solution.py:238
  168.4 0.6 collective-permute-start.23
  169.5 1.6 collective-permute-done.19.refs_1_
  172.1 3.4 %finish.1 = (bf16[256,8192]{1,0:T(8,128)(2,1)}, bf16[256,1024]{1,0:T(8,128)(2,1)}) custom-call(s32[4]{0:T(128)} %pad_add_fusion.core_ref.where_ref, f32[1]{0:T(128)} %bitcast.5.scale_ref, bf16[4,256,256]{2,1,0:T(8,128)(2,1)} %collective-permute-done.15.refs_0_, bf16[2,256,256]{2,1,0:T(8,128)(2,1)} %copy-done.8, ...), custom_call_target="tpu_custom_call", output_to_operand_aliasing={{0}: (7, {})} | custom-call | tf_op jit(solution)/shard_map/finish/pallas_call | solution.py:303
  175.5 2.3 %join.1 = bf16[512,1024]{1,0:T(8,128)(2,1)} custom-call(s32[4]{0:T(128)} %pad_add_fusion.core_ref.where_ref, bf16[256,1024]{1,0:T(8,128)(2,1)} %copy-done.3, bf16[272,1024]{1,0:T(8,128)(2,1)} %collective-permute-done.24.theirs_ref), custom_call_target="tpu_custom_call" | custom-call | tf_op jit(solution)/shard_map/join/pallas_call | solution.py:326
  (56 shorter events, 3.0 us)
Async XLA Ops:
  7.2 54.4 %all-gather.5.cloned.1.call-start = ((), (), s32[]{:S(2)}) async-start(), calls=%async_computation.3 | async-start | bytes 2621440 | tf_op jit(solution)/shard_map/all_gather | solution.py:352
  7.9 3.6 %copy-start = (bf16[256,1024]{1,0:T(8,128)(2,1)S(1)}, bf16[256,1024]{1,0:T(8,128)(2,1)}, u32[]{:S(2)}) copy-start(bf16[256,1024]{1,0:T(8,128)(2,1)} %refs_0_.9) | copy-start | bytes 1572868
  9.5 1.0 copy-start.1
  11.5 15.1 %collective-permute-start.1 = (bf16[256,1024]{1,0:T(8,128)(2,1)S(1)}, bf16[256,1024]{1,0:T(8,128)(2,1)}, u32[]{:S(2)}, u32[]{:S(2)}) collective-permute-start(bf16[256,1024]{1,0:T(8,128)(2,1)S(1)} %copy-done), channel_id=1, source_target_pairs={{0,16},{16,0},{1,17},{17,1},{2,18},{18,2},{3,19},{19,3},{4,20},{20... | collective-permute-start | bytes 1572872 | tf_op jit(solution)/shard_map/ppermute | solution.py:25
  14.5 13.5 %collective-permute-start = (bf16[256,1024]{1,0:T(8,128)(2,1)S(1)}, bf16[256,1024]{1,0:T(8,128)(2,1)}, u32[]{:S(2)}, u32[]{:S(2)}) collective-permute-start(bf16[256,1024]{1,0:T(8,128)(2,1)S(1)} %copy-done), channel_id=1, source_target_pairs={{0,2},{2,0},{1,3},{3,1},{4,6},{6,4},{5,7},{7,5},{8,10},{10,8},{9,1... | collective-permute-start | bytes 1572872 | tf_op jit(solution)/shard_map/ppermute | solution.py:25
  30.0 6.9 %collective-permute-start.2 = (bf16[128,1024]{1,0:T(8,128)(2,1)S(1)}, bf16[128,1024]{1,0:T(8,128)(2,1)S(1)}, u32[]{:S(2)}, u32[]{:S(2)}) collective-permute-start(bf16[128,1024]{1,0:T(8,128)(2,1)S(1)} %slice.15), channel_id=1, source_target_pairs={{0,2},{2,0},{1,3},{3,1},{4,6},{6,4},{5,7},{7,5},{8,10},{10,8},{9,1... | collective-permute-start | bytes 786440 | tf_op jit(solution)/shard_map/ppermute | solution.py:25
  31.5 6.7 %collective-permute-start.3 = (bf16[128,1024]{1,0:T(8,128)(2,1)S(1)}, bf16[128,1024]{1,0:T(8,128)(2,1)}, u32[]{:S(2)}, u32[]{:S(2)}) collective-permute-start(bf16[128,1024]{1,0:T(8,128)(2,1)S(1)} %slice.16), channel_id=1, source_target_pairs={{0,16},{16,0},{1,17},{17,1},{2,18},{18,2},{3,19},{19,3},{4,20},{20... | collective-permute-start | bytes 786440 | tf_op jit(solution)/shard_map/ppermute | solution.py:25
  33.4 9.5 %collective-permute-start.5 = (bf16[16,1024]{1,0:T(8,128)(2,1)S(1)}, bf16[16,1024]{1,0:T(8,128)(2,1)S(1)}, u32[]{:S(2)}, u32[]{:S(2)}) collective-permute-start(bf16[16,1024]{1,0:T(8,128)(2,1)S(1)} %broadcast_in_dim.4), channel_id=1, source_target_pairs={{0,4},{4,0},{8,12},{12,8},{1,5},{5,1},{9,13},{13,9},{2,6},{6,2},{1... | collective-permute-start | bytes 98312 | tf_op jit(solution)/shard_map/ppermute | solution.py:25
  38.2 54.2 %all-to-all-start = ((bf16[8,256,1024]{2,1,0:T(8,128)(2,1)}), bf16[8,256,1024]{2,1,0:T(8,128)(2,1)}, u32[]{:S(2)}, u32[]{:S(2)}) async-start(bf16[8,256,1024]{2,1,0:T(8,128)(2,1)} %get-tuple-element.85), calls=%async_computation | async-start | bytes 8388608 | tf_op jit(solution)/shard_map/all_to_all | solution.py:362
  42.8 77.2 %all-gather.7.cloned.1.call-start = ((), (), s32[]{:S(2)}) async-start(), calls=%async_computation.4 | async-start | bytes 2621440 | tf_op jit(solution)/shard_map/all_gather | solution.py:354
  42.9 18.8 %collective-permute-start.6 = (bf16[16,1024]{1,0:T(8,128)(2,1)S(1)}, bf16[16,1024]{1,0:T(8,128)(2,1)S(1)}, u32[]{:S(2)}, u32[]{:S(2)}) collective-permute-start(bf16[16,1024]{1,0:T(8,128)(2,1)S(1)} %broadcast_maximum_fusion), channel_id=1, source_target_pairs={{0,8},{4,12},{8,0},{12,4},{1,9},{5,13},{9,1},{13,5},{2,10},{6,14},... | collective-permute-start | bytes 98312 | tf_op jit(solution)/shard_map/ppermute | solution.py:25
  46.3 22.2 %copy-start.4 = (bf16[256,1024]{1,0:T(8,128)(2,1)S(1)}, bf16[256,1024]{1,0:T(8,128)(2,1)}, u32[]{:S(2)}) copy-start(bf16[256,1024]{1,0:T(8,128)(2,1)} %get-tuple-element.93) | copy-start | bytes 1572868
  61.6 91.8 %reduce-scatter.2.cloned.1.call-start = ((), (), s32[]{:S(2)}) async-start(), calls=%async_computation.2 | async-start | bytes 2621440 | tf_op jit(solution)/shard_map/reduce_scatter | solution.py:388
  61.7 7.7 %copy-start.2 = (bf16[1024,1024]{1,0:T(8,128)(2,1)S(1)}, bf16[1024,1024]{1,0:T(8,128)(2,1)}, u32[]{:S(2)}) copy-start(bf16[1024,1024]{1,0:T(8,128)(2,1)} %all-gather.5.cloned.1.call-done) | copy-start | bytes 6291460
  68.0 4.5 %collective-permute-start.7 = (bf16[1024,1024]{1,0:T(8,128)(2,1)}, bf16[1024,1024]{1,0:T(8,128)(2,1)}, u32[]{:S(2)}, u32[]{:S(2)}) collective-permute-start(bf16[1024,1024]{1,0:T(8,128)(2,1)} %constant_dynamic-update-slice_fusion.refs_0_), channel_id=1, source_target_pairs={{0,1},{1,0},{2,3},{3,2},{4,5},{5,4},{6,7},{7,6},{8,9},{9,8},{10,11... | collective-permute-start | bytes 6291464 | tf_op jit(solution)/shard_map/ppermute | solution.py:25
  68.0 7.5 %collective-permute-start.4 = (bf16[8,256,512]{2,1,0:T(8,128)(2,1)}, bf16[8,256,512]{2,1,0:T(8,128)(2,1)}, u32[]{:S(2)}, u32[]{:S(2)}) collective-permute-start(bf16[8,256,512]{2,1,0:T(8,128)(2,1)} %get-tuple-element.86), channel_id=1, source_target_pairs={{0,1},{1,0},{2,3},{3,2},{4,5},{5,4},{6,7},{7,6},{8,9},{9,8},{10,11... | collective-permute-start | bytes 6291464 | tf_op jit(solution)/shard_map/ppermute | solution.py:25
  72.5 30.3 %collective-permute-start.8 = (bf16[272,1024]{1,0:T(8,128)(2,1)}, bf16[272,1024]{1,0:T(8,128)(2,1)S(1)}, u32[]{:S(2)}, u32[]{:S(2)}) collective-permute-start(bf16[272,1024]{1,0:T(8,128)(2,1)} %pad_maximum_fusion), channel_id=1, source_target_pairs={{0,2},{2,0},{1,3},{3,1},{4,6},{6,4},{5,7},{7,5},{8,10},{10,8},{9,1... | collective-permute-start | bytes 1671176 | tf_op jit(solution)/shard_map/ppermute | solution.py:25
  102.8 11.8 %copy-start.5 = (bf16[272,1024]{1,0:T(8,128)(2,1)}, bf16[272,1024]{1,0:T(8,128)(2,1)S(1)}, u32[]{:S(2)}) copy-start(bf16[272,1024]{1,0:T(8,128)(2,1)S(1)} %collective-permute-done.8.refs_2_) | copy-start | bytes 1671172
  103.8 13.9 %collective-permute-start.10 = (bf16[256,1024]{1,0:T(8,128)(2,1)}, bf16[256,1024]{1,0:T(8,128)(2,1)}, u32[]{:S(2)}, u32[]{:S(2)}) collective-permute-start(bf16[256,1024]{1,0:T(8,128)(2,1)} %slice.17), channel_id=1, source_target_pairs={{0,16},{16,0},{1,17},{17,1},{2,18},{18,2},{3,19},{19,3},{4,20},{20... | collective-permute-start | bytes 1572872 | tf_op jit(solution)/shard_map/ppermute | solution.py:25
  105.2 13.6 %collective-permute-start.9 = (bf16[256,1024]{1,0:T(8,128)(2,1)}, bf16[256,1024]{1,0:T(8,128)(2,1)}, u32[]{:S(2)}, u32[]{:S(2)}) collective-permute-start(bf16[256,1024]{1,0:T(8,128)(2,1)} %get-tuple-element.104), channel_id=1, source_target_pairs={{0,2},{2,0},{1,3},{3,1},{4,6},{6,4},{5,7},{7,5},{8,10},{10,8},{9,1... | collective-permute-start | bytes 1572872 | tf_op jit(solution)/shard_map/ppermute | solution.py:25
  118.9 12.7 %collective-permute-start.11 = (bf16[256,1024]{1,0:T(8,128)(2,1)}, bf16[256,1024]{1,0:T(8,128)(2,1)}, u32[]{:S(2)}, u32[]{:S(2)}) collective-permute-start(bf16[256,1024]{1,0:T(8,128)(2,1)} %get-tuple-element.111), channel_id=1, source_target_pairs={{0,2},{2,0},{1,3},{3,1},{4,6},{6,4},{5,7},{7,5},{8,10},{10,8},{9,1... | collective-permute-start | bytes 1572872 | tf_op jit(solution)/shard_map/ppermute | solution.py:25
  119.4 12.4 %collective-permute-start.12 = (bf16[256,1024]{1,0:T(8,128)(2,1)}, bf16[256,1024]{1,0:T(8,128)(2,1)}, u32[]{:S(2)}, u32[]{:S(2)}) collective-permute-start(bf16[256,1024]{1,0:T(8,128)(2,1)} %collective-permute-done.9.refs_4_), channel_id=1, source_target_pairs={{0,16},{16,0},{1,17},{17,1},{2,18},{18,2},{3,19},{19,3},{4,20},{20... | collective-permute-start | bytes 1572872 | tf_op jit(solution)/shard_map/ppermute | solution.py:25
  120.0 15.2 %collective-permute-start.13 = (bf16[4,256,256]{2,1,0:T(8,128)(2,1)}, bf16[4,256,256]{2,1,0:T(8,128)(2,1)}, u32[]{:S(2)}, u32[]{:S(2)}) collective-permute-start(bf16[4,256,256]{2,1,0:T(8,128)(2,1)} %get-tuple-element.126), channel_id=1, source_target_pairs={{0,1},{1,0},{2,3},{3,2},{4,5},{5,4},{6,7},{7,6},{8,9},{9,8},{10,11... | collective-permute-start | bytes 1572872 | tf_op jit(solution)/shard_map/ppermute | solution.py:25
  120.0 11.8 %copy-start.6 = (bf16[256,1024]{1,0:T(8,128)(2,1)S(1)}, bf16[256,1024]{1,0:T(8,128)(2,1)}, u32[]{:S(2)}) copy-start(bf16[256,1024]{1,0:T(8,128)(2,1)} %get-tuple-element.129) | copy-start | bytes 1572868
  120.0 13.9 %copy-start.11 = (bf16[1,256,256]{2,1,0:T(8,128)(2,1)S(1)}, bf16[1,256,256]{2,1,0:T(8,128)(2,1)}, u32[]{:S(2)}) copy-start(bf16[1,256,256]{2,1,0:T(8,128)(2,1)} %get-tuple-element.127) | copy-start | bytes 393220
  131.9 13.6 %collective-permute-start.16 = (bf16[256,1024]{1,0:T(8,128)(2,1)S(1)}, bf16[256,1024]{1,0:T(8,128)(2,1)}, u32[]{:S(2)}, u32[]{:S(2)}) collective-permute-start(bf16[256,1024]{1,0:T(8,128)(2,1)S(1)} %copy-done.6), channel_id=1, source_target_pairs={{0,2},{2,0},{1,3},{3,1},{4,6},{6,4},{5,7},{7,5},{8,10},{10,8},{9,1... | collective-permute-start | bytes 1572872 | tf_op jit(solution)/shard_map/ppermute | solution.py:25
  133.3 12.1 %collective-permute-start.17 = (bf16[256,1024]{1,0:T(8,128)(2,1)}, bf16[256,1024]{1,0:T(8,128)(2,1)}, u32[]{:S(2)}, u32[]{:S(2)}) collective-permute-start(bf16[256,1024]{1,0:T(8,128)(2,1)} %collective-permute-done.11.refs_4_), channel_id=1, source_target_pairs={{0,16},{16,0},{1,17},{17,1},{2,18},{18,2},{3,19},{19,3},{4,20},{20... | collective-permute-start | bytes 1572872 | tf_op jit(solution)/shard_map/ppermute | solution.py:25
  133.9 1.3 collective-permute-start.14
  134.5 23.7 %collective-permute-start.18 = (bf16[4,256,256]{2,1,0:T(8,128)(2,1)}, bf16[4,256,256]{2,1,0:T(8,128)(2,1)}, u32[]{:S(2)}, u32[]{:S(2)}) collective-permute-start(bf16[4,256,256]{2,1,0:T(8,128)(2,1)} %get-tuple-element.138), channel_id=1, source_target_pairs={{0,1},{1,0},{2,3},{3,2},{4,5},{5,4},{6,7},{7,6},{8,9},{9,8},{10,11... | collective-permute-start | bytes 1572872 | tf_op jit(solution)/shard_map/ppermute | solution.py:25
  135.2 0.7 copy-start.9
  145.4 18.4 %collective-permute-start.20 = (bf16[256,1024]{1,0:T(8,128)(2,1)}, bf16[256,1024]{1,0:T(8,128)(2,1)}, u32[]{:S(2)}, u32[]{:S(2)}) collective-permute-start(bf16[256,1024]{1,0:T(8,128)(2,1)} %dynamic-slice_bitcast_fusion), channel_id=1, source_target_pairs={{0,2},{2,0},{1,3},{3,1},{4,6},{6,4},{5,7},{7,5},{8,10},{10,8},{9,1... | collective-permute-start | bytes 1572872 | tf_op jit(solution)/shard_map/ppermute | solution.py:25
  149.0 8.0 %collective-permute-start.21 = (f32[8,128]{1,0:T(8,128)S(1)}, f32[8,128]{1,0:T(8,128)S(1)}, u32[]{:S(2)}, u32[]{:S(2)}) collective-permute-start(f32[8,128]{1,0:T(8,128)S(1)} %broadcast_in_dim.10), channel_id=1, source_target_pairs={{0,1},{1,0},{2,3},{3,2},{4,5},{5,4},{6,7},{7,6},{8,9},{9,8},{10,11... | collective-permute-start | bytes 12296 | tf_op jit(solution)/shard_map/ppermute | solution.py:25
  154.6 9.2 %copy-start.3 = (bf16[256,1024]{1,0:T(8,128)(2,1)}, bf16[256,1024]{1,0:T(8,128)(2,1)S(1)}, u32[]{:S(2)}) copy-start(bf16[256,1024]{1,0:T(8,128)(2,1)S(1)} %multiply_convert_fusion.mine_ref) | copy-start | bytes 1572868
  155.5 20.0 %collective-permute-start.24 = (bf16[272,1024]{1,0:T(8,128)(2,1)}, bf16[272,1024]{1,0:T(8,128)(2,1)}, u32[]{:S(2)}, u32[]{:S(2)}) collective-permute-start(bf16[272,1024]{1,0:T(8,128)(2,1)} %pad.4), channel_id=1, source_target_pairs={{0,16},{16,0},{1,17},{17,1},{2,18},{18,2},{3,19},{19,3},{4,20},{20... | collective-permute-start | bytes 1671176 | tf_op jit(solution)/shard_map/ppermute | solution.py:25
  158.2 11.3 %collective-permute-start.15 = (bf16[4,256,256]{2,1,0:T(8,128)(2,1)}, bf16[4,256,256]{2,1,0:T(8,128)(2,1)}, u32[]{:S(2)}, u32[]{:S(2)}) collective-permute-start(bf16[4,256,256]{2,1,0:T(8,128)(2,1)} %get-tuple-element.128), channel_id=1, source_target_pairs={{0,1},{1,0},{2,3},{3,2},{4,5},{5,4},{6,7},{7,6},{8,9},{9,8},{10,11... | collective-permute-start | bytes 1572872 | tf_op jit(solution)/shard_map/ppermute | solution.py:25
  168.4 2.9 %collective-permute-start.23 = (bf16[256,1024]{1,0:T(8,128)(2,1)}, bf16[256,1024]{1,0:T(8,128)(2,1)S(1)}, u32[]{:S(2)}, u32[]{:S(2)}) collective-permute-start(bf16[256,1024]{1,0:T(8,128)(2,1)} %get-tuple-element.150), channel_id=1, source_target_pairs={{0,1},{1,0},{2,3},{3,2},{4,5},{5,4},{6,7},{7,6},{8,9},{9,8},{10,11... | collective-permute-start | bytes 1572872 | tf_op jit(solution)/shard_map/ppermute | solution.py:25
  168.9 2.1 %collective-permute-start.19 = (bf16[2,256,256]{2,1,0:T(8,128)(2,1)}, bf16[2,256,256]{2,1,0:T(8,128)(2,1)S(1)}, u32[]{:S(2)}, u32[]{:S(2)}) collective-permute-start(bf16[2,256,256]{2,1,0:T(8,128)(2,1)} %get-tuple-element.139), channel_id=1, source_target_pairs={{0,1},{1,0},{2,3},{3,2},{4,5},{5,4},{6,7},{7,6},{8,9},{9,8},{10,11... | collective-permute-start | bytes 786440 | tf_op jit(solution)/shard_map/ppermute | solution.py:25
  169.0 2.2 %collective-permute-start.22 = (bf16[1,256,256]{2,1,0:T(8,128)(2,1)}, bf16[1,256,256]{2,1,0:T(8,128)(2,1)S(1)}, u32[]{:S(2)}, u32[]{:S(2)}) collective-permute-start(bf16[1,256,256]{2,1,0:T(8,128)(2,1)} %get-tuple-element.148), channel_id=1, source_target_pairs={{0,1},{1,0},{2,3},{3,2},{4,5},{5,4},{6,7},{7,6},{8,9},{9,8},{10,11... | collective-permute-start | bytes 393224 | tf_op jit(solution)/shard_map/ppermute | solution.py:25
  171.1 0.7 copy-start.8
  171.3 0.6 copy-start.10
  171.3 0.8 copy-start.7
Sparse Core Ops, SparseCore 0:
  11.6 49.9 all-gather.4
  63.8 44.7 all-gather.6
  110.8 42.5 reduce-scatter.1

commit v4 on v3

--- a/solution.py
+++ b/solution.py
@@ -79,12 +79,12 @@
     tile = width // 4
 
     def kernel(slots_ref, swapped_ref, *refs):
-        cots_ref, refs = refs[:2], refs[2 + len(state) :]
+        cots_ref, refs = refs[:4], refs[4 + len(state) :]
         out_ref, lhs, rhs, out, sem, out_sem = refs
         copies = []
         for s in range(sources):
             place = pl.ds(pl.multiple_of(slots_ref[s] * tokens, tokens), tokens)
-            source = cots_ref[s // 4].at[pl.ds(s % 4 * tokens, tokens)]
+            source = cots_ref[s // 4].at[pl.ds(s % 4 * tokens, tokens)] if s % 4 < 3 else cots_ref[2 + s // 4]
             copies.append(pltpu.make_async_copy(source, rhs.at[place], sem.at[count, s]))
         for i, t in enumerate(tiles):
             at = pl.ds(t * tile, tile)
@@ -111,9 +111,9 @@
     return pl.pallas_call(
         kernel,
         out_shape=jax.ShapeDtypeStruct((width, features), BF16),
-        in_specs=[SMEM] + [ANY] * (3 + len(state)),
+        in_specs=[SMEM] + [ANY] * (5 + len(state)),
         out_specs=ANY,
-        input_output_aliases={4: 0} if state else {},
+        input_output_aliases={6: 0} if state else {},
         scratch_shapes=[
             pltpu.VMEM((count, sources * tokens, tile), BF16),
             pltpu.VMEM((sources * tokens, features), BF16),
@@ -159,10 +159,7 @@
         for b, (array, row, (k, side, part)) in enumerate(units):
             ref = [r for r, known in zip(array_refs, arrays) if known is array][0]
             at = pl.multiple_of((1 - where_ref[2] if part else where_ref[2]) * half, half)
-            if len(array.shape) == 3:
-                source = ref.at[where_ref[3] ^ k]
-            else:
-                source = ref.at[pl.ds(at if row is None else row, half)]
+            source = ref.at[where_ref[3] ^ k] if row is None else ref.at[pl.ds(row, half)]
             block = (where_ref[3] ^ k) * 2 + (1 - where_ref[1] if side else where_ref[1])
             pairs = [
                 (source, wgt.at[b]),
@@ -280,39 +277,81 @@
     return pl.ds(pl.multiple_of(at, half), half)
 
 
-def finish(where, scale, gradient, arrived, units, sums):
-    half = arrived[0].shape[2]
+def finish(where, scale, hidden, cotangent, unit, weights, sums, gradient, arrived, units):
+    tokens, width = hidden.shape
+    half, features = weights[0].shape
     counts = [len(some) for some in units]
 
-    def kernel(where_ref, scale_ref, *refs):
-        arrived_refs, refs = refs[: len(units)], refs[len(units) :]
-        a_ref, b_ref, _, gradient_ref, keys_ref, sem = refs
-        copies = []
-        for ref, some in zip(arrived_refs, units):
-            for e, unit in enumerate(some):
-                columns = unit_columns(where_ref, 2 * half, unit, 1)
-                copies.append(
-                    pltpu.make_async_copy(ref.at[e], gradient_ref.at[:, columns], sem.at[len(copies)])
+    def kernel(where_ref, scale_ref, hidden_ref, cot_ref, *refs):
+        weight_refs, sum_refs, arrived_refs, refs = refs[:2], refs[2:4], refs[4 : 4 + len(units)], refs[5 + len(units) :]
+        gradient_ref, keys_ref, hid, cot, wgt, near, far, held, new, sem, held_sem, out_sem = refs
+        place = functools.partial(unit_columns, where_ref, 2 * half)
+        loads = [pltpu.make_async_copy(cot_ref, cot, sem.at[0])]
+        for i in range(2):
+            loads.append(pltpu.make_async_copy(weight_refs[i], wgt.at[i], sem.at[1 + i]))
+            columns = hidden_ref.at[:, place(unit, i)]
+            loads.append(pltpu.make_async_copy(columns, hid.at[i], sem.at[3 + i]))
+        loads.append(pltpu.make_async_copy(sum_refs[0], near, sem.at[5]))
+        loads.append(pltpu.make_async_copy(sum_refs[1], far, sem.at[6]))
+        for copy in loads:
+            copy.start()
+        fills, stores = [], []
+        for j, (ref, some) in enumerate(zip(arrived_refs, units)):
+            first = sum(counts[:j])
+            fills.append(pltpu.make_async_copy(ref, held.at[pl.ds(first, len(some))], held_sem.at[j]))
+            fills[-1].start()
+            for e, one in enumerate(some):
+                target = gradient_ref.at[:, place(one, 1)]
+                stores.append(pltpu.make_async_copy(held.at[first + e], target, out_sem.at[2 + first + e]))
+        for copy in loads[:5]:
+            copy.wait()
+        for i in range(2):
+            new[i] = (
+                lax.dot_general(
+                    cot[...], wgt[i], (((1,), (1,)), ((), ())), preferred_element_type=F32
                 )
-        for copy in copies:
-            copy.start()
-        keys_ref[...] = ((a_ref[...] + b_ref[...].astype(F32)) * scale_ref[0]).astype(BF16)
-        for copy in copies:
+                * scale_ref[0]
+            ).astype(BF16)
+            target = gradient_ref.at[:, place(unit, i)]
+            stores.append(pltpu.make_async_copy(new.at[i], target, out_sem.at[i]))
+            stores[-1].start()
+        for copy in fills:
+            copy.wait()
+        for copy in stores[:-2]:
+            copy.start()
+        total = jnp.dot(hid[0], wgt[0], preferred_element_type=F32)
+        total += jnp.dot(hid[1], wgt[1], preferred_element_type=F32)
+        for copy in loads[5:]:
+            copy.wait()
+        keys_ref[...] = ((total + near[...] + far[...].astype(F32)) * scale_ref[0]).astype(BF16)
+        for copy in stores:
             copy.wait()
 
     return pl.pallas_call(
         kernel,
         out_shape=[
             jax.ShapeDtypeStruct(gradient.shape, BF16),
-            jax.ShapeDtypeStruct(sums[0].shape, BF16),
+            jax.ShapeDtypeStruct((tokens, features), BF16),
         ],
-        in_specs=[SMEM, SMEM] + [VMEM] * (len(units) + 2) + [ANY],
+        in_specs=[SMEM, SMEM] + [ANY] * (7 + len(units)),
         out_specs=[ANY, VMEM],
-        input_output_aliases={len(units) + 4: 0},
-        scratch_shapes=[pltpu.SemaphoreType.DMA((sum(counts),))],
+        input_output_aliases={8 + len(units): 0},
+        scratch_shapes=[
+            pltpu.VMEM((2, tokens, half), BF16),
+            pltpu.VMEM((tokens, features), BF16),
+            pltpu.VMEM((2, half, features), BF16),
+            pltpu.VMEM((tokens, features), F32),
+            pltpu.VMEM((tokens, features), BF16),
+            pltpu.VMEM((sum(counts), tokens, half), BF16),
+            pltpu.VMEM((2, tokens, half), BF16),
+            pltpu.SemaphoreType.DMA((7,)),
+            pltpu.SemaphoreType.DMA((len(units),)),
+            pltpu.SemaphoreType.DMA((2 + sum(counts),)),
+        ],
+        cost_estimate=CHEAP,
         compiler_params=PARAMS,
         name="finish",
-    )(where, scale, *arrived, *sums, gradient)
+    )(where, scale, hidden, cotangent, *weights, *sums, *arrived, gradient)
 
 
 def join(where, mine, theirs):
@@ -344,22 +383,20 @@
     nz = lax.axis_size("z")
     token_count = tokens * lax.axis_size(("replica", "z", "x", "core"))
 
-    codes = quantize(key_weight, limit)
     half = rows // 2
-    own = lax.dynamic_slice_in_dim(codes, r * half, half, 0)
-    rest = lax.dynamic_slice_in_dim(codes, (1 - r) * half, half, 0)
+    own = quantize(lax.dynamic_slice_in_dim(key_weight, r * half, half, 0), limit)
+    rest = quantize(lax.dynamic_slice_in_dim(key_weight, (1 - r) * half, half, 0), limit)
     hidden, own, rest = lax.optimization_barrier((hidden, own, rest))
     mine = lax.all_gather(own, "z", axis=0)
-    rest, mine = lax.optimization_barrier((rest, mine))
-    theirs = lax.all_gather(rest, "z", axis=0)
+    rest0, mine = lax.optimization_barrier((rest, mine))
+    rest1, rest2 = swap(rest0, "z", 1), swap(rest0, "z", 2)
 
     cots = [swap(cotangent, "x"), swap(cotangent, "replica")]
     for_group, for_other = pack(where, hidden, rows, nz)
     for_group, *cots = lax.optimization_barrier((for_group, *cots))
+    swapped = lax.all_to_all(for_group, ("replica", "x", "core"), 0, 0, tiled=True)
     cut = tokens // 2
-    cots += [swap(cots[1][:cut], "x"), swap(cots[0][cut:], "replica")]
-    for_group, *cots = lax.optimization_barrier((for_group, *cots))
-    swapped = lax.all_to_all(for_group, ("replica", "x", "core"), 0, 0, tiled=True)
+    diagonal = [swap(cots[1][:cut], "x"), swap(cots[0][cut:], "replica")]
     peaks = jnp.max(jnp.abs(key_weight), axis=0, keepdims=True)
     peaks = jnp.broadcast_to(peaks, (16, peaks.shape[1]))
     for k in (1, 2):
@@ -367,6 +404,9 @@
     cots = jnp.concatenate([cotangent, *cots], axis=0)
     cots, peaks = lax.optimization_barrier((cots, peaks))
     cots = [cots, swap(cots, "core")]
+    rest1, rest2, *diagonal = lax.optimization_barrier((rest1, rest2, *diagonal))
+    diagonal = jnp.concatenate(diagonal, axis=0)
+    diagonal = [diagonal, swap(diagonal, "core")]
     slots = [
         ((r ^ dr) * 2 + (x ^ dx)) * 2 + (c ^ dc) for dc in (0, 1) for dr in (0, 1) for dx in (0, 1)
     ]
@@ -376,40 +416,39 @@
     parts = [jnp.concatenate([own, peaks])]
     parts += [lax.dynamic_index_in_dim(mine, z ^ k, keepdims=False) for k in (1, 2, 3)]
     cots[1], *parts = lax.optimization_barrier((cots[1], *parts))
-    side0 = swap(parts[0], "x")
+    side0, rest3 = swap(parts[0], "x"), swap(parts[3], "replica")
     swapped, other = lax.optimization_barrier((swapped, other))
-    term = weight_terms(slots, swapped, cots, (0, 1, 2, 3), [])
+    term = weight_terms(slots, swapped, cots + diagonal, (0, 1, 2, 3), [])
     stage = functools.partial(consume, where, scale, hidden, other, [cotangent, cots[1]])
 
     def codes_of(units):
         return [unit for _, _, unit in units]
 
-    term, side0, *parts = lax.optimization_barrier((term, side0, *parts))
-    total = lax.psum_scatter(term, "z", scatter_dimension=0, tiled=True).astype(F32)
+    term, side0, rest3, *parts = lax.optimization_barrier((term, side0, rest3, *parts))
+    total = lax.psum_scatter(term, "z", scatter_dimension=0, tiled=True)
     side1, other0 = swap(parts[1], "x"), swap(side0[:half], "replica")
-    units = [(codes, None, (0, 0, part)) for part in (0, 1)] + [(mine, None, (k, 0, 0)) for k in (1, 2, 3)]
+    units = [(own, 0, (0, 0, 0)), (rest0, 0, (0, 0, 1))] + [(mine, None, (k, 0, 0)) for k in (1, 2, 3)]
     *state, away0, away1 = stage(units, [], None)
     first = ([swap(away0, "core"), swap(away1, "core")], codes_of(units))
 
     side1, other0, *rest = lax.optimization_barrier((side1, other0, *state, *parts))
     state, parts = rest[:3], rest[3:]
     side2, other1 = swap(parts[2], "x"), swap(side1, "replica")
-    units = [(side0, 0, (0, 1, 0)), (other0, 0, (0, 1, 1)), (side1, 0, (1, 1, 0)), (theirs, None, (1, 0, 1))]
+    units = [(side0, 0, (0, 1, 0)), (other0, 0, (0, 1, 1)), (side1, 0, (1, 1, 0)), (rest1, 0, (1, 0, 1))]
     *state, away = stage(units, state, None)
     second = ([swap(away, "core")], codes_of(units))
 
     side2, other1, *rest = lax.optimization_barrier((side2, other1, *state, *parts))
     state, parts = rest[:3], rest[3:]
     side3, other2 = swap(parts[3], "x"), swap(side2, "replica")
-    units = [(theirs, None, (2, 0, 1)), (theirs, None, (3, 0, 1)), (other1, 0, (1, 1, 1)), (side2, 0, (2, 1, 0))]
+    units = [(rest2, 0, (2, 0, 1)), (rest3, 0, (3, 0, 1)), (other1, 0, (1, 1, 1)), (side2, 0, (2, 1, 0))]
     *state, away = stage(units, state, first)
     late, late_units = [swap(away, "core")], [codes_of(units)]
 
-    rest = lax.dynamic_index_in_dim(theirs, z ^ 3, keepdims=False)
-    side3, other2, rest, *state = lax.optimization_barrier((side3, other2, rest, *state))
-    other3 = swap(rest, "x")
+    side3, other2, rest3, *state = lax.optimization_barrier((side3, other2, rest3, *state))
+    other3 = swap(rest3, "x")
     units = [(other2, 0, (2, 1, 1)), (side3, 0, (3, 1, 0))]
-    *state, away = stage(units, state, second)
+    *state, away = stage(units, state, second, last=True)
     late.append(swap(away, "core"))
     late_units.append(codes_of(units))
 
@@ -418,14 +457,21 @@
     peak = jnp.maximum(peak, swap(peak, "core"))
     peak_ratio = (peak[0, 0] / limit).reshape(1)
 
-    share = (total * token_count ** (-0.5)).astype(BF16)
+    share = (total.astype(F32) * token_count ** (-0.5)).astype(BF16)
     other_share = swap(jnp.pad(share, ((0, 16), (0, 0))), "replica")
-    other3, peak_ratio, *state = lax.optimization_barrier((other3, peak_ratio, *state))
-    *state, away = stage([(other3, 0, (3, 1, 1))], state, None, last=True)
-    late.append(swap(away, "core"))
-    late_units.append([(3, 1, 1)])
-    sums = [state[0], swap(state[1], "core")]
-    input_gradient, projected_keys = finish(where, scale, state[2], late, late_units, sums)
+    other3, peak_ratio = lax.optimization_barrier((other3, peak_ratio))
+    input_gradient, projected_keys = finish(
+        where,
+        scale,
+        hidden,
+        cotangent,
+        (3, 1, 1),
+        [other3, swap(other3, "core")],
+        [state[0], swap(state[1], "core")],
+        state[2],
+        late,
+        late_units,
+    )
     weight_gradient = join(where, share, other_share)
     return (projected_keys, input_gradient, weight_gradient, peak_ratio)
 

time: 186 us -> 177 us (0.952)
  local copies, waits for them, and re-layouts: 18.7 us -> 8.17 us
  Pallas kernels: 55.8 us -> 52.7 us
  starting transfers between devices: 26.8 us -> 29.6 us
  other arithmetic: 7.46 us -> 9.73 us
    ppermute x25 -> x29, waiting for transfers between devices: 22.4 us -> 47.1 us  [swap(): return lax.ppermute(block, axis, [(i, i ^ mask) for i in range(size)])]
    all_to_all x1, waiting for transfers between devices: 16.9 us -> 0.01 us  [body(): lax.all_to_all(for_group, ('replica', 'x', 'core'), 0, 0, tiled=True)]
    unnamed x28 -> x29, local copies, waits for them, and re-layouts: 7.98 us -> 1.91 us
    pallas_call x5 -> x4, Pallas kernels: 34 us -> 29.7 us  [consume(): pl.pallas_call(kernel, out_shape=[sums, jax.ShapeDtypeStruct(sums.shape,...]
    reduce_scatter x1, waiting for transfers between devices: 4.33 us -> 0.02 us  [body(): total = lax.psum_scatter(term, 'z', scatter_dimension=0, tiled=True)]
    all_gather x1, waiting for transfers between devices: 15.3 us -> 11.2 us  [body(): mine = lax.all_gather(own, 'z', axis=0)]
    ppermute x25 -> x29, starting transfers between devices: 22.1 us -> 24.8 us  [swap(): return lax.ppermute(block, axis, [(i, i ^ mask) for i in range(size)])]
    concatenate x0 -> x1, other arithmetic: none -> 2.55 us  [body(): cots = jnp.concatenate([cotangent, *cots], axis=0)]
  transfers between devices with their start and end apart: 29 -> 32, of which waited for: 17 -> 18; matrix products, arithmetic and copies ran while one was open for 11% -> 8% of each run, Pallas kernels for 29% -> 29%
where the time goes in v4:
time: 177 us
  waiting for transfers between devices  58.4 us (33%)
  Pallas kernels  52.7 us (30%)
  starting transfers between devices  29.6 us (17%)
  between operations  18.1 us (10%)
  other arithmetic  9.73 us (5%)
  local copies, waits for them, and re-layouts  8.17 us (5%)
    ppermute x29, waiting for transfers between devices, swap(): return lax.ppermute(block, axis, [(i, i ^ mask) for i in range(size)])  47.1 us
    pallas_call x4, Pallas kernels, consume(): pl.pallas_call(kernel, out_shape=[sums, jax.ShapeDtypeStruct(sums.shape,...  29.7 us
    ppermute x29, starting transfers between devices, swap(): return lax.ppermute(block, axis, [(i, i ^ mask) for i in range(size)])  24.8 us
    all_gather x1, waiting for transfers between devices, body(): mine = lax.all_gather(own, 'z', axis=0)  11.2 us
    pallas_call x1, Pallas kernels, weight_terms(): pl.pallas_call(kernel, out_shape=jax.ShapeDtypeStruct((width, features),...  9.45 us
    pallas_call x1, Pallas kernels, pack(): pl.pallas_call(kernel, out_shape=[jax.ShapeDtypeStruct((group, tokens, nz...  6.65 us
    all_to_all x1, starting transfers between devices, body(): lax.all_to_all(for_group, ('replica', 'x', 'core'), 0, 0, tiled=True)  4.69 us
    pallas_call x1, Pallas kernels, finish(): pl.pallas_call(kernel, out_shape=[jax.ShapeDtypeStruct(gradient.shape, BF...  4.61 us
  transfers between devices with their start and end apart: 32, of which 18 were waited for; matrix products, arithmetic and copies ran while one was open for 8% of the time, Pallas kernels for 29%

profile of v4, /device:TPU:0, one launch (start us, length us, event | category | flops | bytes accessed | tf_op | source)
XLA Modules:
  0.0 176.7 jit_solution(16205484822483864594)
XLA Ops:
  8.0 2.5 %clamp_convert_fusion = (bf16[256,1024]{1,0:T(8,128)(2,1)}, bf16[256,1024]{1,0:T(8,128)(2,1)}) fusion(bf16[512,1024]{1,0:T(8,128)(2,1)} %param.5, s32[]{:T(128)S(6)} %select_n.17, f32[]{:T(128)S(6)} %div.11, s32[]{:T(128)S(6)} %select_n.16), kind=kLoop, calls=%fused_computation.3 | loop fusion | flops 2097152 | bytes 2097164 | tf_op jit(solution)/shard_map/convert_element_type | solution.py:20
  10.5 3.0 %collective-permute-start.1 = (bf16[256,1024]{1,0:T(8,128)(2,1)S(1)}, bf16[256,1024]{1,0:T(8,128)(2,1)}, u32[]{:S(2)}, u32[]{:S(2)}) collective-permute-start(bf16[256,1024]{1,0:T(8,128)(2,1)S(1)} %copy-done.1), channel_id=1, source_target_pairs={{0,16},{16,0},{1,17},{17,1},{2,18},{18,2},{3,19},{19,3},{4,20},{20... | collective-permute-start | bytes 1572872 | tf_op jit(solution)/shard_map/ppermute | solution.py:25
  13.5 1.5 collective-permute-start
  15.0 0.6 pad_add_fusion.core_ref.where_ref
  15.6 6.7 %pack.1 = (bf16[8,256,1024]{2,1,0:T(8,128)(2,1)}, bf16[8,256,512]{2,1,0:T(8,128)(2,1)}) custom-call(s32[4]{0:T(128)} %pad_add_fusion.core_ref.where_ref, bf16[256,8192]{1,0:T(8,128)(2,1)} %hidden_ref.5), custom_call_target="tpu_custom_call" | custom-call | tf_op jit(solution)/shard_map/pack/pallas_call | solution.py:61
  22.2 3.3 %collective-permute-done.1 = bf16[256,1024]{1,0:T(8,128)(2,1)} collective-permute-done((bf16[256,1024]{1,0:T(8,128)(2,1)S(1)}, bf16[256,1024]{1,0:T(8,128)(2,1)}, u32[]{:S(2)}, u32[]{:S(2)}) %collective-permute-start.1) | collective-permute-done | bytes 524320 | tf_op jit(solution)/shard_map/ppermute | solution.py:25
  25.5 1.5 collective-permute-done
  27.0 4.7 %all-to-all-start = ((bf16[8,256,1024]{2,1,0:T(8,128)(2,1)}), bf16[8,256,1024]{2,1,0:T(8,128)(2,1)}, u32[]{:S(2)}, u32[]{:S(2)}) async-start(bf16[8,256,1024]{2,1,0:T(8,128)(2,1)} %get-tuple-element.75), calls=%async_computation | async-start | bytes 8388608 | tf_op jit(solution)/shard_map/all_to_all | solution.py:397
  31.9 1.6 collective-permute-start.3
  33.5 5.1 %collective-permute-done.3 = bf16[16,1024]{1,0:T(8,128)(2,1)S(1)} collective-permute-done((bf16[16,1024]{1,0:T(8,128)(2,1)S(1)}, bf16[16,1024]{1,0:T(8,128)(2,1)S(1)}, u32[]{:S(2)}, u32[]{:S(2)}) %collective-permute-start.3) | collective-permute-done | bytes 32800 | tf_op jit(solution)/shard_map/ppermute | solution.py:25
  38.6 1.6 collective-permute-start.4
  40.2 6.0 %collective-permute-done.4 = bf16[16,1024]{1,0:T(8,128)(2,1)S(1)} collective-permute-done((bf16[16,1024]{1,0:T(8,128)(2,1)S(1)}, bf16[16,1024]{1,0:T(8,128)(2,1)S(1)}, u32[]{:S(2)}, u32[]{:S(2)}) %collective-permute-start.4) | collective-permute-done | bytes 32800 | tf_op jit(solution)/shard_map/ppermute | solution.py:25
  46.3 2.6 %pad_maximum_fusion.refs_0_ = bf16[768,1024]{1,0:T(8,128)(2,1)} fusion(bf16[256,1024]{1,0:T(8,128)(2,1)} %collective-permute-done.1, bf16[256,1024]{1,0:T(8,128)(2,1)} %collective-permute-done, bf16[256,1024]{1,0:T(8,128)(2,1)S(1)} %copy-done.1), kind=kLoop, calls=%fused_computation | loop fusion | flops 4718592 | bytes 3145728 | tf_op jit(solution)/shard_map/concatenate | solution.py:404
  48.9 0.5 collective-permute-start.2
  49.4 11.2 %all-gather.3.cloned.1.call-done = bf16[1024,1024]{1,0:T(8,128)(2,1)} async-done(((bf16[256,1024]{1,0:T(8,128)(2,1)}), bf16[1024,1024]{1,0:T(8,128)(2,1)}) %all-gather.3.cloned.1.call-update) | async-done | bytes 2097168 | tf_op jit(solution)/shard_map/all_gather | solution.py:390
  60.6 1.1 collective-permute-start.7
  61.7 0.5 collective-permute-start.6
  62.3 1.1 slice.16
  63.4 1.0 slice.15
  64.4 1.5 collective-permute-start.8
  65.9 1.6 collective-permute-start.9
  67.5 0.8 pad_maximum_fusion.1
  68.3 1.2 dynamic-slice_bitcast_fusion
  69.5 15.9 %collective-permute-done.8 = bf16[128,1024]{1,0:T(8,128)(2,1)S(1)} collective-permute-done((bf16[128,1024]{1,0:T(8,128)(2,1)S(1)}, bf16[128,1024]{1,0:T(8,128)(2,1)S(1)}, u32[]{:S(2)}, u32[]{:S(2)}) %collective-permute-start.8) | collective-permute-done | bytes 262176 | tf_op jit(solution)/shard_map/ppermute | solution.py:25
  85.4 0.3 collective-permute-start.11
  86.0 0.7 collective-permute-done.6.refs_5_
  86.7 0.8 copy-done.7
  87.5 1.4 collective-permute-start.12
  89.0 0.6 stack.55.slots_ref
  89.6 9.5 %weight_terms.1 = bf16[1024,1024]{1,0:T(8,128)(2,1)} custom-call(s32[8]{0:T(128)} %stack.55.slots_ref, bf16[8,256,1024]{2,1,0:T(8,128)(2,1)} %all-to-all-done.swapped_ref, bf16[768,1024]{1,0:T(8,128)(2,1)} %pad_maximum_fusion.refs_0_, bf16[768,1024]{1,0:T(8,128)(2,1)} %copy-done, bf16[256,1024]{1,0:T(8,128)(2,1)} %copy-done.7, ...), custom_call_target="tpu_custom_call" | custom-call | flops 1 | bytes 1 | tf_op jit(solution)/shard_map/weight_terms/pallas_call | solution.py:111
  99.1 3.1 %collective-permute-done.12.refs_3_ = bf16[256,1024]{1,0:T(8,128)(2,1)} collective-permute-done((bf16[256,1024]{1,0:T(8,128)(2,1)}, bf16[256,1024]{1,0:T(8,128)(2,1)}, u32[]{:S(2)}, u32[]{:S(2)}) %collective-permute-start.12) | collective-permute-done | bytes 524320 | tf_op jit(solution)/shard_map/ppermute | solution.py:25
  102.2 0.9 slice.17
  103.2 1.4 collective-permute-start.14
  104.6 1.5 collective-permute-start.13
  106.1 9.2 %consume.4 = (f32[256,1024]{1,0:T(8,128)}, f32[256,1024]{1,0:T(8,128)}, bf16[256,8192]{1,0:T(8,128)(2,1)}, bf16[4,256,256]{2,1,0:T(8,128)(2,1)}, bf16[1,256,256]{2,1,0:T(8,128)(2,1)}) custom-call(s32[4]{0:T(128)} %pad_add_fusion.core_ref.where_ref, f32[1]{0:T(128)} %bitcast.5.scale_ref, bf16[256,8192]{1,0:T(8,128)(2,1)} %hidden_ref.5, ...), custom_call_target="tpu_custom_call" | custom-call | flops 1 | bytes 1 | tf_op jit(solution)/shard_map/consume/pallas_call | solution.py:235
  115.2 1.8 %collective-permute-done.14.refs_3_ = bf16[256,1024]{1,0:T(8,128)(2,1)} collective-permute-done((bf16[256,1024]{1,0:T(8,128)(2,1)}, bf16[256,1024]{1,0:T(8,128)(2,1)}, u32[]{:S(2)}, u32[]{:S(2)}) %collective-permute-start.14) | collective-permute-done | bytes 524320 | tf_op jit(solution)/shard_map/ppermute | solution.py:25
  117.0 1.2 collective-permute-done.13.refs_4_
  118.2 1.5 collective-permute-start.15
  119.7 0.5 collective-permute-start.16
  120.2 7.6 %consume.5 = (f32[256,1024]{1,0:T(8,128)}, f32[256,1024]{1,0:T(8,128)}, bf16[256,8192]{1,0:T(8,128)(2,1)}, bf16[4,256,256]{2,1,0:T(8,128)(2,1)}) custom-call(s32[4]{0:T(128)} %pad_add_fusion.core_ref.where_ref, f32[1]{0:T(128)} %bitcast.5.scale_ref, bf16[256,8192]{1,0:T(8,128)(2,1)} %hidden_ref.5, ...), custom_call_target="tpu_custom_call", output_to_operand_aliasing={{0}: (10, {}), {2}: (12, {}), {1}: (11, {})} | custom-call | flops 1 | bytes 1 | tf_op jit(solution)/shard_map/consume/pallas_call | solution.py:235
  127.8 2.9 %collective-permute-done.15.refs_5_ = bf16[256,1024]{1,0:T(8,128)(2,1)S(1)} collective-permute-done((bf16[256,1024]{1,0:T(8,128)(2,1)}, bf16[256,1024]{1,0:T(8,128)(2,1)S(1)}, u32[]{:S(2)}, u32[]{:S(2)}) %collective-permute-start.15) | collective-permute-done | bytes 524320 | tf_op jit(solution)/shard_map/ppermute | solution.py:25
  130.8 1.3 collective-permute-done.16.refs_4_
  132.1 1.0 collective-permute-start.17
  133.0 0.6 collective-permute-start.18
  133.6 0.6 reduce_max.28
  134.2 0.5 collective-permute-start.24
  134.7 0.2 collective-permute-done.20.refs_10_
  135.0 0.6 copy-done.12
  135.6 7.6 %consume.6 = (f32[256,1024]{1,0:T(8,128)}, f32[256,1024]{1,0:T(8,128)}, bf16[256,8192]{1,0:T(8,128)(2,1)}, bf16[4,256,256]{2,1,0:T(8,128)(2,1)}) custom-call(s32[4]{0:T(128)} %pad_add_fusion.core_ref.where_ref, f32[1]{0:T(128)} %bitcast.5.scale_ref, bf16[256,8192]{1,0:T(8,128)(2,1)} %hidden_ref.5, ...), custom_call_target="tpu_custom_call", output_to_operand_aliasing={{0}: (10, {}), {2}: (12, {}), {1}: (11, {})} | custom-call | flops 1 | bytes 1 | tf_op jit(solution)/shard_map/consume/pallas_call | solution.py:235
  143.4 1.2 collective-permute-done.18.refs_2_
  144.6 0.7 collective-permute-start.21
  145.3 1.4 slice_reduce_fusion
  148.1 1.1 multiply_convert_fusion.mine_ref
  149.2 0.9 pad.4
  150.2 1.1 collective-permute-start.28
  151.2 0.5 slice.19
  152.4 0.2 collective-permute-start.26
  152.7 5.4 %consume.7 = (f32[256,1024]{1,0:T(8,128)}, bf16[256,1024]{1,0:T(8,128)(2,1)}, bf16[256,8192]{1,0:T(8,128)(2,1)}, bf16[2,256,256]{2,1,0:T(8,128)(2,1)}) custom-call(s32[4]{0:T(128)} %pad_add_fusion.core_ref.where_ref, f32[1]{0:T(128)} %bitcast.5.scale_ref, bf16[256,8192]{1,0:T(8,128)(2,1)} %hidden_ref.5, ...), custom_call_target="tpu_custom_call", output_to_operand_aliasing={{0}: (8, {}), {2}: (10, {})} | custom-call | flops 1 | bytes 1 | tf_op jit(solution)/shard_map/consume/pallas_call | solution.py:235
  158.0 0.4 collective-permute-start.25
  158.6 0.3 collective-permute-start.27
  159.0 2.0 %collective-permute-done.27.refs_5_ = bf16[2,256,256]{2,1,0:T(8,128)(2,1)S(1)} collective-permute-done((bf16[2,256,256]{2,1,0:T(8,128)(2,1)}, bf16[2,256,256]{2,1,0:T(8,128)(2,1)S(1)}, u32[]{:S(2)}, u32[]{:S(2)}) %collective-permute-start.27) | collective-permute-done | bytes 262176 | tf_op jit(solution)/shard_map/ppermute | solution.py:25
  161.0 0.5 collective-permute-done.23.refs_1_
  161.9 4.6 %finish.1 = (bf16[256,8192]{1,0:T(8,128)(2,1)}, bf16[256,1024]{1,0:T(8,128)(2,1)}) custom-call(s32[4]{0:T(128)} %pad_add_fusion.core_ref.where_ref, f32[1]{0:T(128)} %bitcast.5.scale_ref, bf16[256,8192]{1,0:T(8,128)(2,1)} %hidden_ref.5, bf16[256,1024]{1,0:T(8,128)(2,1)} %cot_ref.1, ...), custom_call_target="tpu_custom_call", output_to_operand_aliasing={{0}: (10, {})} | custom-call | flops 1 | bytes 1 | tf_op jit(solution)/shard_map/finish/pallas_call | solution.py:330
  166.5 2.3 %join.1 = bf16[512,1024]{1,0:T(8,128)(2,1)} custom-call(s32[4]{0:T(128)} %pad_add_fusion.core_ref.where_ref, bf16[256,1024]{1,0:T(8,128)(2,1)} %copy-done.4, bf16[272,1024]{1,0:T(8,128)(2,1)} %collective-permute-done.28.theirs_ref), custom_call_target="tpu_custom_call" | custom-call | tf_op jit(solution)/shard_map/join/pallas_call | solution.py:365
  (60 shorter events, 1.4 us)
Async XLA Ops:
  7.2 3.3 %copy-start.1 = (bf16[256,1024]{1,0:T(8,128)(2,1)S(1)}, bf16[256,1024]{1,0:T(8,128)(2,1)}, u32[]{:S(2)}) copy-start(bf16[256,1024]{1,0:T(8,128)(2,1)} %cot_ref.1) | copy-start | bytes 1572868
  7.2 53.4 %all-gather.3.cloned.1.call-start = ((), (), s32[]{:S(2)}) async-start(), calls=%async_computation.3 | async-start | bytes 2621440 | tf_op jit(solution)/shard_map/all_gather | solution.py:390
  10.5 15.1 %collective-permute-start.1 = (bf16[256,1024]{1,0:T(8,128)(2,1)S(1)}, bf16[256,1024]{1,0:T(8,128)(2,1)}, u32[]{:S(2)}, u32[]{:S(2)}) collective-permute-start(bf16[256,1024]{1,0:T(8,128)(2,1)S(1)} %copy-done.1), channel_id=1, source_target_pairs={{0,16},{16,0},{1,17},{17,1},{2,18},{18,2},{3,19},{19,3},{4,20},{20... | collective-permute-start | bytes 1572872 | tf_op jit(solution)/shard_map/ppermute | solution.py:25
  13.5 13.5 %collective-permute-start = (bf16[256,1024]{1,0:T(8,128)(2,1)S(1)}, bf16[256,1024]{1,0:T(8,128)(2,1)}, u32[]{:S(2)}, u32[]{:S(2)}) collective-permute-start(bf16[256,1024]{1,0:T(8,128)(2,1)S(1)} %copy-done.1), channel_id=1, source_target_pairs={{0,2},{2,0},{1,3},{3,1},{4,6},{6,4},{5,7},{7,5},{8,10},{10,8},{9,1... | collective-permute-start | bytes 1572872 | tf_op jit(solution)/shard_map/ppermute | solution.py:25
  27.0 4.8 %copy-start.5 = (bf16[512,1024]{1,0:T(8,128)(2,1)S(1)}, bf16[512,1024]{1,0:T(8,128)(2,1)}, u32[]{:S(2)}) copy-start(bf16[512,1024]{1,0:T(8,128)(2,1)} %param.5) | copy-start | bytes 3145732
  27.0 62.6 %all-to-all-start = ((bf16[8,256,1024]{2,1,0:T(8,128)(2,1)}), bf16[8,256,1024]{2,1,0:T(8,128)(2,1)}, u32[]{:S(2)}, u32[]{:S(2)}) async-start(bf16[8,256,1024]{2,1,0:T(8,128)(2,1)} %get-tuple-element.75), calls=%async_computation | async-start | bytes 8388608 | tf_op jit(solution)/shard_map/all_to_all | solution.py:397
  31.7 116.4 %reduce-scatter.2.cloned.1.call-start = ((), (), s32[]{:S(2)}) async-start(), calls=%async_computation.2 | async-start | bytes 2621440 | tf_op jit(solution)/shard_map/reduce_scatter | solution.py:428
  31.9 6.7 %collective-permute-start.3 = (bf16[16,1024]{1,0:T(8,128)(2,1)S(1)}, bf16[16,1024]{1,0:T(8,128)(2,1)S(1)}, u32[]{:S(2)}, u32[]{:S(2)}) collective-permute-start(bf16[16,1024]{1,0:T(8,128)(2,1)S(1)} %broadcast_in_dim.4), channel_id=1, source_target_pairs={{0,4},{4,0},{8,12},{12,8},{1,5},{5,1},{9,13},{13,9},{2,6},{6,2},{1... | collective-permute-start | bytes 98312 | tf_op jit(solution)/shard_map/ppermute | solution.py:25
  38.6 7.7 %collective-permute-start.4 = (bf16[16,1024]{1,0:T(8,128)(2,1)S(1)}, bf16[16,1024]{1,0:T(8,128)(2,1)S(1)}, u32[]{:S(2)}, u32[]{:S(2)}) collective-permute-start(bf16[16,1024]{1,0:T(8,128)(2,1)S(1)} %broadcast_maximum_fusion), channel_id=1, source_target_pairs={{0,8},{4,12},{8,0},{12,4},{1,9},{5,13},{9,1},{13,5},{2,10},{6,14},... | collective-permute-start | bytes 98312 | tf_op jit(solution)/shard_map/ppermute | solution.py:25
  46.3 21.2 %copy-start.2 = (bf16[256,1024]{1,0:T(8,128)(2,1)S(1)}, bf16[256,1024]{1,0:T(8,128)(2,1)}, u32[]{:S(2)}) copy-start(bf16[256,1024]{1,0:T(8,128)(2,1)} %get-tuple-element.81.refs_2_) | copy-start | bytes 1572868
  48.9 17.0 %collective-permute-start.5 = (bf16[768,1024]{1,0:T(8,128)(2,1)}, bf16[768,1024]{1,0:T(8,128)(2,1)S(1)}, u32[]{:S(2)}, u32[]{:S(2)}) collective-permute-start(bf16[768,1024]{1,0:T(8,128)(2,1)} %pad_maximum_fusion.refs_0_), channel_id=1, source_target_pairs={{0,1},{1,0},{2,3},{3,2},{4,5},{5,4},{6,7},{7,6},{8,9},{9,8},{10,11... | collective-permute-start | bytes 4718600 | tf_op jit(solution)/shard_map/ppermute | solution.py:25
  48.9 40.7 %collective-permute-start.2 = (bf16[8,256,512]{2,1,0:T(8,128)(2,1)}, bf16[8,256,512]{2,1,0:T(8,128)(2,1)}, u32[]{:S(2)}, u32[]{:S(2)}) collective-permute-start(bf16[8,256,512]{2,1,0:T(8,128)(2,1)} %get-tuple-element.76), channel_id=1, source_target_pairs={{0,1},{1,0},{2,3},{3,2},{4,5},{5,4},{6,7},{7,6},{8,9},{9,8},{10,11... | collective-permute-start | bytes 6291464 | tf_op jit(solution)/shard_map/ppermute | solution.py:25
  60.6 25.4 %collective-permute-start.7 = (bf16[256,1024]{1,0:T(8,128)(2,1)}, bf16[256,1024]{1,0:T(8,128)(2,1)}, u32[]{:S(2)}, u32[]{:S(2)}) collective-permute-start(bf16[256,1024]{1,0:T(8,128)(2,1)} %get-tuple-element.86.refs_3_), channel_id=1, source_target_pairs={{0,8},{4,12},{8,0},{12,4},{1,9},{5,13},{9,1},{13,5},{2,10},{6,14},... | collective-permute-start | bytes 1572872 | tf_op jit(solution)/shard_map/ppermute | solution.py:25
  61.7 24.9 %collective-permute-start.6 = (bf16[256,1024]{1,0:T(8,128)(2,1)}, bf16[256,1024]{1,0:T(8,128)(2,1)}, u32[]{:S(2)}, u32[]{:S(2)}) collective-permute-start(bf16[256,1024]{1,0:T(8,128)(2,1)} %get-tuple-element.86.refs_3_), channel_id=1, source_target_pairs={{0,4},{4,0},{8,12},{12,8},{1,5},{5,1},{9,13},{13,9},{2,6},{6,2},{1... | collective-permute-start | bytes 1572872 | tf_op jit(solution)/shard_map/ppermute | solution.py:25
  62.3 6.0 %copy-start.3 = (bf16[1024,1024]{1,0:T(8,128)(2,1)S(1)}, bf16[1024,1024]{1,0:T(8,128)(2,1)}, u32[]{:S(2)}) copy-start(bf16[1024,1024]{1,0:T(8,128)(2,1)} %all-gather.3.cloned.1.call-done) | copy-start | bytes 6291460
  64.4 21.1 %collective-permute-start.8 = (bf16[128,1024]{1,0:T(8,128)(2,1)S(1)}, bf16[128,1024]{1,0:T(8,128)(2,1)S(1)}, u32[]{:S(2)}, u32[]{:S(2)}) collective-permute-start(bf16[128,1024]{1,0:T(8,128)(2,1)S(1)} %slice.15), channel_id=1, source_target_pairs={{0,2},{2,0},{1,3},{3,1},{4,6},{6,4},{5,7},{7,5},{8,10},{10,8},{9,1... | collective-permute-start | bytes 786440 | tf_op jit(solution)/shard_map/ppermute | solution.py:25
  65.9 3.6 %copy-start = (bf16[768,1024]{1,0:T(8,128)(2,1)}, bf16[768,1024]{1,0:T(8,128)(2,1)S(1)}, u32[]{:S(2)}) copy-start(bf16[768,1024]{1,0:T(8,128)(2,1)S(1)} %collective-permute-done.5.refs_1_) | copy-start | bytes 4718596
  65.9 19.9 %collective-permute-start.9 = (bf16[128,1024]{1,0:T(8,128)(2,1)S(1)}, bf16[128,1024]{1,0:T(8,128)(2,1)S(1)}, u32[]{:S(2)}, u32[]{:S(2)}) collective-permute-start(bf16[128,1024]{1,0:T(8,128)(2,1)S(1)} %slice.16), channel_id=1, source_target_pairs={{0,16},{16,0},{1,17},{17,1},{2,18},{18,2},{3,19},{19,3},{4,20},{20... | collective-permute-start | bytes 786440 | tf_op jit(solution)/shard_map/ppermute | solution.py:25
  85.4 16.8 %collective-permute-start.11 = (bf16[272,1024]{1,0:T(8,128)(2,1)}, bf16[272,1024]{1,0:T(8,128)(2,1)S(1)}, u32[]{:S(2)}, u32[]{:S(2)}) collective-permute-start(bf16[272,1024]{1,0:T(8,128)(2,1)} %pad_maximum_fusion.1), channel_id=1, source_target_pairs={{0,2},{2,0},{1,3},{3,1},{4,6},{6,4},{5,7},{7,5},{8,10},{10,8},{9,1... | collective-permute-start | bytes 1671176 | tf_op jit(solution)/shard_map/ppermute | solution.py:25
  86.7 0.8 copy-start.7
  87.5 2.0 %collective-permute-start.10 = (bf16[256,1024]{1,0:T(8,128)(2,1)S(1)}, bf16[256,1024]{1,0:T(8,128)(2,1)}, u32[]{:S(2)}, u32[]{:S(2)}) collective-permute-start(bf16[256,1024]{1,0:T(8,128)(2,1)S(1)} %constant_dynamic-update-slice_fusion.refs_2_), channel_id=1, source_target_pairs={{0,1},{1,0},{2,3},{3,2},{4,5},{5,4},{6,7},{7,6},{8,9},{9,8},{10,11... | collective-permute-start | bytes 1572872 | tf_op jit(solution)/shard_map/ppermute | solution.py:25
  87.5 14.7 %collective-permute-start.12 = (bf16[256,1024]{1,0:T(8,128)(2,1)}, bf16[256,1024]{1,0:T(8,128)(2,1)}, u32[]{:S(2)}, u32[]{:S(2)}) collective-permute-start(bf16[256,1024]{1,0:T(8,128)(2,1)} %get-tuple-element.112), channel_id=1, source_target_pairs={{0,16},{16,0},{1,17},{17,1},{2,18},{18,2},{3,19},{19,3},{4,20},{20... | collective-permute-start | bytes 1572872 | tf_op jit(solution)/shard_map/ppermute | solution.py:25
  102.2 13.0 %copy-start.6 = (bf16[272,1024]{1,0:T(8,128)(2,1)}, bf16[272,1024]{1,0:T(8,128)(2,1)S(1)}, u32[]{:S(2)}) copy-start(bf16[272,1024]{1,0:T(8,128)(2,1)S(1)} %collective-permute-done.11.refs_2_) | copy-start | bytes 1671172
  103.2 13.9 %collective-permute-start.14 = (bf16[256,1024]{1,0:T(8,128)(2,1)}, bf16[256,1024]{1,0:T(8,128)(2,1)}, u32[]{:S(2)}, u32[]{:S(2)}) collective-permute-start(bf16[256,1024]{1,0:T(8,128)(2,1)} %slice.17), channel_id=1, source_target_pairs={{0,16},{16,0},{1,17},{17,1},{2,18},{18,2},{3,19},{19,3},{4,20},{20... | collective-permute-start | bytes 1572872 | tf_op jit(solution)/shard_map/ppermute | solution.py:25
  104.6 13.6 %collective-permute-start.13 = (bf16[256,1024]{1,0:T(8,128)(2,1)}, bf16[256,1024]{1,0:T(8,128)(2,1)}, u32[]{:S(2)}, u32[]{:S(2)}) collective-permute-start(bf16[256,1024]{1,0:T(8,128)(2,1)} %get-tuple-element.93), channel_id=1, source_target_pairs={{0,2},{2,0},{1,3},{3,1},{4,6},{6,4},{5,7},{7,5},{8,10},{10,8},{9,1... | collective-permute-start | bytes 1572872 | tf_op jit(solution)/shard_map/ppermute | solution.py:25
  118.2 12.6 %collective-permute-start.15 = (bf16[256,1024]{1,0:T(8,128)(2,1)}, bf16[256,1024]{1,0:T(8,128)(2,1)S(1)}, u32[]{:S(2)}, u32[]{:S(2)}) collective-permute-start(bf16[256,1024]{1,0:T(8,128)(2,1)} %get-tuple-element.101), channel_id=1, source_target_pairs={{0,2},{2,0},{1,3},{3,1},{4,6},{6,4},{5,7},{7,5},{8,10},{10,8},{9,1... | collective-permute-start | bytes 1572872 | tf_op jit(solution)/shard_map/ppermute | solution.py:25
  119.7 12.4 %collective-permute-start.16 = (bf16[256,1024]{1,0:T(8,128)(2,1)}, bf16[256,1024]{1,0:T(8,128)(2,1)}, u32[]{:S(2)}, u32[]{:S(2)}) collective-permute-start(bf16[256,1024]{1,0:T(8,128)(2,1)} %collective-permute-done.13.refs_4_), channel_id=1, source_target_pairs={{0,16},{16,0},{1,17},{17,1},{2,18},{18,2},{3,19},{19,3},{4,20},{20... | collective-permute-start | bytes 1572872 | tf_op jit(solution)/shard_map/ppermute | solution.py:25
  120.2 13.4 %copy-start.13 = (bf16[1,256,256]{2,1,0:T(8,128)(2,1)S(1)}, bf16[1,256,256]{2,1,0:T(8,128)(2,1)}, u32[]{:S(2)}) copy-start(bf16[1,256,256]{2,1,0:T(8,128)(2,1)} %get-tuple-element.121) | copy-start | bytes 393220
  120.2 14.8 %collective-permute-start.19 = (bf16[4,256,256]{2,1,0:T(8,128)(2,1)}, bf16[4,256,256]{2,1,0:T(8,128)(2,1)}, u32[]{:S(2)}, u32[]{:S(2)}) collective-permute-start(bf16[4,256,256]{2,1,0:T(8,128)(2,1)} %get-tuple-element.120), channel_id=1, source_target_pairs={{0,1},{1,0},{2,3},{3,2},{4,5},{5,4},{6,7},{7,6},{8,9},{9,8},{10,11... | collective-permute-start | bytes 1572872 | tf_op jit(solution)/shard_map/ppermute | solution.py:25
  130.8 1.3 copy-start.9
  132.1 11.4 %collective-permute-start.17 = (bf16[256,1024]{1,0:T(8,128)(2,1)}, bf16[256,1024]{1,0:T(8,128)(2,1)S(1)}, u32[]{:S(2)}, u32[]{:S(2)}) collective-permute-start(bf16[256,1024]{1,0:T(8,128)(2,1)} %get-tuple-element.112), channel_id=1, source_target_pairs={{0,2},{2,0},{1,3},{3,1},{4,6},{6,4},{5,7},{7,5},{8,10},{10,8},{9,1... | collective-permute-start | bytes 1572872 | tf_op jit(solution)/shard_map/ppermute | solution.py:25
  133.0 11.6 %collective-permute-start.18 = (bf16[256,1024]{1,0:T(8,128)(2,1)}, bf16[256,1024]{1,0:T(8,128)(2,1)}, u32[]{:S(2)}, u32[]{:S(2)}) collective-permute-start(bf16[256,1024]{1,0:T(8,128)(2,1)} %copy-done.9), channel_id=1, source_target_pairs={{0,16},{16,0},{1,17},{17,1},{2,18},{18,2},{3,19},{19,3},{4,20},{20... | collective-permute-start | bytes 1572872 | tf_op jit(solution)/shard_map/ppermute | solution.py:25
  133.6 1.3 collective-permute-start.20
  134.2 18.4 %collective-permute-start.24 = (bf16[4,256,256]{2,1,0:T(8,128)(2,1)}, bf16[4,256,256]{2,1,0:T(8,128)(2,1)}, u32[]{:S(2)}, u32[]{:S(2)}) collective-permute-start(bf16[4,256,256]{2,1,0:T(8,128)(2,1)} %get-tuple-element.132), channel_id=1, source_target_pairs={{0,1},{1,0},{2,3},{3,2},{4,5},{5,4},{6,7},{7,6},{8,9},{9,8},{10,11... | collective-permute-start | bytes 1572872 | tf_op jit(solution)/shard_map/ppermute | solution.py:25
  135.0 0.7 copy-start.12
  143.4 4.6 %copy-start.8 = (bf16[256,1024]{1,0:T(8,128)(2,1)}, bf16[256,1024]{1,0:T(8,128)(2,1)S(1)}, u32[]{:S(2)}) copy-start(bf16[256,1024]{1,0:T(8,128)(2,1)S(1)} %collective-permute-done.17.refs_3_) | copy-start | bytes 1572868
  144.6 13.8 %collective-permute-start.21 = (bf16[256,1024]{1,0:T(8,128)(2,1)}, bf16[256,1024]{1,0:T(8,128)(2,1)}, u32[]{:S(2)}, u32[]{:S(2)}) collective-permute-start(bf16[256,1024]{1,0:T(8,128)(2,1)} %collective-permute-done.12.refs_3_), channel_id=1, source_target_pairs={{0,2},{2,0},{1,3},{3,1},{4,6},{6,4},{5,7},{7,5},{8,10},{10,8},{9,1... | collective-permute-start | bytes 1572872 | tf_op jit(solution)/shard_map/ppermute | solution.py:25
  148.0 3.3 %collective-permute-start.22 = (f32[8,128]{1,0:T(8,128)S(1)}, f32[8,128]{1,0:T(8,128)S(1)}, u32[]{:S(2)}, u32[]{:S(2)}) collective-permute-start(f32[8,128]{1,0:T(8,128)S(1)} %broadcast_in_dim.10), channel_id=1, source_target_pairs={{0,1},{1,0},{2,3},{3,2},{4,5},{5,4},{6,7},{7,6},{8,9},{9,8},{10,11... | collective-permute-start | bytes 12296 | tf_op jit(solution)/shard_map/ppermute | solution.py:25
  149.2 8.8 %copy-start.4 = (bf16[256,1024]{1,0:T(8,128)(2,1)}, bf16[256,1024]{1,0:T(8,128)(2,1)S(1)}, u32[]{:S(2)}) copy-start(bf16[256,1024]{1,0:T(8,128)(2,1)S(1)} %multiply_convert_fusion.mine_ref) | copy-start | bytes 1572868
  150.2 16.3 %collective-permute-start.28 = (bf16[272,1024]{1,0:T(8,128)(2,1)}, bf16[272,1024]{1,0:T(8,128)(2,1)}, u32[]{:S(2)}, u32[]{:S(2)}) collective-permute-start(bf16[272,1024]{1,0:T(8,128)(2,1)} %pad.4), channel_id=1, source_target_pairs={{0,16},{16,0},{1,17},{17,1},{2,18},{18,2},{3,19},{19,3},{4,20},{20... | collective-permute-start | bytes 1671176 | tf_op jit(solution)/shard_map/ppermute | solution.py:25
  152.4 6.5 %collective-permute-start.26 = (bf16[4,256,256]{2,1,0:T(8,128)(2,1)}, bf16[4,256,256]{2,1,0:T(8,128)(2,1)}, u32[]{:S(2)}, u32[]{:S(2)}) collective-permute-start(bf16[4,256,256]{2,1,0:T(8,128)(2,1)} %get-tuple-element.135), channel_id=1, source_target_pairs={{0,1},{1,0},{2,3},{3,2},{4,5},{5,4},{6,7},{7,6},{8,9},{9,8},{10,11... | collective-permute-start | bytes 1572872 | tf_op jit(solution)/shard_map/ppermute | solution.py:25
  158.0 2.9 %collective-permute-start.25 = (bf16[256,1024]{1,0:T(8,128)(2,1)}, bf16[256,1024]{1,0:T(8,128)(2,1)S(1)}, u32[]{:S(2)}, u32[]{:S(2)}) collective-permute-start(bf16[256,1024]{1,0:T(8,128)(2,1)} %get-tuple-element.134), channel_id=1, source_target_pairs={{0,1},{1,0},{2,3},{3,2},{4,5},{5,4},{6,7},{7,6},{8,9},{9,8},{10,11... | collective-permute-start | bytes 1572872 | tf_op jit(solution)/shard_map/ppermute | solution.py:25
  158.4 3.1 %collective-permute-start.23 = (bf16[256,1024]{1,0:T(8,128)(2,1)}, bf16[256,1024]{1,0:T(8,128)(2,1)}, u32[]{:S(2)}, u32[]{:S(2)}) collective-permute-start(bf16[256,1024]{1,0:T(8,128)(2,1)} %collective-permute-done.21.refs_0_), channel_id=1, source_target_pairs={{0,1},{1,0},{2,3},{3,2},{4,5},{5,4},{6,7},{7,6},{8,9},{9,8},{10,11... | collective-permute-start | bytes 1572872 | tf_op jit(solution)/shard_map/ppermute | solution.py:25
  158.6 2.4 %collective-permute-start.27 = (bf16[2,256,256]{2,1,0:T(8,128)(2,1)}, bf16[2,256,256]{2,1,0:T(8,128)(2,1)S(1)}, u32[]{:S(2)}, u32[]{:S(2)}) collective-permute-start(bf16[2,256,256]{2,1,0:T(8,128)(2,1)} %get-tuple-element.136), channel_id=1, source_target_pairs={{0,1},{1,0},{2,3},{3,2},{4,5},{5,4},{6,7},{7,6},{8,9},{9,8},{10,11... | collective-permute-start | bytes 786440 | tf_op jit(solution)/shard_map/ppermute | solution.py:25
  161.0 0.7 copy-start.11
  161.0 0.9 copy-start.10
Sparse Core Ops, SparseCore 0:
  10.6 49.9 all-gather.2
  102.4 44.4 reduce-scatter.1

commit v5 on v4

--- a/solution.py
+++ b/solution.py
@@ -81,24 +81,31 @@
     def kernel(slots_ref, swapped_ref, *refs):
         cots_ref, refs = refs[:4], refs[4 + len(state) :]
         out_ref, lhs, rhs, out, sem, out_sem = refs
-        copies = []
+        shared = []
         for s in range(sources):
             place = pl.ds(pl.multiple_of(slots_ref[s] * tokens, tokens), tokens)
             source = cots_ref[s // 4].at[pl.ds(s % 4 * tokens, tokens)] if s % 4 < 3 else cots_ref[2 + s // 4]
-            copies.append(pltpu.make_async_copy(source, rhs.at[place], sem.at[count, s]))
+            shared.append(pltpu.make_async_copy(source, rhs.at[place], sem.at[count, s]))
+        loads = []
         for i, t in enumerate(tiles):
             at = pl.ds(t * tile, tile)
-            for s in range(sources):
-                place = pl.ds(s * tokens, tokens)
-                copies.append(
+            places = [pl.ds(s * tokens, tokens) for s in range(sources)]
+            loads.append(
+                [
                     pltpu.make_async_copy(swapped_ref.at[s, :, at], lhs.at[i, place], sem.at[i, s])
-                )
-        for copy in copies:
-            copy.start()
+                    for s, place in enumerate(places)
+                ]
+            )
+        for copy in shared + loads[0]:
+            copy.start()
+        for copy in shared:
+            copy.wait()
         stores = []
         for i, t in enumerate(tiles):
-            for copy in copies[(i + 1 if i else 0) * sources : (i + 2) * sources]:
+            for copy in loads[i]:
                 copy.wait()
+            for copy in loads[i + 1] if i + 1 < count else []:
+                copy.start()
             out[i] = lax.dot_general(
                 lhs[i], rhs[...], (((0,), (0,)), ((), ())), preferred_element_type=F32
             ).astype(BF16)
@@ -355,11 +362,11 @@
 
 
 def join(where, mine, theirs):
-    half, features = mine.shape
+    half, features = mine.shape[0] - 16, mine.shape[1]
 
     def kernel(where_ref, mine_ref, theirs_ref, out_ref):
         at = pl.multiple_of(where_ref[2] * half, half)
-        out_ref[pl.ds(at, half), :] = mine_ref[...]
+        out_ref[pl.ds(at, half), :] = mine_ref[pl.ds(0, half), :]
         out_ref[pl.ds(half - at, half), :] = theirs_ref[pl.ds(0, half), :]
 
     return pl.pallas_call(
@@ -416,7 +423,8 @@
     parts = [jnp.concatenate([own, peaks])]
     parts += [lax.dynamic_index_in_dim(mine, z ^ k, keepdims=False) for k in (1, 2, 3)]
     cots[1], *parts = lax.optimization_barrier((cots[1], *parts))
-    side0, rest3 = swap(parts[0], "x"), swap(parts[3], "replica")
+    side0 = swap(parts[0], "x")
+    rest3 = swap(jnp.concatenate([parts[3], peaks]), "replica")
     swapped, other = lax.optimization_barrier((swapped, other))
     term = weight_terms(slots, swapped, cots + diagonal, (0, 1, 2, 3), [])
     stage = functools.partial(consume, where, scale, hidden, other, [cotangent, cots[1]])
@@ -425,8 +433,9 @@
         return [unit for _, _, unit in units]
 
     term, side0, rest3, *parts = lax.optimization_barrier((term, side0, rest3, *parts))
+    rest3 = rest3[:half]
     total = lax.psum_scatter(term, "z", scatter_dimension=0, tiled=True)
-    side1, other0 = swap(parts[1], "x"), swap(side0[:half], "replica")
+    side1, other0 = swap(parts[1], "x"), swap(side0, "replica")
     units = [(own, 0, (0, 0, 0)), (rest0, 0, (0, 0, 1))] + [(mine, None, (k, 0, 0)) for k in (1, 2, 3)]
     *state, away0, away1 = stage(units, [], None)
     first = ([swap(away0, "core"), swap(away1, "core")], codes_of(units))
@@ -438,7 +447,12 @@
     *state, away = stage(units, state, None)
     second = ([swap(away, "core")], codes_of(units))
 
-    side2, other1, *rest = lax.optimization_barrier((side2, other1, *state, *parts))
+    peak = jnp.maximum(jnp.max(peaks), jnp.max(side0[half:]))
+    peak = jnp.full((8, 128), peak.astype(F32))
+    peak = jnp.maximum(peak, swap(peak, "core"))
+    peak_ratio = (peak[0, 0] / limit).reshape(1)
+
+    side2, other1, peak_ratio, *rest = lax.optimization_barrier((side2, other1, peak_ratio, *state, *parts))
     state, parts = rest[:3], rest[3:]
     side3, other2 = swap(parts[3], "x"), swap(side2, "replica")
     units = [(rest2, 0, (2, 0, 1)), (rest3, 0, (3, 0, 1)), (other1, 0, (1, 1, 1)), (side2, 0, (2, 1, 0))]
@@ -452,14 +466,8 @@
     late.append(swap(away, "core"))
     late_units.append(codes_of(units))
 
-    peak = jnp.maximum(jnp.max(peaks), jnp.max(side0[half:]))
-    peak = jnp.full((8, 128), peak.astype(F32))
-    peak = jnp.maximum(peak, swap(peak, "core"))
-    peak_ratio = (peak[0, 0] / limit).reshape(1)
-
-    share = (total.astype(F32) * token_count ** (-0.5)).astype(BF16)
-    other_share = swap(jnp.pad(share, ((0, 16), (0, 0))), "replica")
-    other3, peak_ratio = lax.optimization_barrier((other3, peak_ratio))
+    share = jnp.pad((total.astype(F32) * token_count ** (-0.5)).astype(BF16), ((0, 16), (0, 0)))
+    other_share = swap(share, "replica")
     input_gradient, projected_keys = finish(
         where,
         scale,

time: 177 us -> 177 us (level)
  transfers between devices with their start and end apart: 32 -> 32, of which waited for: 18 -> 16; matrix products, arithmetic and copies ran while one was open for 8% -> 8% of each run, Pallas kernels for 29% -> 29%
where the time goes in v5:
time: 177 us
  waiting for transfers between devices  57.5 us (32%)
  Pallas kernels  52.8 us (30%)
  starting transfers between devices  29.7 us (17%)
  between operations  18.1 us (10%)
  other arithmetic  10.6 us (6%)
  local copies, waits for them, and re-layouts  7.94 us (4%)
    ppermute x29, waiting for transfers between devices, swap(): return lax.ppermute(block, axis, [(i, i ^ mask) for i in range(size)])  46.2 us
    pallas_call x4, Pallas kernels, consume(): pl.pallas_call(kernel, out_shape=[sums, jax.ShapeDtypeStruct(sums.shape,...  29.5 us
    ppermute x29, starting transfers between devices, swap(): return lax.ppermute(block, axis, [(i, i ^ mask) for i in range(size)])  25 us
    all_gather x1, waiting for transfers between devices, body(): mine = lax.all_gather(own, 'z', axis=0)  11.3 us
    pallas_call x1, Pallas kernels, weight_terms(): pl.pallas_call(kernel, out_shape=jax.ShapeDtypeStruct((width, features),...  9.69 us
    pallas_call x1, Pallas kernels, pack(): pl.pallas_call(kernel, out_shape=[jax.ShapeDtypeStruct((group, tokens, nz...  6.69 us
    all_to_all x1, starting transfers between devices, body(): lax.all_to_all(for_group, ('replica', 'x', 'core'), 0, 0, tiled=True)  4.68 us
    pallas_call x1, Pallas kernels, finish(): pl.pallas_call(kernel, out_shape=[jax.ShapeDtypeStruct(gradient.shape, BF...  4.61 us
  transfers between devices with their start and end apart: 32, of which 16 were waited for; matrix products, arithmetic and copies ran while one was open for 8% of the time, Pallas kernels for 29%

profile of v5, /device:TPU:0, one launch (start us, length us, event | category | flops | bytes accessed | tf_op | source)
XLA Modules:
  0.0 176.7 jit_solution(11507811516181191969)
XLA Ops:
  8.0 2.5 %clamp_convert_fusion = (bf16[256,1024]{1,0:T(8,128)(2,1)}, bf16[256,1024]{1,0:T(8,128)(2,1)}) fusion(bf16[512,1024]{1,0:T(8,128)(2,1)} %param.5, s32[]{:T(128)S(6)} %select_n.17, f32[]{:T(128)S(6)} %div.11, s32[]{:T(128)S(6)} %select_n.16), kind=kLoop, calls=%fused_computation.3 | loop fusion | flops 2097152 | bytes 2097164 | tf_op jit(solution)/shard_map/convert_element_type | solution.py:20
  10.5 3.0 %collective-permute-start.1 = (bf16[256,1024]{1,0:T(8,128)(2,1)S(1)}, bf16[256,1024]{1,0:T(8,128)(2,1)}, u32[]{:S(2)}, u32[]{:S(2)}) collective-permute-start(bf16[256,1024]{1,0:T(8,128)(2,1)S(1)} %copy-done.1), channel_id=1, source_target_pairs={{0,16},{16,0},{1,17},{17,1},{2,18},{18,2},{3,19},{19,3},{4,20},{20... | collective-permute-start | bytes 1572872 | tf_op jit(solution)/shard_map/ppermute | solution.py:25
  13.5 1.5 collective-permute-start
  15.0 0.6 pad_add_fusion.core_ref.where_ref
  15.6 6.7 %pack.1 = (bf16[8,256,1024]{2,1,0:T(8,128)(2,1)}, bf16[8,256,512]{2,1,0:T(8,128)(2,1)}) custom-call(s32[4]{0:T(128)} %pad_add_fusion.core_ref.where_ref, bf16[256,8192]{1,0:T(8,128)(2,1)} %hidden_ref.5), custom_call_target="tpu_custom_call" | custom-call | tf_op jit(solution)/shard_map/pack/pallas_call | solution.py:61
  22.3 3.2 %collective-permute-done.1 = bf16[256,1024]{1,0:T(8,128)(2,1)} collective-permute-done((bf16[256,1024]{1,0:T(8,128)(2,1)S(1)}, bf16[256,1024]{1,0:T(8,128)(2,1)}, u32[]{:S(2)}, u32[]{:S(2)}) %collective-permute-start.1) | collective-permute-done | bytes 524320 | tf_op jit(solution)/shard_map/ppermute | solution.py:25
  25.5 1.5 collective-permute-done
  27.0 4.7 %all-to-all-start = ((bf16[8,256,1024]{2,1,0:T(8,128)(2,1)}), bf16[8,256,1024]{2,1,0:T(8,128)(2,1)}, u32[]{:S(2)}, u32[]{:S(2)}) async-start(bf16[8,256,1024]{2,1,0:T(8,128)(2,1)} %get-tuple-element.74), calls=%async_computation | async-start | bytes 8388608 | tf_op jit(solution)/shard_map/all_to_all | solution.py:404
  31.9 1.6 collective-permute-start.3
  33.5 5.1 %collective-permute-done.3 = bf16[16,1024]{1,0:T(8,128)(2,1)S(1)} collective-permute-done((bf16[16,1024]{1,0:T(8,128)(2,1)S(1)}, bf16[16,1024]{1,0:T(8,128)(2,1)S(1)}, u32[]{:S(2)}, u32[]{:S(2)}) %collective-permute-start.3) | collective-permute-done | bytes 32800 | tf_op jit(solution)/shard_map/ppermute | solution.py:25
  38.6 1.6 collective-permute-start.4
  40.2 6.1 %collective-permute-done.4 = bf16[16,1024]{1,0:T(8,128)(2,1)S(1)} collective-permute-done((bf16[16,1024]{1,0:T(8,128)(2,1)S(1)}, bf16[16,1024]{1,0:T(8,128)(2,1)S(1)}, u32[]{:S(2)}, u32[]{:S(2)}) %collective-permute-start.4) | collective-permute-done | bytes 32800 | tf_op jit(solution)/shard_map/ppermute | solution.py:25
  46.3 2.5 %pad_maximum_fusion.refs_0_ = bf16[768,1024]{1,0:T(8,128)(2,1)} fusion(bf16[256,1024]{1,0:T(8,128)(2,1)} %collective-permute-done.1, bf16[256,1024]{1,0:T(8,128)(2,1)} %collective-permute-done, bf16[256,1024]{1,0:T(8,128)(2,1)S(1)} %copy-done.1), kind=kLoop, calls=%fused_computation | loop fusion | flops 4718592 | bytes 3145728 | tf_op jit(solution)/shard_map/concatenate | solution.py:411
  48.8 0.5 collective-permute-start.2
  49.3 11.3 %all-gather.3.cloned.1.call-done = bf16[1024,1024]{1,0:T(8,128)(2,1)} async-done(((bf16[256,1024]{1,0:T(8,128)(2,1)}), bf16[1024,1024]{1,0:T(8,128)(2,1)}) %all-gather.3.cloned.1.call-update) | async-done | bytes 2097168 | tf_op jit(solution)/shard_map/all_gather | solution.py:397
  60.6 1.1 collective-permute-start.7
  61.7 0.5 collective-permute-start.6
  62.3 1.1 slice.16
  63.4 1.0 slice.15
  64.4 1.6 collective-permute-start.8
  65.9 0.9 pad_maximum_fusion.2
  66.8 1.5 collective-permute-start.9
  68.3 1.1 dynamic-slice_bitcast_fusion
  69.5 0.8 pad_maximum_fusion.1
  70.3 15.1 %collective-permute-done.8 = bf16[128,1024]{1,0:T(8,128)(2,1)S(1)} collective-permute-done((bf16[128,1024]{1,0:T(8,128)(2,1)S(1)}, bf16[128,1024]{1,0:T(8,128)(2,1)S(1)}, u32[]{:S(2)}, u32[]{:S(2)}) %collective-permute-start.8) | collective-permute-done | bytes 262176 | tf_op jit(solution)/shard_map/ppermute | solution.py:25
  85.4 1.5 collective-permute-start.12
  86.9 0.5 collective-permute-start.11
  87.5 0.8 copy-done.6
  88.3 0.6 stack.55.slots_ref
  88.9 1.5 collective-permute-done.10.refs_3_
  90.4 9.7 %weight_terms.1 = bf16[1024,1024]{1,0:T(8,128)(2,1)} custom-call(s32[8]{0:T(128)} %stack.55.slots_ref, bf16[8,256,1024]{2,1,0:T(8,128)(2,1)} %all-to-all-done.swapped_ref, bf16[768,1024]{1,0:T(8,128)(2,1)} %pad_maximum_fusion.refs_0_, bf16[768,1024]{1,0:T(8,128)(2,1)} %copy-done, bf16[256,1024]{1,0:T(8,128)(2,1)} %copy-done.6, ...), custom_call_target="tpu_custom_call" | custom-call | flops 1 | bytes 1 | tf_op jit(solution)/shard_map/weight_terms/pallas_call | solution.py:118
  100.1 1.1 collective-permute-done.11.refs_2_
  101.2 0.6 collective-permute-start.14
  101.9 0.6 collective-permute-start.13
  102.4 8.9 %consume.4 = (f32[256,1024]{1,0:T(8,128)}, f32[256,1024]{1,0:T(8,128)}, bf16[256,8192]{1,0:T(8,128)(2,1)}, bf16[4,256,256]{2,1,0:T(8,128)(2,1)}, bf16[1,256,256]{2,1,0:T(8,128)(2,1)}) custom-call(s32[4]{0:T(128)} %pad_add_fusion.core_ref.where_ref, f32[1]{0:T(128)} %bitcast.5.scale_ref, bf16[256,8192]{1,0:T(8,128)(2,1)} %hidden_ref.5, ...), custom_call_target="tpu_custom_call" | custom-call | flops 1 | bytes 1 | tf_op jit(solution)/shard_map/consume/pallas_call | solution.py:242
  111.4 3.4 %collective-permute-done.13.refs_4_ = bf16[256,1024]{1,0:T(8,128)(2,1)} collective-permute-done((bf16[256,1024]{1,0:T(8,128)(2,1)}, bf16[256,1024]{1,0:T(8,128)(2,1)}, u32[]{:S(2)}, u32[]{:S(2)}) %collective-permute-start.13) | collective-permute-done | bytes 524320 | tf_op jit(solution)/shard_map/ppermute | solution.py:25
  114.8 0.4 collective-permute-done.14.refs_3_
  115.2 1.5 collective-permute-start.15
  116.6 1.0 collective-permute-start.16
  117.7 0.6 reduce_max.28
  118.3 1.4 slice_reduce_fusion
  121.1 0.5 collective-permute-start.20
  121.6 0.7 collective-permute-done.17
  122.2 0.5 slice.18
  123.4 7.6 %consume.5 = (f32[256,1024]{1,0:T(8,128)}, f32[256,1024]{1,0:T(8,128)}, bf16[256,8192]{1,0:T(8,128)(2,1)}, bf16[4,256,256]{2,1,0:T(8,128)(2,1)}) custom-call(s32[4]{0:T(128)} %pad_add_fusion.core_ref.where_ref, f32[1]{0:T(128)} %bitcast.5.scale_ref, bf16[256,8192]{1,0:T(8,128)(2,1)} %hidden_ref.5, ...), custom_call_target="tpu_custom_call", output_to_operand_aliasing={{0}: (10, {}), {2}: (12, {}), {1}: (11, {})} | custom-call | flops 1 | bytes 1 | tf_op jit(solution)/shard_map/consume/pallas_call | solution.py:242
  131.1 0.6 collective-permute-start.18
  131.7 1.0 collective-permute-start.19
  132.6 1.9 %slice.19.refs_3_ = bf16[256,1024]{1,0:T(8,128)(2,1)} slice(bf16[272,1024]{1,0:T(8,128)(2,1)} %collective-permute-done.12), slice={[0:256], [0:1024]} | slice | bytes 1048576 | tf_op jit(solution)/shard_map/slice | solution.py:436
  134.5 0.5 collective-permute-start.24
  135.0 0.6 copy-done.8
  135.7 7.6 %consume.6 = (f32[256,1024]{1,0:T(8,128)}, f32[256,1024]{1,0:T(8,128)}, bf16[256,8192]{1,0:T(8,128)(2,1)}, bf16[4,256,256]{2,1,0:T(8,128)(2,1)}) custom-call(s32[4]{0:T(128)} %pad_add_fusion.core_ref.where_ref, f32[1]{0:T(128)} %bitcast.5.scale_ref, bf16[256,8192]{1,0:T(8,128)(2,1)} %hidden_ref.5, ...), custom_call_target="tpu_custom_call", output_to_operand_aliasing={{0}: (10, {}), {2}: (12, {}), {1}: (11, {})} | custom-call | flops 1 | bytes 1 | tf_op jit(solution)/shard_map/consume/pallas_call | solution.py:242
  143.3 1.9 %collective-permute-done.18.refs_3_ = bf16[256,1024]{1,0:T(8,128)(2,1)} collective-permute-done((bf16[256,1024]{1,0:T(8,128)(2,1)S(1)}, bf16[256,1024]{1,0:T(8,128)(2,1)}, u32[]{:S(2)}, u32[]{:S(2)}) %collective-permute-start.18) | collective-permute-done | bytes 524320 | tf_op jit(solution)/shard_map/ppermute | solution.py:25
  145.2 0.5 collective-permute-done.19.refs_2_
  145.7 1.4 collective-permute-start.22
  147.2 1.1 multiply_convert_fusion
  148.4 1.1 collective-permute-start.28
  149.4 5.4 %consume.7 = (f32[256,1024]{1,0:T(8,128)}, bf16[256,1024]{1,0:T(8,128)(2,1)}, bf16[256,8192]{1,0:T(8,128)(2,1)}, bf16[2,256,256]{2,1,0:T(8,128)(2,1)}) custom-call(s32[4]{0:T(128)} %pad_add_fusion.core_ref.where_ref, f32[1]{0:T(128)} %bitcast.5.scale_ref, bf16[256,8192]{1,0:T(8,128)(2,1)} %hidden_ref.5, ...), custom_call_target="tpu_custom_call", output_to_operand_aliasing={{0}: (8, {}), {2}: (10, {})} | custom-call | flops 1 | bytes 1 | tf_op jit(solution)/shard_map/consume/pallas_call | solution.py:242
  154.8 0.6 collective-permute-start.25
  155.4 3.5 %collective-permute-done.22.refs_0_ = bf16[256,1024]{1,0:T(8,128)(2,1)} collective-permute-done((bf16[256,1024]{1,0:T(8,128)(2,1)}, bf16[256,1024]{1,0:T(8,128)(2,1)}, u32[]{:S(2)}, u32[]{:S(2)}) %collective-permute-start.22) | collective-permute-done | bytes 524320 | tf_op jit(solution)/shard_map/ppermute | solution.py:25
  158.9 0.5 collective-permute-start.27
  159.4 1.6 collective-permute-done.27.refs_5_
  161.1 0.5 collective-permute-done.23.refs_1_
  161.8 4.6 %finish.1 = (bf16[256,8192]{1,0:T(8,128)(2,1)}, bf16[256,1024]{1,0:T(8,128)(2,1)}) custom-call(s32[4]{0:T(128)} %pad_add_fusion.core_ref.where_ref, f32[1]{0:T(128)} %bitcast.5.scale_ref, bf16[256,8192]{1,0:T(8,128)(2,1)} %hidden_ref.5, bf16[256,1024]{1,0:T(8,128)(2,1)} %cot_ref.1, ...), custom_call_target="tpu_custom_call", output_to_operand_aliasing={{0}: (10, {})} | custom-call | flops 1 | bytes 1 | tf_op jit(solution)/shard_map/finish/pallas_call | solution.py:337
  166.4 2.3 %join.1 = bf16[512,1024]{1,0:T(8,128)(2,1)} custom-call(s32[4]{0:T(128)} %pad_add_fusion.core_ref.where_ref, bf16[272,1024]{1,0:T(8,128)(2,1)} %copy-done.5, bf16[272,1024]{1,0:T(8,128)(2,1)} %collective-permute-done.28.theirs_ref), custom_call_target="tpu_custom_call" | custom-call | tf_op jit(solution)/shard_map/join/pallas_call | solution.py:372
  (53 shorter events, 0.7 us)
Async XLA Ops:
  7.2 3.3 %copy-start.1 = (bf16[256,1024]{1,0:T(8,128)(2,1)S(1)}, bf16[256,1024]{1,0:T(8,128)(2,1)}, u32[]{:S(2)}) copy-start(bf16[256,1024]{1,0:T(8,128)(2,1)} %cot_ref.1) | copy-start | bytes 1572868
  7.2 53.4 %all-gather.3.cloned.1.call-start = ((), (), s32[]{:S(2)}) async-start(), calls=%async_computation.3 | async-start | bytes 2621440 | tf_op jit(solution)/shard_map/all_gather | solution.py:397
  10.5 15.1 %collective-permute-start.1 = (bf16[256,1024]{1,0:T(8,128)(2,1)S(1)}, bf16[256,1024]{1,0:T(8,128)(2,1)}, u32[]{:S(2)}, u32[]{:S(2)}) collective-permute-start(bf16[256,1024]{1,0:T(8,128)(2,1)S(1)} %copy-done.1), channel_id=1, source_target_pairs={{0,16},{16,0},{1,17},{17,1},{2,18},{18,2},{3,19},{19,3},{4,20},{20... | collective-permute-start | bytes 1572872 | tf_op jit(solution)/shard_map/ppermute | solution.py:25
  13.5 13.5 %collective-permute-start = (bf16[256,1024]{1,0:T(8,128)(2,1)S(1)}, bf16[256,1024]{1,0:T(8,128)(2,1)}, u32[]{:S(2)}, u32[]{:S(2)}) collective-permute-start(bf16[256,1024]{1,0:T(8,128)(2,1)S(1)} %copy-done.1), channel_id=1, source_target_pairs={{0,2},{2,0},{1,3},{3,1},{4,6},{6,4},{5,7},{7,5},{8,10},{10,8},{9,1... | collective-permute-start | bytes 1572872 | tf_op jit(solution)/shard_map/ppermute | solution.py:25
  27.0 4.7 %copy-start.4 = (bf16[512,1024]{1,0:T(8,128)(2,1)S(1)}, bf16[512,1024]{1,0:T(8,128)(2,1)}, u32[]{:S(2)}) copy-start(bf16[512,1024]{1,0:T(8,128)(2,1)} %param.5) | copy-start | bytes 3145732
  27.0 61.9 %all-to-all-start = ((bf16[8,256,1024]{2,1,0:T(8,128)(2,1)}), bf16[8,256,1024]{2,1,0:T(8,128)(2,1)}, u32[]{:S(2)}, u32[]{:S(2)}) async-start(bf16[8,256,1024]{2,1,0:T(8,128)(2,1)} %get-tuple-element.74), calls=%async_computation | async-start | bytes 8388608 | tf_op jit(solution)/shard_map/all_to_all | solution.py:404
  31.7 115.5 %reduce-scatter.2.cloned.1.call-start = ((), (), s32[]{:S(2)}) async-start(), calls=%async_computation.2 | async-start | bytes 2621440 | tf_op jit(solution)/shard_map/reduce_scatter | solution.py:437
  31.9 6.8 %collective-permute-start.3 = (bf16[16,1024]{1,0:T(8,128)(2,1)S(1)}, bf16[16,1024]{1,0:T(8,128)(2,1)S(1)}, u32[]{:S(2)}, u32[]{:S(2)}) collective-permute-start(bf16[16,1024]{1,0:T(8,128)(2,1)S(1)} %broadcast_in_dim.4), channel_id=1, source_target_pairs={{0,4},{4,0},{8,12},{12,8},{1,5},{5,1},{9,13},{13,9},{2,6},{6,2},{1... | collective-permute-start | bytes 98312 | tf_op jit(solution)/shard_map/ppermute | solution.py:25
  38.6 7.6 %collective-permute-start.4 = (bf16[16,1024]{1,0:T(8,128)(2,1)S(1)}, bf16[16,1024]{1,0:T(8,128)(2,1)S(1)}, u32[]{:S(2)}, u32[]{:S(2)}) collective-permute-start(bf16[16,1024]{1,0:T(8,128)(2,1)S(1)} %broadcast_maximum_fusion), channel_id=1, source_target_pairs={{0,8},{4,12},{8,0},{12,4},{1,9},{5,13},{9,1},{13,5},{2,10},{6,14},... | collective-permute-start | bytes 98312 | tf_op jit(solution)/shard_map/ppermute | solution.py:25
  46.3 19.6 %copy-start.2 = (bf16[256,1024]{1,0:T(8,128)(2,1)S(1)}, bf16[256,1024]{1,0:T(8,128)(2,1)}, u32[]{:S(2)}) copy-start(bf16[256,1024]{1,0:T(8,128)(2,1)} %get-tuple-element.80.refs_2_) | copy-start | bytes 1572868
  48.8 18.0 %collective-permute-start.5 = (bf16[768,1024]{1,0:T(8,128)(2,1)}, bf16[768,1024]{1,0:T(8,128)(2,1)S(1)}, u32[]{:S(2)}, u32[]{:S(2)}) collective-permute-start(bf16[768,1024]{1,0:T(8,128)(2,1)} %pad_maximum_fusion.refs_0_), channel_id=1, source_target_pairs={{0,1},{1,0},{2,3},{3,2},{4,5},{5,4},{6,7},{7,6},{8,9},{9,8},{10,11... | collective-permute-start | bytes 4718600 | tf_op jit(solution)/shard_map/ppermute | solution.py:25
  48.8 40.1 %collective-permute-start.2 = (bf16[8,256,512]{2,1,0:T(8,128)(2,1)}, bf16[8,256,512]{2,1,0:T(8,128)(2,1)}, u32[]{:S(2)}, u32[]{:S(2)}) collective-permute-start(bf16[8,256,512]{2,1,0:T(8,128)(2,1)} %get-tuple-element.75), channel_id=1, source_target_pairs={{0,1},{1,0},{2,3},{3,2},{4,5},{5,4},{6,7},{7,6},{8,9},{9,8},{10,11... | collective-permute-start | bytes 6291464 | tf_op jit(solution)/shard_map/ppermute | solution.py:25
  60.6 26.9 %collective-permute-start.7 = (bf16[256,1024]{1,0:T(8,128)(2,1)}, bf16[256,1024]{1,0:T(8,128)(2,1)}, u32[]{:S(2)}, u32[]{:S(2)}) collective-permute-start(bf16[256,1024]{1,0:T(8,128)(2,1)} %get-tuple-element.85.refs_3_), channel_id=1, source_target_pairs={{0,8},{4,12},{8,0},{12,4},{1,9},{5,13},{9,1},{13,5},{2,10},{6,14},... | collective-permute-start | bytes 1572872 | tf_op jit(solution)/shard_map/ppermute | solution.py:25
  61.7 25.7 %collective-permute-start.6 = (bf16[256,1024]{1,0:T(8,128)(2,1)}, bf16[256,1024]{1,0:T(8,128)(2,1)}, u32[]{:S(2)}, u32[]{:S(2)}) collective-permute-start(bf16[256,1024]{1,0:T(8,128)(2,1)} %get-tuple-element.85.refs_3_), channel_id=1, source_target_pairs={{0,4},{4,0},{8,12},{12,8},{1,5},{5,1},{9,13},{13,9},{2,6},{6,2},{1... | collective-permute-start | bytes 1572872 | tf_op jit(solution)/shard_map/ppermute | solution.py:25
  62.3 6.1 %copy-start.3 = (bf16[1024,1024]{1,0:T(8,128)(2,1)S(1)}, bf16[1024,1024]{1,0:T(8,128)(2,1)}, u32[]{:S(2)}) copy-start(bf16[1024,1024]{1,0:T(8,128)(2,1)} %all-gather.3.cloned.1.call-done) | copy-start | bytes 6291460
  64.4 21.1 %collective-permute-start.8 = (bf16[128,1024]{1,0:T(8,128)(2,1)S(1)}, bf16[128,1024]{1,0:T(8,128)(2,1)S(1)}, u32[]{:S(2)}, u32[]{:S(2)}) collective-permute-start(bf16[128,1024]{1,0:T(8,128)(2,1)S(1)} %slice.15), channel_id=1, source_target_pairs={{0,2},{2,0},{1,3},{3,1},{4,6},{6,4},{5,7},{7,5},{8,10},{10,8},{9,1... | collective-permute-start | bytes 786440 | tf_op jit(solution)/shard_map/ppermute | solution.py:25
  66.8 3.5 %copy-start = (bf16[768,1024]{1,0:T(8,128)(2,1)}, bf16[768,1024]{1,0:T(8,128)(2,1)S(1)}, u32[]{:S(2)}) copy-start(bf16[768,1024]{1,0:T(8,128)(2,1)S(1)} %collective-permute-done.5.refs_1_) | copy-start | bytes 4718596
  66.8 20.1 %collective-permute-start.9 = (bf16[128,1024]{1,0:T(8,128)(2,1)S(1)}, bf16[128,1024]{1,0:T(8,128)(2,1)S(1)}, u32[]{:S(2)}, u32[]{:S(2)}) collective-permute-start(bf16[128,1024]{1,0:T(8,128)(2,1)S(1)} %slice.16), channel_id=1, source_target_pairs={{0,16},{16,0},{1,17},{17,1},{2,18},{18,2},{3,19},{19,3},{4,20},{20... | collective-permute-start | bytes 786440 | tf_op jit(solution)/shard_map/ppermute | solution.py:25
  85.4 14.6 %collective-permute-start.12 = (bf16[272,1024]{1,0:T(8,128)(2,1)}, bf16[272,1024]{1,0:T(8,128)(2,1)}, u32[]{:S(2)}, u32[]{:S(2)}) collective-permute-start(bf16[272,1024]{1,0:T(8,128)(2,1)} %pad_maximum_fusion.1), channel_id=1, source_target_pairs={{0,16},{16,0},{1,17},{17,1},{2,18},{18,2},{3,19},{19,3},{4,20},{20... | collective-permute-start | bytes 1671176 | tf_op jit(solution)/shard_map/ppermute | solution.py:25
  86.9 14.3 %collective-permute-start.11 = (bf16[272,1024]{1,0:T(8,128)(2,1)}, bf16[272,1024]{1,0:T(8,128)(2,1)}, u32[]{:S(2)}, u32[]{:S(2)}) collective-permute-start(bf16[272,1024]{1,0:T(8,128)(2,1)} %pad_maximum_fusion.2), channel_id=1, source_target_pairs={{0,2},{2,0},{1,3},{3,1},{4,6},{6,4},{5,7},{7,5},{8,10},{10,8},{9,1... | collective-permute-start | bytes 1671176 | tf_op jit(solution)/shard_map/ppermute | solution.py:25
  87.5 0.8 copy-start.6
  88.3 2.0 %collective-permute-start.10 = (bf16[256,1024]{1,0:T(8,128)(2,1)S(1)}, bf16[256,1024]{1,0:T(8,128)(2,1)}, u32[]{:S(2)}, u32[]{:S(2)}) collective-permute-start(bf16[256,1024]{1,0:T(8,128)(2,1)S(1)} %constant_dynamic-update-slice_fusion.refs_2_), channel_id=1, source_target_pairs={{0,1},{1,0},{2,3},{3,2},{4,5},{5,4},{6,7},{7,6},{8,9},{9,8},{10,11... | collective-permute-start | bytes 1572872 | tf_op jit(solution)/shard_map/ppermute | solution.py:25
  101.2 13.9 %collective-permute-start.14 = (bf16[272,1024]{1,0:T(8,128)(2,1)}, bf16[272,1024]{1,0:T(8,128)(2,1)}, u32[]{:S(2)}, u32[]{:S(2)}) collective-permute-start(bf16[272,1024]{1,0:T(8,128)(2,1)} %collective-permute-done.11.refs_2_), channel_id=1, source_target_pairs={{0,16},{16,0},{1,17},{17,1},{2,18},{18,2},{3,19},{19,3},{4,20},{20... | collective-permute-start | bytes 1671176 | tf_op jit(solution)/shard_map/ppermute | solution.py:25
  101.9 13.0 %collective-permute-start.13 = (bf16[256,1024]{1,0:T(8,128)(2,1)}, bf16[256,1024]{1,0:T(8,128)(2,1)}, u32[]{:S(2)}, u32[]{:S(2)}) collective-permute-start(bf16[256,1024]{1,0:T(8,128)(2,1)} %get-tuple-element.92), channel_id=1, source_target_pairs={{0,2},{2,0},{1,3},{3,1},{4,6},{6,4},{5,7},{7,5},{8,10},{10,8},{9,1... | collective-permute-start | bytes 1572872 | tf_op jit(solution)/shard_map/ppermute | solution.py:25
  115.2 15.9 %collective-permute-start.15 = (bf16[256,1024]{1,0:T(8,128)(2,1)}, bf16[256,1024]{1,0:T(8,128)(2,1)}, u32[]{:S(2)}, u32[]{:S(2)}) collective-permute-start(bf16[256,1024]{1,0:T(8,128)(2,1)} %get-tuple-element.100), channel_id=1, source_target_pairs={{0,2},{2,0},{1,3},{3,1},{4,6},{6,4},{5,7},{7,5},{8,10},{10,8},{9,1... | collective-permute-start | bytes 1572872 | tf_op jit(solution)/shard_map/ppermute | solution.py:25
  116.6 14.4 %collective-permute-start.16 = (bf16[256,1024]{1,0:T(8,128)(2,1)}, bf16[256,1024]{1,0:T(8,128)(2,1)}, u32[]{:S(2)}, u32[]{:S(2)}) collective-permute-start(bf16[256,1024]{1,0:T(8,128)(2,1)} %collective-permute-done.13.refs_4_), channel_id=1, source_target_pairs={{0,16},{16,0},{1,17},{17,1},{2,18},{18,2},{3,19},{19,3},{4,20},{20... | collective-permute-start | bytes 1572872 | tf_op jit(solution)/shard_map/ppermute | solution.py:25
  121.0 1.2 collective-permute-start.17
  121.1 13.9 %collective-permute-start.20 = (bf16[4,256,256]{2,1,0:T(8,128)(2,1)}, bf16[4,256,256]{2,1,0:T(8,128)(2,1)}, u32[]{:S(2)}, u32[]{:S(2)}) collective-permute-start(bf16[4,256,256]{2,1,0:T(8,128)(2,1)} %get-tuple-element.119), channel_id=1, source_target_pairs={{0,1},{1,0},{2,3},{3,2},{4,5},{5,4},{6,7},{7,6},{8,9},{9,8},{10,11... | collective-permute-start | bytes 1572872 | tf_op jit(solution)/shard_map/ppermute | solution.py:25
  123.4 9.2 %copy-start.9 = (bf16[1,256,256]{2,1,0:T(8,128)(2,1)S(1)}, bf16[1,256,256]{2,1,0:T(8,128)(2,1)}, u32[]{:S(2)}) copy-start(bf16[1,256,256]{2,1,0:T(8,128)(2,1)} %get-tuple-element.120) | copy-start | bytes 393220
  131.1 14.1 %collective-permute-start.18 = (bf16[256,1024]{1,0:T(8,128)(2,1)S(1)}, bf16[256,1024]{1,0:T(8,128)(2,1)}, u32[]{:S(2)}, u32[]{:S(2)}) collective-permute-start(bf16[256,1024]{1,0:T(8,128)(2,1)S(1)} %get-tuple-element.111), channel_id=1, source_target_pairs={{0,2},{2,0},{1,3},{3,1},{4,6},{6,4},{5,7},{7,5},{8,10},{10,8},{9,1... | collective-permute-start | bytes 1572872 | tf_op jit(solution)/shard_map/ppermute | solution.py:25
  131.7 14.1 %collective-permute-start.19 = (bf16[256,1024]{1,0:T(8,128)(2,1)}, bf16[256,1024]{1,0:T(8,128)(2,1)}, u32[]{:S(2)}, u32[]{:S(2)}) collective-permute-start(bf16[256,1024]{1,0:T(8,128)(2,1)} %collective-permute-done.15.refs_5_), channel_id=1, source_target_pairs={{0,16},{16,0},{1,17},{17,1},{2,18},{18,2},{3,19},{19,3},{4,20},{20... | collective-permute-start | bytes 1572872 | tf_op jit(solution)/shard_map/ppermute | solution.py:25
  132.6 2.4 %collective-permute-start.21 = (bf16[1,256,256]{2,1,0:T(8,128)(2,1)S(1)}, bf16[1,256,256]{2,1,0:T(8,128)(2,1)S(1)}, u32[]{:S(2)}, u32[]{:S(2)}) collective-permute-start(bf16[1,256,256]{2,1,0:T(8,128)(2,1)S(1)} %copy-done.9), channel_id=1, source_target_pairs={{0,1},{1,0},{2,3},{3,2},{4,5},{5,4},{6,7},{7,6},{8,9},{9,8},{10,11... | collective-permute-start | bytes 393224 | tf_op jit(solution)/shard_map/ppermute | solution.py:25
  134.5 14.9 %collective-permute-start.24 = (bf16[4,256,256]{2,1,0:T(8,128)(2,1)}, bf16[4,256,256]{2,1,0:T(8,128)(2,1)}, u32[]{:S(2)}, u32[]{:S(2)}) collective-permute-start(bf16[4,256,256]{2,1,0:T(8,128)(2,1)} %get-tuple-element.130), channel_id=1, source_target_pairs={{0,1},{1,0},{2,3},{3,2},{4,5},{5,4},{6,7},{7,6},{8,9},{9,8},{10,11... | collective-permute-start | bytes 1572872 | tf_op jit(solution)/shard_map/ppermute | solution.py:25
  135.0 0.7 copy-start.8
  145.7 13.2 %collective-permute-start.22 = (bf16[256,1024]{1,0:T(8,128)(2,1)}, bf16[256,1024]{1,0:T(8,128)(2,1)}, u32[]{:S(2)}, u32[]{:S(2)}) collective-permute-start(bf16[256,1024]{1,0:T(8,128)(2,1)} %slice.19.refs_3_), channel_id=1, source_target_pairs={{0,2},{2,0},{1,3},{3,1},{4,6},{6,4},{5,7},{7,5},{8,10},{10,8},{9,1... | collective-permute-start | bytes 1572872 | tf_op jit(solution)/shard_map/ppermute | solution.py:25
  148.3 6.5 %copy-start.5 = (bf16[272,1024]{1,0:T(8,128)(2,1)}, bf16[272,1024]{1,0:T(8,128)(2,1)S(1)}, u32[]{:S(2)}) copy-start(bf16[272,1024]{1,0:T(8,128)(2,1)S(1)} %pad.4.mine_ref) | copy-start | bytes 1671172
  148.4 18.0 %collective-permute-start.28 = (bf16[272,1024]{1,0:T(8,128)(2,1)S(1)}, bf16[272,1024]{1,0:T(8,128)(2,1)}, u32[]{:S(2)}, u32[]{:S(2)}) collective-permute-start(bf16[272,1024]{1,0:T(8,128)(2,1)S(1)} %pad.4.mine_ref), channel_id=1, source_target_pairs={{0,16},{16,0},{1,17},{17,1},{2,18},{18,2},{3,19},{19,3},{4,20},{20... | collective-permute-start | bytes 1671176 | tf_op jit(solution)/shard_map/ppermute | solution.py:25
  149.4 10.0 %collective-permute-start.26 = (bf16[4,256,256]{2,1,0:T(8,128)(2,1)}, bf16[4,256,256]{2,1,0:T(8,128)(2,1)}, u32[]{:S(2)}, u32[]{:S(2)}) collective-permute-start(bf16[4,256,256]{2,1,0:T(8,128)(2,1)} %get-tuple-element.133), channel_id=1, source_target_pairs={{0,1},{1,0},{2,3},{3,2},{4,5},{5,4},{6,7},{7,6},{8,9},{9,8},{10,11... | collective-permute-start | bytes 1572872 | tf_op jit(solution)/shard_map/ppermute | solution.py:25
  154.8 6.3 %collective-permute-start.25 = (bf16[256,1024]{1,0:T(8,128)(2,1)}, bf16[256,1024]{1,0:T(8,128)(2,1)}, u32[]{:S(2)}, u32[]{:S(2)}) collective-permute-start(bf16[256,1024]{1,0:T(8,128)(2,1)} %get-tuple-element.132), channel_id=1, source_target_pairs={{0,1},{1,0},{2,3},{3,2},{4,5},{5,4},{6,7},{7,6},{8,9},{9,8},{10,11... | collective-permute-start | bytes 1572872 | tf_op jit(solution)/shard_map/ppermute | solution.py:25
  158.9 2.6 %collective-permute-start.23 = (bf16[256,1024]{1,0:T(8,128)(2,1)}, bf16[256,1024]{1,0:T(8,128)(2,1)}, u32[]{:S(2)}, u32[]{:S(2)}) collective-permute-start(bf16[256,1024]{1,0:T(8,128)(2,1)} %collective-permute-done.22.refs_0_), channel_id=1, source_target_pairs={{0,1},{1,0},{2,3},{3,2},{4,5},{5,4},{6,7},{7,6},{8,9},{9,8},{10,11... | collective-permute-start | bytes 1572872 | tf_op jit(solution)/shard_map/ppermute | solution.py:25
  158.9 2.2 %collective-permute-start.27 = (bf16[2,256,256]{2,1,0:T(8,128)(2,1)}, bf16[2,256,256]{2,1,0:T(8,128)(2,1)S(1)}, u32[]{:S(2)}, u32[]{:S(2)}) collective-permute-start(bf16[2,256,256]{2,1,0:T(8,128)(2,1)} %get-tuple-element.134), channel_id=1, source_target_pairs={{0,1},{1,0},{2,3},{3,2},{4,5},{5,4},{6,7},{7,6},{8,9},{9,8},{10,11... | collective-permute-start | bytes 786440 | tf_op jit(solution)/shard_map/ppermute | solution.py:25
  161.1 0.7 copy-start.7
Sparse Core Ops, SparseCore 0:
  10.6 49.9 all-gather.2
  101.4 43.2 reduce-scatter.1

commit v6 on v4

--- a/solution.py
+++ b/solution.py
@@ -355,11 +355,11 @@
 
 
 def join(where, mine, theirs):
-    half, features = mine.shape
+    half, features = mine.shape[0] - 16, mine.shape[1]
 
     def kernel(where_ref, mine_ref, theirs_ref, out_ref):
         at = pl.multiple_of(where_ref[2] * half, half)
-        out_ref[pl.ds(at, half), :] = mine_ref[...]
+        out_ref[pl.ds(at, half), :] = mine_ref[pl.ds(0, half), :]
         out_ref[pl.ds(half - at, half), :] = theirs_ref[pl.ds(0, half), :]
 
     return pl.pallas_call(
@@ -416,7 +416,8 @@
     parts = [jnp.concatenate([own, peaks])]
     parts += [lax.dynamic_index_in_dim(mine, z ^ k, keepdims=False) for k in (1, 2, 3)]
     cots[1], *parts = lax.optimization_barrier((cots[1], *parts))
-    side0, rest3 = swap(parts[0], "x"), swap(parts[3], "replica")
+    side0 = swap(parts[0], "x")
+    rest3 = swap(jnp.concatenate([parts[3], peaks]), "replica")
     swapped, other = lax.optimization_barrier((swapped, other))
     term = weight_terms(slots, swapped, cots + diagonal, (0, 1, 2, 3), [])
     stage = functools.partial(consume, where, scale, hidden, other, [cotangent, cots[1]])
@@ -425,41 +426,43 @@
         return [unit for _, _, unit in units]
 
     term, side0, rest3, *parts = lax.optimization_barrier((term, side0, rest3, *parts))
+    rest3 = rest3[:half]
     total = lax.psum_scatter(term, "z", scatter_dimension=0, tiled=True)
-    side1, other0 = swap(parts[1], "x"), swap(side0[:half], "replica")
+    side1, other0 = swap(parts[1], "x"), swap(side0, "replica")
     units = [(own, 0, (0, 0, 0)), (rest0, 0, (0, 0, 1))] + [(mine, None, (k, 0, 0)) for k in (1, 2, 3)]
     *state, away0, away1 = stage(units, [], None)
     first = ([swap(away0, "core"), swap(away1, "core")], codes_of(units))
 
-    side1, other0, *rest = lax.optimization_barrier((side1, other0, *state, *parts))
-    state, parts = rest[:3], rest[3:]
-    side2, other1 = swap(parts[2], "x"), swap(side1, "replica")
+    peak = jnp.maximum(peaks, side0[half:])
+    peak = jnp.max(jnp.maximum(peak, swap(peak, "core"))).astype(F32)
+    peak_ratio = (peak / limit).reshape(1)
+
+    parts[2], *state = lax.optimization_barrier((parts[2], *state))
+    side2 = swap(parts[2], "x")
+    side1, other0, peak_ratio, *state = lax.optimization_barrier((side1, other0, peak_ratio, *state))
+    other1 = swap(side1, "replica")
     units = [(side0, 0, (0, 1, 0)), (other0, 0, (0, 1, 1)), (side1, 0, (1, 1, 0)), (rest1, 0, (1, 0, 1))]
     *state, away = stage(units, state, None)
     second = ([swap(away, "core")], codes_of(units))
 
-    side2, other1, *rest = lax.optimization_barrier((side2, other1, *state, *parts))
-    state, parts = rest[:3], rest[3:]
-    side3, other2 = swap(parts[3], "x"), swap(side2, "replica")
+    parts[3], *state = lax.optimization_barrier((parts[3], *state))
+    side3 = swap(parts[3], "x")
+    side2, other1, *state = lax.optimization_barrier((side2, other1, *state))
+    other2 = swap(side2, "replica")
     units = [(rest2, 0, (2, 0, 1)), (rest3, 0, (3, 0, 1)), (other1, 0, (1, 1, 1)), (side2, 0, (2, 1, 0))]
     *state, away = stage(units, state, first)
     late, late_units = [swap(away, "core")], [codes_of(units)]
 
-    side3, other2, rest3, *state = lax.optimization_barrier((side3, other2, rest3, *state))
+    rest3, *state = lax.optimization_barrier((rest3, *state))
     other3 = swap(rest3, "x")
+    side3, other2, *state = lax.optimization_barrier((side3, other2, *state))
     units = [(other2, 0, (2, 1, 1)), (side3, 0, (3, 1, 0))]
     *state, away = stage(units, state, second, last=True)
     late.append(swap(away, "core"))
     late_units.append(codes_of(units))
 
-    peak = jnp.maximum(jnp.max(peaks), jnp.max(side0[half:]))
-    peak = jnp.full((8, 128), peak.astype(F32))
-    peak = jnp.maximum(peak, swap(peak, "core"))
-    peak_ratio = (peak[0, 0] / limit).reshape(1)
-
-    share = (total.astype(F32) * token_count ** (-0.5)).astype(BF16)
-    other_share = swap(jnp.pad(share, ((0, 16), (0, 0))), "replica")
-    other3, peak_ratio = lax.optimization_barrier((other3, peak_ratio))
+    share = jnp.pad((total.astype(F32) * token_count ** (-0.5)).astype(BF16), ((0, 16), (0, 0)))
+    other_share = swap(share, "replica")
     input_gradient, projected_keys = finish(
         where,
         scale,

time: 177 us -> 172 us (0.972)
  waiting for transfers between devices: 58.4 us -> 53.1 us
    ppermute x29, waiting for transfers between devices: 47.1 us -> 37.1 us  [swap(): return lax.ppermute(block, axis, [(i, i ^ mask) for i in range(size)])]
    reduce_scatter x1, waiting for transfers between devices: 0.02 us -> 4.72 us  [body(): total = lax.psum_scatter(term, 'z', scatter_dimension=0, tiled=True)]
    concatenate x0 -> x1, other arithmetic: none -> 1.88 us  [body(): rest3 = swap(jnp.concatenate([parts[3], peaks]), 'replica')]
  transfers between devices with their start and end apart: 32 -> 32, of which waited for: 18 -> 13; matrix products, arithmetic and copies ran while one was open for 8% -> 8% of each run, Pallas kernels for 29% -> 29%
where the time goes in v6:
time: 172 us; the launch traced here: 171 us
  waiting for transfers between devices  53.1 us (31%)
  Pallas kernels  52.3 us (30%)
  starting transfers between devices  30.5 us (18%)
  between operations  16.8 us (10%)
  other arithmetic  11 us (6%)
  local copies, waits for them, and re-layouts  7.59 us (4%)
    ppermute x29, waiting for transfers between devices, swap(): return lax.ppermute(block, axis, [(i, i ^ mask) for i in range(size)])  37.1 us
    pallas_call x4, Pallas kernels, consume(): pl.pallas_call(kernel, out_shape=[sums, jax.ShapeDtypeStruct(sums.shape,...  29.3 us
    ppermute x29, starting transfers between devices, swap(): return lax.ppermute(block, axis, [(i, i ^ mask) for i in range(size)])  25.7 us
    all_gather x1, waiting for transfers between devices, body(): mine = lax.all_gather(own, 'z', axis=0)  11.2 us
    pallas_call x1, Pallas kernels, weight_terms(): pl.pallas_call(kernel, out_shape=jax.ShapeDtypeStruct((width, features),...  9.45 us
    pallas_call x1, Pallas kernels, pack(): pl.pallas_call(kernel, out_shape=[jax.ShapeDtypeStruct((group, tokens, nz...  6.65 us
    reduce_scatter x1, waiting for transfers between devices, body(): total = lax.psum_scatter(term, 'z', scatter_dimension=0, tiled=True)  4.72 us
    all_to_all x1, starting transfers between devices, body(): lax.all_to_all(for_group, ('replica', 'x', 'core'), 0, 0, tiled=True)  4.69 us
  transfers between devices with their start and end apart: 32, of which 13 were waited for; matrix products, arithmetic and copies ran while one was open for 8% of the time, Pallas kernels for 29%

profile of v6, /device:TPU:0, one launch (start us, length us, event | category | flops | bytes accessed | tf_op | source)
XLA Modules:
  0.0 171.4 jit_solution(9020370382820923082)
XLA Ops:
  8.0 2.4 %clamp_convert_fusion = (bf16[256,1024]{1,0:T(8,128)(2,1)}, bf16[256,1024]{1,0:T(8,128)(2,1)}) fusion(bf16[512,1024]{1,0:T(8,128)(2,1)} %param.5, s32[]{:T(128)S(6)} %select_n.17, f32[]{:T(128)S(6)} %div.11, s32[]{:T(128)S(6)} %select_n.16), kind=kLoop, calls=%fused_computation.3 | loop fusion | flops 2097152 | bytes 2097164 | tf_op jit(solution)/shard_map/convert_element_type | solution.py:20
  10.4 3.0 %collective-permute-start.1 = (bf16[256,1024]{1,0:T(8,128)(2,1)S(1)}, bf16[256,1024]{1,0:T(8,128)(2,1)}, u32[]{:S(2)}, u32[]{:S(2)}) collective-permute-start(bf16[256,1024]{1,0:T(8,128)(2,1)S(1)} %copy-done.1), channel_id=1, source_target_pairs={{0,16},{16,0},{1,17},{17,1},{2,18},{18,2},{3,19},{19,3},{4,20},{20... | collective-permute-start | bytes 1572872 | tf_op jit(solution)/shard_map/ppermute | solution.py:25
  13.5 1.5 collective-permute-start
  15.0 0.6 pad_add_fusion.core_ref.where_ref
  15.6 6.7 %pack.1 = (bf16[8,256,1024]{2,1,0:T(8,128)(2,1)}, bf16[8,256,512]{2,1,0:T(8,128)(2,1)}) custom-call(s32[4]{0:T(128)} %pad_add_fusion.core_ref.where_ref, bf16[256,8192]{1,0:T(8,128)(2,1)} %hidden_ref.5), custom_call_target="tpu_custom_call" | custom-call | tf_op jit(solution)/shard_map/pack/pallas_call | solution.py:61
  22.2 3.3 %collective-permute-done.1 = bf16[256,1024]{1,0:T(8,128)(2,1)} collective-permute-done((bf16[256,1024]{1,0:T(8,128)(2,1)S(1)}, bf16[256,1024]{1,0:T(8,128)(2,1)}, u32[]{:S(2)}, u32[]{:S(2)}) %collective-permute-start.1) | collective-permute-done | bytes 524320 | tf_op jit(solution)/shard_map/ppermute | solution.py:25
  25.5 1.5 collective-permute-done
  27.0 4.7 %all-to-all-start = ((bf16[8,256,1024]{2,1,0:T(8,128)(2,1)}), bf16[8,256,1024]{2,1,0:T(8,128)(2,1)}, u32[]{:S(2)}, u32[]{:S(2)}) async-start(bf16[8,256,1024]{2,1,0:T(8,128)(2,1)} %get-tuple-element.82), calls=%async_computation | async-start | bytes 8388608 | tf_op jit(solution)/shard_map/all_to_all | solution.py:397
  31.7 0.0 reduce-scatter.2.cloned.1.call-start
  31.7 0.1 abs_reduce_fusion
  31.9 1.6 collective-permute-start.3
  33.5 5.1 %collective-permute-done.3 = bf16[16,1024]{1,0:T(8,128)(2,1)S(1)} collective-permute-done((bf16[16,1024]{1,0:T(8,128)(2,1)S(1)}, bf16[16,1024]{1,0:T(8,128)(2,1)S(1)}, u32[]{:S(2)}, u32[]{:S(2)}) %collective-permute-start.3) | collective-permute-done | bytes 32800 | tf_op jit(solution)/shard_map/ppermute | solution.py:25
  38.6 1.6 collective-permute-start.4
  40.2 6.0 %collective-permute-done.4 = bf16[16,1024]{1,0:T(8,128)(2,1)S(1)} collective-permute-done((bf16[16,1024]{1,0:T(8,128)(2,1)S(1)}, bf16[16,1024]{1,0:T(8,128)(2,1)S(1)}, u32[]{:S(2)}, u32[]{:S(2)}) %collective-permute-start.4) | collective-permute-done | bytes 32800 | tf_op jit(solution)/shard_map/ppermute | solution.py:25
  46.3 2.6 %pad_maximum_fusion.refs_0_ = bf16[768,1024]{1,0:T(8,128)(2,1)} fusion(bf16[256,1024]{1,0:T(8,128)(2,1)} %collective-permute-done.1, bf16[256,1024]{1,0:T(8,128)(2,1)} %collective-permute-done, bf16[256,1024]{1,0:T(8,128)(2,1)S(1)} %copy-done.1), kind=kLoop, calls=%fused_computation | loop fusion | flops 4718592 | bytes 3145728 | tf_op jit(solution)/shard_map/concatenate | solution.py:404
  48.8 0.5 collective-permute-start.2
  49.3 11.2 %all-gather.3.cloned.1.call-done = bf16[1024,1024]{1,0:T(8,128)(2,1)} async-done(((bf16[256,1024]{1,0:T(8,128)(2,1)}), bf16[1024,1024]{1,0:T(8,128)(2,1)}) %all-gather.3.cloned.1.call-update) | async-done | bytes 2097168 | tf_op jit(solution)/shard_map/all_gather | solution.py:390
  60.6 1.1 collective-permute-start.7
  61.7 0.5 collective-permute-start.6
  62.2 1.1 slice.13
  63.4 1.0 slice.12
  64.3 1.6 collective-permute-start.8
  65.9 0.8 pad_maximum_fusion.2
  66.8 1.5 collective-permute-start.9
  68.3 1.2 dynamic-slice_bitcast_fusion
  69.4 1.9 %pad_maximum_fusion.1 = bf16[272,1024]{1,0:T(8,128)(2,1)} fusion(bf16[16,1024]{1,0:T(8,128)(2,1)S(1)} %fusion, bf16[256,1024]{1,0:T(8,128)(2,1)} %get-tuple-element.137), kind=kLoop, calls=%fused_computation.5 | loop fusion | flops 1114112 | bytes 1114112 | tf_op jit(solution)/shard_map/concatenate | solution.py:420
  71.3 14.1 %collective-permute-done.8 = bf16[128,1024]{1,0:T(8,128)(2,1)S(1)} collective-permute-done((bf16[128,1024]{1,0:T(8,128)(2,1)S(1)}, bf16[128,1024]{1,0:T(8,128)(2,1)S(1)}, u32[]{:S(2)}, u32[]{:S(2)}) %collective-permute-start.8) | collective-permute-done | bytes 262176 | tf_op jit(solution)/shard_map/ppermute | solution.py:25
  85.4 1.5 collective-permute-start.12
  86.9 0.5 collective-permute-start.11
  87.5 0.8 copy-done.8
  88.3 0.1 collective-permute-start.10
  88.4 0.7 stack.55.slots_ref
  89.1 1.3 collective-permute-done.10.refs_3_
  90.4 9.4 %weight_terms.1 = bf16[1024,1024]{1,0:T(8,128)(2,1)} custom-call(s32[8]{0:T(128)} %stack.55.slots_ref, bf16[8,256,1024]{2,1,0:T(8,128)(2,1)} %all-to-all-done.swapped_ref, bf16[768,1024]{1,0:T(8,128)(2,1)} %pad_maximum_fusion.refs_0_, bf16[768,1024]{1,0:T(8,128)(2,1)} %copy-done, bf16[256,1024]{1,0:T(8,128)(2,1)} %copy-done.6, ...), custom_call_target="tpu_custom_call" | custom-call | flops 1 | bytes 1 | tf_op jit(solution)/shard_map/weight_terms/pallas_call | solution.py:111
  99.9 0.1 collective-permute-done.12
  100.0 1.2 collective-permute-done.11.refs_2_
  101.3 0.6 collective-permute-start.15
  101.9 0.6 collective-permute-start.14
  102.4 0.8 slice_maximum_fusion
  103.2 8.9 %consume.4 = (f32[256,1024]{1,0:T(8,128)}, f32[256,1024]{1,0:T(8,128)}, bf16[256,8192]{1,0:T(8,128)(2,1)}, bf16[4,256,256]{2,1,0:T(8,128)(2,1)}, bf16[1,256,256]{2,1,0:T(8,128)(2,1)}) custom-call(s32[4]{0:T(128)} %pad_add_fusion.core_ref.where_ref, f32[1]{0:T(128)} %bitcast.5.scale_ref, bf16[256,8192]{1,0:T(8,128)(2,1)} %hidden_ref.5, ...), custom_call_target="tpu_custom_call" | custom-call | flops 1 | bytes 1 | tf_op jit(solution)/shard_map/consume/pallas_call | solution.py:235
  112.2 1.5 collective-permute-start.13
  113.7 0.6 maximum_reduce_fusion
  115.0 1.6 collective-permute-start.17
  116.5 0.5 collective-permute-start.19
  117.1 1.9 %slice.14.refs_3_ = bf16[256,1024]{1,0:T(8,128)(2,1)} slice(bf16[272,1024]{1,0:T(8,128)(2,1)} %collective-permute-done.12), slice={[0:256], [0:1024]} | slice | bytes 1048576 | tf_op jit(solution)/shard_map/slice | solution.py:429
  118.9 7.4 %consume.5 = (f32[256,1024]{1,0:T(8,128)}, f32[256,1024]{1,0:T(8,128)}, bf16[256,8192]{1,0:T(8,128)(2,1)}, bf16[4,256,256]{2,1,0:T(8,128)(2,1)}) custom-call(s32[4]{0:T(128)} %pad_add_fusion.core_ref.where_ref, f32[1]{0:T(128)} %bitcast.5.scale_ref, bf16[256,8192]{1,0:T(8,128)(2,1)} %hidden_ref.5, ...), custom_call_target="tpu_custom_call", output_to_operand_aliasing={{0}: (10, {}), {2}: (12, {}), {1}: (11, {})} | custom-call | flops 1 | bytes 1 | tf_op jit(solution)/shard_map/consume/pallas_call | solution.py:235
  126.4 1.1 collective-permute-start.22
  127.4 2.0 %collective-permute-done.17.refs_4_ = bf16[256,1024]{1,0:T(8,128)(2,1)} collective-permute-done((bf16[256,1024]{1,0:T(8,128)(2,1)}, bf16[256,1024]{1,0:T(8,128)(2,1)}, u32[]{:S(2)}, u32[]{:S(2)}) %collective-permute-start.17) | collective-permute-done | bytes 524320 | tf_op jit(solution)/shard_map/ppermute | solution.py:25
  129.4 1.5 collective-permute-start.23
  130.9 0.6 copy-done.10
  131.6 7.6 %consume.6 = (f32[256,1024]{1,0:T(8,128)}, f32[256,1024]{1,0:T(8,128)}, bf16[256,8192]{1,0:T(8,128)(2,1)}, bf16[4,256,256]{2,1,0:T(8,128)(2,1)}) custom-call(s32[4]{0:T(128)} %pad_add_fusion.core_ref.where_ref, f32[1]{0:T(128)} %bitcast.5.scale_ref, bf16[256,8192]{1,0:T(8,128)(2,1)} %hidden_ref.5, ...), custom_call_target="tpu_custom_call", output_to_operand_aliasing={{0}: (10, {}), {2}: (12, {}), {1}: (11, {})} | custom-call | flops 1 | bytes 1 | tf_op jit(solution)/shard_map/consume/pallas_call | solution.py:235
  139.2 0.7 collective-permute-start.20
  139.8 4.7 %reduce-scatter.2.cloned.1.call-done = bf16[256,1024]{1,0:T(8,128)(2,1)} async-done(((bf16[1024,1024]{1,0:T(8,128)(2,1)}), bf16[256,1024]{1,0:T(8,128)(2,1)}) %reduce-scatter.2.cloned.1.call-update) | async-done | bytes 524304 | tf_op jit(solution)/shard_map/reduce_scatter | solution.py:430
  144.6 1.1 multiply_convert_fusion
  145.8 1.6 collective-permute-start.28
  147.3 5.4 %consume.7 = (f32[256,1024]{1,0:T(8,128)}, bf16[256,1024]{1,0:T(8,128)(2,1)}, bf16[256,8192]{1,0:T(8,128)(2,1)}, bf16[2,256,256]{2,1,0:T(8,128)(2,1)}) custom-call(s32[4]{0:T(128)} %pad_add_fusion.core_ref.where_ref, f32[1]{0:T(128)} %bitcast.5.scale_ref, bf16[256,8192]{1,0:T(8,128)(2,1)} %hidden_ref.5, ...), custom_call_target="tpu_custom_call", output_to_operand_aliasing={{0}: (8, {}), {2}: (10, {})} | custom-call | flops 1 | bytes 1 | tf_op jit(solution)/shard_map/consume/pallas_call | solution.py:235
  152.7 0.6 collective-permute-start.25
  153.3 0.1 collective-permute-start.21
  153.4 0.4 collective-permute-start.27
  153.8 2.0 %collective-permute-done.27.refs_5_ = bf16[2,256,256]{2,1,0:T(8,128)(2,1)S(1)} collective-permute-done((bf16[2,256,256]{2,1,0:T(8,128)(2,1)}, bf16[2,256,256]{2,1,0:T(8,128)(2,1)S(1)}, u32[]{:S(2)}, u32[]{:S(2)}) %collective-permute-start.27) | collective-permute-done | bytes 262176 | tf_op jit(solution)/shard_map/ppermute | solution.py:25
  155.8 0.5 collective-permute-done.21.refs_1_
  156.3 0.2 copy-done.9
  156.5 4.6 %finish.1 = (bf16[256,8192]{1,0:T(8,128)(2,1)}, bf16[256,1024]{1,0:T(8,128)(2,1)}) custom-call(s32[4]{0:T(128)} %pad_add_fusion.core_ref.where_ref, f32[1]{0:T(128)} %bitcast.5.scale_ref, bf16[256,8192]{1,0:T(8,128)(2,1)} %hidden_ref.5, bf16[256,1024]{1,0:T(8,128)(2,1)} %cot_ref.1, ...), custom_call_target="tpu_custom_call", output_to_operand_aliasing={{0}: (10, {})} | custom-call | flops 1 | bytes 1 | tf_op jit(solution)/shard_map/finish/pallas_call | solution.py:330
  161.1 2.3 %join.1 = bf16[512,1024]{1,0:T(8,128)(2,1)} custom-call(s32[4]{0:T(128)} %pad_add_fusion.core_ref.where_ref, bf16[272,1024]{1,0:T(8,128)(2,1)} %copy-done.5, bf16[272,1024]{1,0:T(8,128)(2,1)} %collective-permute-done.28.theirs_ref), custom_call_target="tpu_custom_call" | custom-call | tf_op jit(solution)/shard_map/join/pallas_call | solution.py:365
  (52 shorter events, 0.3 us)
Async XLA Ops:
  7.2 3.3 %copy-start.1 = (bf16[256,1024]{1,0:T(8,128)(2,1)S(1)}, bf16[256,1024]{1,0:T(8,128)(2,1)}, u32[]{:S(2)}) copy-start(bf16[256,1024]{1,0:T(8,128)(2,1)} %cot_ref.1) | copy-start | bytes 1572868
  7.2 53.4 %all-gather.3.cloned.1.call-start = ((), (), s32[]{:S(2)}) async-start(), calls=%async_computation.3 | async-start | bytes 2621440 | tf_op jit(solution)/shard_map/all_gather | solution.py:390
  10.4 15.1 %collective-permute-start.1 = (bf16[256,1024]{1,0:T(8,128)(2,1)S(1)}, bf16[256,1024]{1,0:T(8,128)(2,1)}, u32[]{:S(2)}, u32[]{:S(2)}) collective-permute-start(bf16[256,1024]{1,0:T(8,128)(2,1)S(1)} %copy-done.1), channel_id=1, source_target_pairs={{0,16},{16,0},{1,17},{17,1},{2,18},{18,2},{3,19},{19,3},{4,20},{20... | collective-permute-start | bytes 1572872 | tf_op jit(solution)/shard_map/ppermute | solution.py:25
  13.5 13.5 %collective-permute-start = (bf16[256,1024]{1,0:T(8,128)(2,1)S(1)}, bf16[256,1024]{1,0:T(8,128)(2,1)}, u32[]{:S(2)}, u32[]{:S(2)}) collective-permute-start(bf16[256,1024]{1,0:T(8,128)(2,1)S(1)} %copy-done.1), channel_id=1, source_target_pairs={{0,2},{2,0},{1,3},{3,1},{4,6},{6,4},{5,7},{7,5},{8,10},{10,8},{9,1... | collective-permute-start | bytes 1572872 | tf_op jit(solution)/shard_map/ppermute | solution.py:25
  27.0 4.8 %copy-start.4 = (bf16[512,1024]{1,0:T(8,128)(2,1)S(1)}, bf16[512,1024]{1,0:T(8,128)(2,1)}, u32[]{:S(2)}) copy-start(bf16[512,1024]{1,0:T(8,128)(2,1)} %param.5) | copy-start | bytes 3145732
  27.0 62.1 %all-to-all-start = ((bf16[8,256,1024]{2,1,0:T(8,128)(2,1)}), bf16[8,256,1024]{2,1,0:T(8,128)(2,1)}, u32[]{:S(2)}, u32[]{:S(2)}) async-start(bf16[8,256,1024]{2,1,0:T(8,128)(2,1)} %get-tuple-element.82), calls=%async_computation | async-start | bytes 8388608 | tf_op jit(solution)/shard_map/all_to_all | solution.py:397
  31.7 112.9 %reduce-scatter.2.cloned.1.call-start = ((), (), s32[]{:S(2)}) async-start(), calls=%async_computation.2 | async-start | bytes 2621440 | tf_op jit(solution)/shard_map/reduce_scatter | solution.py:430
  31.9 6.7 %collective-permute-start.3 = (bf16[16,1024]{1,0:T(8,128)(2,1)S(1)}, bf16[16,1024]{1,0:T(8,128)(2,1)S(1)}, u32[]{:S(2)}, u32[]{:S(2)}) collective-permute-start(bf16[16,1024]{1,0:T(8,128)(2,1)S(1)} %broadcast_in_dim.2), channel_id=1, source_target_pairs={{0,4},{4,0},{8,12},{12,8},{1,5},{5,1},{9,13},{13,9},{2,6},{6,2},{1... | collective-permute-start | bytes 98312 | tf_op jit(solution)/shard_map/ppermute | solution.py:25
  38.6 7.7 %collective-permute-start.4 = (bf16[16,1024]{1,0:T(8,128)(2,1)S(1)}, bf16[16,1024]{1,0:T(8,128)(2,1)S(1)}, u32[]{:S(2)}, u32[]{:S(2)}) collective-permute-start(bf16[16,1024]{1,0:T(8,128)(2,1)S(1)} %broadcast_maximum_fusion), channel_id=1, source_target_pairs={{0,8},{4,12},{8,0},{12,4},{1,9},{5,13},{9,1},{13,5},{2,10},{6,14},... | collective-permute-start | bytes 98312 | tf_op jit(solution)/shard_map/ppermute | solution.py:25
  46.3 19.6 %copy-start.2 = (bf16[256,1024]{1,0:T(8,128)(2,1)S(1)}, bf16[256,1024]{1,0:T(8,128)(2,1)}, u32[]{:S(2)}) copy-start(bf16[256,1024]{1,0:T(8,128)(2,1)} %get-tuple-element.88.refs_2_) | copy-start | bytes 1572868
  48.8 17.9 %collective-permute-start.5 = (bf16[768,1024]{1,0:T(8,128)(2,1)}, bf16[768,1024]{1,0:T(8,128)(2,1)S(1)}, u32[]{:S(2)}, u32[]{:S(2)}) collective-permute-start(bf16[768,1024]{1,0:T(8,128)(2,1)} %pad_maximum_fusion.refs_0_), channel_id=1, source_target_pairs={{0,1},{1,0},{2,3},{3,2},{4,5},{5,4},{6,7},{7,6},{8,9},{9,8},{10,11... | collective-permute-start | bytes 4718600 | tf_op jit(solution)/shard_map/ppermute | solution.py:25
  48.8 40.3 %collective-permute-start.2 = (bf16[8,256,512]{2,1,0:T(8,128)(2,1)}, bf16[8,256,512]{2,1,0:T(8,128)(2,1)}, u32[]{:S(2)}, u32[]{:S(2)}) collective-permute-start(bf16[8,256,512]{2,1,0:T(8,128)(2,1)} %get-tuple-element.83), channel_id=1, source_target_pairs={{0,1},{1,0},{2,3},{3,2},{4,5},{5,4},{6,7},{7,6},{8,9},{9,8},{10,11... | collective-permute-start | bytes 6291464 | tf_op jit(solution)/shard_map/ppermute | solution.py:25
  60.6 26.9 %collective-permute-start.7 = (bf16[256,1024]{1,0:T(8,128)(2,1)}, bf16[256,1024]{1,0:T(8,128)(2,1)S(1)}, u32[]{:S(2)}, u32[]{:S(2)}) collective-permute-start(bf16[256,1024]{1,0:T(8,128)(2,1)} %get-tuple-element.93.refs_3_), channel_id=1, source_target_pairs={{0,8},{4,12},{8,0},{12,4},{1,9},{5,13},{9,1},{13,5},{2,10},{6,14},... | collective-permute-start | bytes 1572872 | tf_op jit(solution)/shard_map/ppermute | solution.py:25
  61.7 26.6 %collective-permute-start.6 = (bf16[256,1024]{1,0:T(8,128)(2,1)}, bf16[256,1024]{1,0:T(8,128)(2,1)}, u32[]{:S(2)}, u32[]{:S(2)}) collective-permute-start(bf16[256,1024]{1,0:T(8,128)(2,1)} %get-tuple-element.93.refs_3_), channel_id=1, source_target_pairs={{0,4},{4,0},{8,12},{12,8},{1,5},{5,1},{9,13},{13,9},{2,6},{6,2},{1... | collective-permute-start | bytes 1572872 | tf_op jit(solution)/shard_map/ppermute | solution.py:25
  62.2 6.0 %copy-start.3 = (bf16[1024,1024]{1,0:T(8,128)(2,1)S(1)}, bf16[1024,1024]{1,0:T(8,128)(2,1)}, u32[]{:S(2)}) copy-start(bf16[1024,1024]{1,0:T(8,128)(2,1)} %all-gather.3.cloned.1.call-done) | copy-start | bytes 6291460
  64.3 21.1 %collective-permute-start.8 = (bf16[128,1024]{1,0:T(8,128)(2,1)S(1)}, bf16[128,1024]{1,0:T(8,128)(2,1)S(1)}, u32[]{:S(2)}, u32[]{:S(2)}) collective-permute-start(bf16[128,1024]{1,0:T(8,128)(2,1)S(1)} %slice.12), channel_id=1, source_target_pairs={{0,2},{2,0},{1,3},{3,1},{4,6},{6,4},{5,7},{7,5},{8,10},{10,8},{9,1... | collective-permute-start | bytes 786440 | tf_op jit(solution)/shard_map/ppermute | solution.py:25
  66.8 4.6 %copy-start = (bf16[768,1024]{1,0:T(8,128)(2,1)}, bf16[768,1024]{1,0:T(8,128)(2,1)S(1)}, u32[]{:S(2)}) copy-start(bf16[768,1024]{1,0:T(8,128)(2,1)S(1)} %collective-permute-done.5.refs_1_) | copy-start | bytes 4718596
  66.8 20.1 %collective-permute-start.9 = (bf16[128,1024]{1,0:T(8,128)(2,1)S(1)}, bf16[128,1024]{1,0:T(8,128)(2,1)S(1)}, u32[]{:S(2)}, u32[]{:S(2)}) collective-permute-start(bf16[128,1024]{1,0:T(8,128)(2,1)S(1)} %slice.13), channel_id=1, source_target_pairs={{0,16},{16,0},{1,17},{17,1},{2,18},{18,2},{3,19},{19,3},{4,20},{20... | collective-permute-start | bytes 786440 | tf_op jit(solution)/shard_map/ppermute | solution.py:25
  85.4 14.6 %collective-permute-start.12 = (bf16[272,1024]{1,0:T(8,128)(2,1)}, bf16[272,1024]{1,0:T(8,128)(2,1)}, u32[]{:S(2)}, u32[]{:S(2)}) collective-permute-start(bf16[272,1024]{1,0:T(8,128)(2,1)} %pad_maximum_fusion.1), channel_id=1, source_target_pairs={{0,16},{16,0},{1,17},{17,1},{2,18},{18,2},{3,19},{19,3},{4,20},{20... | collective-permute-start | bytes 1671176 | tf_op jit(solution)/shard_map/ppermute | solution.py:25
  86.9 14.3 %collective-permute-start.11 = (bf16[272,1024]{1,0:T(8,128)(2,1)}, bf16[272,1024]{1,0:T(8,128)(2,1)}, u32[]{:S(2)}, u32[]{:S(2)}) collective-permute-start(bf16[272,1024]{1,0:T(8,128)(2,1)} %pad_maximum_fusion.2), channel_id=1, source_target_pairs={{0,2},{2,0},{1,3},{3,1},{4,6},{6,4},{5,7},{7,5},{8,10},{10,8},{9,1... | collective-permute-start | bytes 1671176 | tf_op jit(solution)/shard_map/ppermute | solution.py:25
  87.5 0.8 copy-start.8
  88.3 2.1 %copy-start.6 = (bf16[256,1024]{1,0:T(8,128)(2,1)}, bf16[256,1024]{1,0:T(8,128)(2,1)S(1)}, u32[]{:S(2)}) copy-start(bf16[256,1024]{1,0:T(8,128)(2,1)S(1)} %constant_dynamic-update-slice_fusion.refs_2_) | copy-start | bytes 1572868
  88.3 2.1 %collective-permute-start.10 = (bf16[256,1024]{1,0:T(8,128)(2,1)S(1)}, bf16[256,1024]{1,0:T(8,128)(2,1)}, u32[]{:S(2)}, u32[]{:S(2)}) collective-permute-start(bf16[256,1024]{1,0:T(8,128)(2,1)S(1)} %constant_dynamic-update-slice_fusion.refs_2_), channel_id=1, source_target_pairs={{0,1},{1,0},{2,3},{3,2},{4,5},{5,4},{6,7},{7,6},{8,9},{9,8},{10,11... | collective-permute-start | bytes 1572872 | tf_op jit(solution)/shard_map/ppermute | solution.py:25
  101.3 13.7 %collective-permute-start.15 = (bf16[272,1024]{1,0:T(8,128)(2,1)}, bf16[272,1024]{1,0:T(8,128)(2,1)S(1)}, u32[]{:S(2)}, u32[]{:S(2)}) collective-permute-start(bf16[272,1024]{1,0:T(8,128)(2,1)} %collective-permute-done.11.refs_2_), channel_id=1, source_target_pairs={{0,16},{16,0},{1,17},{17,1},{2,18},{18,2},{3,19},{19,3},{4,20},{20... | collective-permute-start | bytes 1671176 | tf_op jit(solution)/shard_map/ppermute | solution.py:25
  101.9 13.1 %collective-permute-start.14 = (bf16[256,1024]{1,0:T(8,128)(2,1)}, bf16[256,1024]{1,0:T(8,128)(2,1)}, u32[]{:S(2)}, u32[]{:S(2)}) collective-permute-start(bf16[256,1024]{1,0:T(8,128)(2,1)} %get-tuple-element.108), channel_id=1, source_target_pairs={{0,2},{2,0},{1,3},{3,1},{4,6},{6,4},{5,7},{7,5},{8,10},{10,8},{9,1... | collective-permute-start | bytes 1572872 | tf_op jit(solution)/shard_map/ppermute | solution.py:25
  103.2 10.5 %collective-permute-start.16 = (bf16[16,1024]{1,0:T(8,128)(2,1)S(1)}, bf16[16,1024]{1,0:T(8,128)(2,1)S(1)}, u32[]{:S(2)}, u32[]{:S(2)}) collective-permute-start(bf16[16,1024]{1,0:T(8,128)(2,1)S(1)} %slice_maximum_fusion), channel_id=1, source_target_pairs={{0,1},{1,0},{2,3},{3,2},{4,5},{5,4},{6,7},{7,6},{8,9},{9,8},{10,11... | collective-permute-start | bytes 98312 | tf_op jit(solution)/shard_map/ppermute | solution.py:25
  112.2 15.3 %collective-permute-start.13 = (bf16[256,1024]{1,0:T(8,128)(2,1)}, bf16[256,1024]{1,0:T(8,128)(2,1)}, u32[]{:S(2)}, u32[]{:S(2)}) collective-permute-start(bf16[256,1024]{1,0:T(8,128)(2,1)} %get-tuple-element.107), channel_id=1, source_target_pairs={{0,2},{2,0},{1,3},{3,1},{4,6},{6,4},{5,7},{7,5},{8,10},{10,8},{9,1... | collective-permute-start | bytes 1572872 | tf_op jit(solution)/shard_map/ppermute | solution.py:25
  115.0 4.0 %copy-start.7 = (bf16[272,1024]{1,0:T(8,128)(2,1)}, bf16[272,1024]{1,0:T(8,128)(2,1)S(1)}, u32[]{:S(2)}) copy-start(bf16[272,1024]{1,0:T(8,128)(2,1)S(1)} %collective-permute-done.15.refs_3_) | copy-start | bytes 1671172
  115.0 14.4 %collective-permute-start.17 = (bf16[256,1024]{1,0:T(8,128)(2,1)}, bf16[256,1024]{1,0:T(8,128)(2,1)}, u32[]{:S(2)}, u32[]{:S(2)}) collective-permute-start(bf16[256,1024]{1,0:T(8,128)(2,1)} %collective-permute-done.14.refs_4_), channel_id=1, source_target_pairs={{0,16},{16,0},{1,17},{17,1},{2,18},{18,2},{3,19},{19,3},{4,20},{20... | collective-permute-start | bytes 1572872 | tf_op jit(solution)/shard_map/ppermute | solution.py:25
  116.5 14.4 %collective-permute-start.18 = (bf16[4,256,256]{2,1,0:T(8,128)(2,1)}, bf16[4,256,256]{2,1,0:T(8,128)(2,1)}, u32[]{:S(2)}, u32[]{:S(2)}) collective-permute-start(bf16[4,256,256]{2,1,0:T(8,128)(2,1)} %get-tuple-element.131), channel_id=1, source_target_pairs={{0,1},{1,0},{2,3},{3,2},{4,5},{5,4},{6,7},{7,6},{8,9},{9,8},{10,11... | collective-permute-start | bytes 1572872 | tf_op jit(solution)/shard_map/ppermute | solution.py:25
  116.5 14.4 %collective-permute-start.19 = (bf16[1,256,256]{2,1,0:T(8,128)(2,1)}, bf16[1,256,256]{2,1,0:T(8,128)(2,1)S(1)}, u32[]{:S(2)}, u32[]{:S(2)}) collective-permute-start(bf16[1,256,256]{2,1,0:T(8,128)(2,1)} %get-tuple-element.132), channel_id=1, source_target_pairs={{0,1},{1,0},{2,3},{3,2},{4,5},{5,4},{6,7},{7,6},{8,9},{9,8},{10,11... | collective-permute-start | bytes 393224 | tf_op jit(solution)/shard_map/ppermute | solution.py:25
  126.4 21.0 %collective-permute-start.22 = (bf16[256,1024]{1,0:T(8,128)(2,1)}, bf16[256,1024]{1,0:T(8,128)(2,1)}, u32[]{:S(2)}, u32[]{:S(2)}) collective-permute-start(bf16[256,1024]{1,0:T(8,128)(2,1)} %get-tuple-element.137), channel_id=1, source_target_pairs={{0,2},{2,0},{1,3},{3,1},{4,6},{6,4},{5,7},{7,5},{8,10},{10,8},{9,1... | collective-permute-start | bytes 1572872 | tf_op jit(solution)/shard_map/ppermute | solution.py:25
  127.4 19.9 %collective-permute-start.24 = (bf16[4,256,256]{2,1,0:T(8,128)(2,1)}, bf16[4,256,256]{2,1,0:T(8,128)(2,1)}, u32[]{:S(2)}, u32[]{:S(2)}) collective-permute-start(bf16[4,256,256]{2,1,0:T(8,128)(2,1)} %get-tuple-element.146), channel_id=1, source_target_pairs={{0,1},{1,0},{2,3},{3,2},{4,5},{5,4},{6,7},{7,6},{8,9},{9,8},{10,11... | collective-permute-start | bytes 1572872 | tf_op jit(solution)/shard_map/ppermute | solution.py:25
  129.4 17.9 %collective-permute-start.23 = (bf16[256,1024]{1,0:T(8,128)(2,1)}, bf16[256,1024]{1,0:T(8,128)(2,1)}, u32[]{:S(2)}, u32[]{:S(2)}) collective-permute-start(bf16[256,1024]{1,0:T(8,128)(2,1)} %collective-permute-done.13.refs_5_), channel_id=1, source_target_pairs={{0,16},{16,0},{1,17},{17,1},{2,18},{18,2},{3,19},{19,3},{4,20},{20... | collective-permute-start | bytes 1572872 | tf_op jit(solution)/shard_map/ppermute | solution.py:25
  130.9 0.7 copy-start.10
  139.2 14.1 %collective-permute-start.20 = (bf16[256,1024]{1,0:T(8,128)(2,1)}, bf16[256,1024]{1,0:T(8,128)(2,1)}, u32[]{:S(2)}, u32[]{:S(2)}) collective-permute-start(bf16[256,1024]{1,0:T(8,128)(2,1)} %slice.14.refs_3_), channel_id=1, source_target_pairs={{0,2},{2,0},{1,3},{3,1},{4,6},{6,4},{5,7},{7,5},{8,10},{10,8},{9,1... | collective-permute-start | bytes 1572872 | tf_op jit(solution)/shard_map/ppermute | solution.py:25
  145.8 7.0 %copy-start.5 = (bf16[272,1024]{1,0:T(8,128)(2,1)}, bf16[272,1024]{1,0:T(8,128)(2,1)S(1)}, u32[]{:S(2)}) copy-start(bf16[272,1024]{1,0:T(8,128)(2,1)S(1)} %pad.4.mine_ref) | copy-start | bytes 1671172
  145.8 15.3 %collective-permute-start.28 = (bf16[272,1024]{1,0:T(8,128)(2,1)S(1)}, bf16[272,1024]{1,0:T(8,128)(2,1)}, u32[]{:S(2)}, u32[]{:S(2)}) collective-permute-start(bf16[272,1024]{1,0:T(8,128)(2,1)S(1)} %pad.4.mine_ref), channel_id=1, source_target_pairs={{0,16},{16,0},{1,17},{17,1},{2,18},{18,2},{3,19},{19,3},{4,20},{20... | collective-permute-start | bytes 1671176 | tf_op jit(solution)/shard_map/ppermute | solution.py:25
  147.3 6.5 %collective-permute-start.26 = (bf16[4,256,256]{2,1,0:T(8,128)(2,1)}, bf16[4,256,256]{2,1,0:T(8,128)(2,1)}, u32[]{:S(2)}, u32[]{:S(2)}) collective-permute-start(bf16[4,256,256]{2,1,0:T(8,128)(2,1)} %get-tuple-element.149), channel_id=1, source_target_pairs={{0,1},{1,0},{2,3},{3,2},{4,5},{5,4},{6,7},{7,6},{8,9},{9,8},{10,11... | collective-permute-start | bytes 1572872 | tf_op jit(solution)/shard_map/ppermute | solution.py:25
  152.7 3.1 %collective-permute-start.25 = (bf16[256,1024]{1,0:T(8,128)(2,1)}, bf16[256,1024]{1,0:T(8,128)(2,1)}, u32[]{:S(2)}, u32[]{:S(2)}) collective-permute-start(bf16[256,1024]{1,0:T(8,128)(2,1)} %get-tuple-element.148), channel_id=1, source_target_pairs={{0,1},{1,0},{2,3},{3,2},{4,5},{5,4},{6,7},{7,6},{8,9},{9,8},{10,11... | collective-permute-start | bytes 1572872 | tf_op jit(solution)/shard_map/ppermute | solution.py:25
  153.3 3.0 %collective-permute-start.21 = (bf16[256,1024]{1,0:T(8,128)(2,1)}, bf16[256,1024]{1,0:T(8,128)(2,1)}, u32[]{:S(2)}, u32[]{:S(2)}) collective-permute-start(bf16[256,1024]{1,0:T(8,128)(2,1)} %collective-permute-done.20.refs_0_), channel_id=1, source_target_pairs={{0,1},{1,0},{2,3},{3,2},{4,5},{5,4},{6,7},{7,6},{8,9},{9,8},{10,11... | collective-permute-start | bytes 1572872 | tf_op jit(solution)/shard_map/ppermute | solution.py:25
  153.4 2.4 %collective-permute-start.27 = (bf16[2,256,256]{2,1,0:T(8,128)(2,1)}, bf16[2,256,256]{2,1,0:T(8,128)(2,1)S(1)}, u32[]{:S(2)}, u32[]{:S(2)}) collective-permute-start(bf16[2,256,256]{2,1,0:T(8,128)(2,1)} %get-tuple-element.150), channel_id=1, source_target_pairs={{0,1},{1,0},{2,3},{3,2},{4,5},{5,4},{6,7},{7,6},{8,9},{9,8},{10,11... | collective-permute-start | bytes 786440 | tf_op jit(solution)/shard_map/ppermute | solution.py:25
  155.8 0.7 copy-start.9
Sparse Core Ops, SparseCore 0:
  10.6 49.9 all-gather.2
  101.4 43.1 reduce-scatter.1

commit v7 on v6

--- a/solution.py
+++ b/solution.py
@@ -32,77 +32,76 @@
         copy.wait()
 
 
-def pack(core, hidden, rows, nz):
+def columns(start, size):
+    return pl.ds(pl.multiple_of(start, size), size)
+
+
+def pack(where, hidden, rows, nz):
     tokens = hidden.shape[0]
     half = rows // 2
-    group, blocks = 8, nz * 2
-
-    def kernel(core_ref, hidden_ref, group_ref, other_ref, sem):
+    chips, blocks = ((0, 0), (0, 1), (1, 0), (1, 1)), nz * 2
+
+    def kernel(where_ref, hidden_ref, *refs):
+        group_refs, other_ref, sem = refs[:4], refs[4], refs[5]
+        c, x, r = where_ref[0], where_ref[1], where_ref[2]
         copies = []
-        for d in range(group):
-            for k in range(nz):
-                start = (k * 4 + d % 4) * rows + (d // 4) * half
-                copies.append(
-                    pltpu.make_async_copy(
-                        hidden_ref.at[:, pl.ds(start, half)],
-                        group_ref.at[d, :, pl.ds(k * half, half)],
-                        sem.at[len(copies)],
+        for ref, (dr, dx) in zip(group_refs, chips):
+            for dc in range(2):
+                for k in range(nz):
+                    start = (k * 4 + (x ^ dx) * 2 + (c ^ dc)) * rows + (r ^ dr) * half
+                    copies.append(
+                        pltpu.make_async_copy(
+                            hidden_ref.at[:, columns(start, half)],
+                            ref.at[dc, :, pl.ds(k * half, half)],
+                            sem.at[len(copies)],
+                        )
                     )
-                )
         for b in range(blocks):
-            start = pl.multiple_of((b * 2 + 1 - core_ref[0]) * rows, rows)
-            copies.append(
-                pltpu.make_async_copy(
-                    hidden_ref.at[:, pl.ds(start, rows)], other_ref.at[b], sem.at[len(copies)]
-                )
-            )
+            source = hidden_ref.at[:, columns((b * 2 + 1 - c) * rows, rows)]
+            copies.append(pltpu.make_async_copy(source, other_ref.at[b], sem.at[len(copies)]))
         run(copies)
 
     return pl.pallas_call(
         kernel,
-        out_shape=[
-            jax.ShapeDtypeStruct((group, tokens, nz * half), BF16),
-            jax.ShapeDtypeStruct((blocks, tokens, rows), BF16),
-        ],
+        out_shape=[jax.ShapeDtypeStruct((2, tokens, nz * half), BF16)] * 4
+        + [jax.ShapeDtypeStruct((blocks, tokens, rows), BF16)],
         in_specs=[SMEM, ANY],
-        out_specs=[VMEM, VMEM],
-        scratch_shapes=[pltpu.SemaphoreType.DMA((group * nz + blocks,))],
+        out_specs=[VMEM] * 5,
+        scratch_shapes=[pltpu.SemaphoreType.DMA((8 * nz + blocks,))],
         compiler_params=PARAMS,
         name="pack",
-    )(core, hidden)
-
-
-def weight_terms(slots, swapped, cotangents, tiles, state):
-    sources, tokens, width = swapped.shape
+    )(where, hidden)
+
+
+def weight_terms(sources, cotangents):
+    tokens, width = sources[0].shape[1:]
     features = cotangents[0].shape[1]
-    count = len(tiles)
-    tile = width // 4
-
-    def kernel(slots_ref, swapped_ref, *refs):
-        cots_ref, refs = refs[:4], refs[4 + len(state) :]
+    total, count = len(sources), 4
+    tile = width // count
+
+    def kernel(*refs):
+        source_refs, cots_ref, refs = refs[:total], refs[total : total + 4], refs[total + 4 :]
         out_ref, lhs, rhs, out, sem, out_sem = refs
         copies = []
-        for s in range(sources):
-            place = pl.ds(pl.multiple_of(slots_ref[s] * tokens, tokens), tokens)
+        for s in range(total):
+            place = pl.ds(s * tokens, tokens)
             source = cots_ref[s // 4].at[pl.ds(s % 4 * tokens, tokens)] if s % 4 < 3 else cots_ref[2 + s // 4]
             copies.append(pltpu.make_async_copy(source, rhs.at[place], sem.at[count, s]))
-        for i, t in enumerate(tiles):
-            at = pl.ds(t * tile, tile)
-            for s in range(sources):
-                place = pl.ds(s * tokens, tokens)
-                copies.append(
-                    pltpu.make_async_copy(swapped_ref.at[s, :, at], lhs.at[i, place], sem.at[i, s])
-                )
+        for i in range(count):
+            at = pl.ds(i * tile, tile)
+            for s in range(total):
+                target = lhs.at[i, pl.ds(s * tokens, tokens)]
+                copies.append(pltpu.make_async_copy(source_refs[s].at[s // 4, :, at], target, sem.at[i, s]))
         for copy in copies:
             copy.start()
         stores = []
-        for i, t in enumerate(tiles):
-            for copy in copies[(i + 1 if i else 0) * sources : (i + 2) * sources]:
+        for i in range(count):
+            for copy in copies[(i + 1 if i else 0) * total : (i + 2) * total]:
                 copy.wait()
             out[i] = lax.dot_general(
                 lhs[i], rhs[...], (((0,), (0,)), ((), ())), preferred_element_type=F32
             ).astype(BF16)
-            target = out_ref.at[pl.ds(t * tile, tile)]
+            target = out_ref.at[pl.ds(i * tile, tile)]
             stores.append(pltpu.make_async_copy(out.at[i], target, out_sem.at[i]))
             stores[-1].start()
         for copy in stores:
@@ -111,20 +110,19 @@
     return pl.pallas_call(
         kernel,
         out_shape=jax.ShapeDtypeStruct((width, features), BF16),
-        in_specs=[SMEM] + [ANY] * (5 + len(state)),
+        in_specs=[ANY] * (total + 4),
         out_specs=ANY,
-        input_output_aliases={6: 0} if state else {},
         scratch_shapes=[
-            pltpu.VMEM((count, sources * tokens, tile), BF16),
-            pltpu.VMEM((sources * tokens, features), BF16),
+            pltpu.VMEM((count, total * tokens, tile), BF16),
+            pltpu.VMEM((total * tokens, features), BF16),
             pltpu.VMEM((count, tile, features), BF16),
-            pltpu.SemaphoreType.DMA((count + 1, sources)),
+            pltpu.SemaphoreType.DMA((count + 1, total)),
             pltpu.SemaphoreType.DMA((count,)),
         ],
         cost_estimate=CHEAP,
         compiler_params=PARAMS,
         name="weight_terms",
-    )(slots, swapped, *cotangents, *state)
+    )(*sources, *cotangents)
 
 
 def consume(where, scale, hidden, other, cotangents, units, state, arrived, last=False):
@@ -392,11 +390,14 @@
     rest1, rest2 = swap(rest0, "z", 1), swap(rest0, "z", 2)
 
     cots = [swap(cotangent, "x"), swap(cotangent, "replica")]
-    for_group, for_other = pack(where, hidden, rows, nz)
-    for_group, *cots = lax.optimization_barrier((for_group, *cots))
-    swapped = lax.all_to_all(for_group, ("replica", "x", "core"), 0, 0, tiled=True)
+    here, for_x, for_y, for_xy, for_other = pack(where, hidden, rows, nz)
+    for_xy, for_y, *cots = lax.optimization_barrier((for_xy, for_y, *cots))
+    via_x, from_y = swap(for_xy, "x"), swap(for_y, "replica")
+    via_x, from_y, for_x = lax.optimization_barrier((via_x, from_y, for_x))
+    from_x, from_xy = swap(for_x, "x"), swap(via_x, "replica")
     cut = tokens // 2
-    diagonal = [swap(cots[1][:cut], "x"), swap(cots[0][cut:], "replica")]
+    after_x, after_y, rest1 = lax.optimization_barrier((cots[0], cots[1], rest1))
+    diagonal = [swap(after_y[:cut], "x"), swap(after_x[cut:], "replica")]
     peaks = jnp.max(jnp.abs(key_weight), axis=0, keepdims=True)
     peaks = jnp.broadcast_to(peaks, (16, peaks.shape[1]))
     for k in (1, 2):
@@ -407,10 +408,6 @@
     rest1, rest2, *diagonal = lax.optimization_barrier((rest1, rest2, *diagonal))
     diagonal = jnp.concatenate(diagonal, axis=0)
     diagonal = [diagonal, swap(diagonal, "core")]
-    slots = [
-        ((r ^ dr) * 2 + (x ^ dx)) * 2 + (c ^ dc) for dc in (0, 1) for dr in (0, 1) for dx in (0, 1)
-    ]
-    slots = jnp.stack(slots).astype(jnp.int32)
     other = swap(for_other, "core")
 
     parts = [jnp.concatenate([own, peaks])]
@@ -418,8 +415,10 @@
     cots[1], *parts = lax.optimization_barrier((cots[1], *parts))
     side0 = swap(parts[0], "x")
     rest3 = swap(jnp.concatenate([parts[3], peaks]), "replica")
-    swapped, other = lax.optimization_barrier((swapped, other))
-    term = weight_terms(slots, swapped, cots + diagonal, (0, 1, 2, 3), [])
+    sources = [here, from_x, from_y, from_xy]
+    sources += [swap(source, "core") for source in sources]
+    other, *sources = lax.optimization_barrier((other, *sources))
+    term = weight_terms(sources, cots + diagonal)
     stage = functools.partial(consume, where, scale, hidden, other, [cotangent, cots[1]])
 
     def codes_of(units):

time: 172 us -> 188 us (1.093)
  waiting for transfers between devices: 53.1 us -> 69.8 us
    ppermute x29 -> x37, waiting for transfers between devices: 37.1 us -> 63.5 us  [swap(): return lax.ppermute(block, axis, [(i, i ^ mask) for i in range(size)])]
    all_gather x1, waiting for transfers between devices: 11.2 us -> 3.89 us  [body(): mine = lax.all_gather(own, 'z', axis=0)]
    all_to_all x1 -> x0, starting transfers between devices: 4.69 us -> none  [body(): lax.all_to_all(for_group, ('replica', 'x', 'core'), 0, 0, tiled=True)]
    ppermute x29 -> x37, starting transfers between devices: 25.7 us -> 30 us  [swap(): return lax.ppermute(block, axis, [(i, i ^ mask) for i in range(size)])]
    reduce_scatter x1, waiting for transfers between devices: 4.72 us -> 2.36 us  [body(): total = lax.psum_scatter(term, 'z', scatter_dimension=0, tiled=True)]
  transfers between devices with their start and end apart: 32 -> 39, of which waited for: 13 -> 16; matrix products, arithmetic and copies ran while one was open for 8% -> 8% of each run, Pallas kernels for 29% -> 27%
where the time goes in v7:
time: 188 us; the launch traced here: 187 us
  waiting for transfers between devices  69.8 us (37%)
  Pallas kernels  52.2 us (28%)
  starting transfers between devices  30.1 us (16%)
  between operations  16.9 us (9%)
  other arithmetic  11.1 us (6%)
  local copies, waits for them, and re-layouts  7.4 us (4%)
    ppermute x37, waiting for transfers between devices, swap(): return lax.ppermute(block, axis, [(i, i ^ mask) for i in range(size)])  63.5 us
    ppermute x37, starting transfers between devices, swap(): return lax.ppermute(block, axis, [(i, i ^ mask) for i in range(size)])  30 us
    pallas_call x4, Pallas kernels, consume(): pl.pallas_call(kernel, out_shape=[sums, jax.ShapeDtypeStruct(sums.shape,...  29.8 us
    pallas_call x1, Pallas kernels, weight_terms(): pl.pallas_call(kernel, out_shape=jax.ShapeDtypeStruct((width, features),...  8.78 us
    pallas_call x1, Pallas kernels, pack(): pl.pallas_call(kernel, out_shape=[jax.ShapeDtypeStruct((2, tokens, nz * h...  6.67 us
    pallas_call x1, Pallas kernels, finish(): pl.pallas_call(kernel, out_shape=[jax.ShapeDtypeStruct(gradient.shape, BF...  4.61 us
    all_gather x1, waiting for transfers between devices, body(): mine = lax.all_gather(own, 'z', axis=0)  3.89 us
  transfers between devices with their start and end apart: 39, of which 16 were waited for; matrix products, arithmetic and copies ran while one was open for 8% of the time, Pallas kernels for 27%

profile of v7, /device:TPU:0, one launch (start us, length us, event | category | flops | bytes accessed | tf_op | source)
XLA Modules:
  0.0 187.4 jit_solution(2933850443110674826)
XLA Ops:
  8.0 2.4 %clamp_convert_fusion = (bf16[256,1024]{1,0:T(8,128)(2,1)}, bf16[256,1024]{1,0:T(8,128)(2,1)}) fusion(bf16[512,1024]{1,0:T(8,128)(2,1)} %param.5, s32[]{:T(128)S(6)} %select_n.17, f32[]{:T(128)S(6)} %div.11, s32[]{:T(128)S(6)} %select_n.16), kind=kLoop, calls=%fused_computation.3 | loop fusion | flops 2097152 | bytes 2097164 | tf_op jit(solution)/shard_map/convert_element_type | solution.py:20
  10.6 3.0 %collective-permute-start.1 = (bf16[256,1024]{1,0:T(8,128)(2,1)S(1)}, bf16[256,1024]{1,0:T(8,128)(2,1)}, u32[]{:S(2)}, u32[]{:S(2)}) collective-permute-start(bf16[256,1024]{1,0:T(8,128)(2,1)S(1)} %copy-done.1), channel_id=1, source_target_pairs={{0,2},{2,0},{1,3},{3,1},{4,6},{6,4},{5,7},{7,5},{8,10},{10,8},{9,1... | collective-permute-start | bytes 1572872 | tf_op jit(solution)/shard_map/ppermute | solution.py:25
  13.6 1.5 collective-permute-start.2
  15.1 0.1 abs_reduce_fusion
  15.2 1.6 collective-permute-start.11
  16.9 2.3 %collective-permute-done.11 = bf16[16,1024]{1,0:T(8,128)(2,1)S(1)} collective-permute-done((bf16[16,1024]{1,0:T(8,128)(2,1)S(1)}, bf16[16,1024]{1,0:T(8,128)(2,1)S(1)}, u32[]{:S(2)}, u32[]{:S(2)}) %collective-permute-start.11) | collective-permute-done | bytes 32800 | tf_op jit(solution)/shard_map/ppermute | solution.py:25
  19.2 2.6 %collective-permute-start.12 = (bf16[16,1024]{1,0:T(8,128)(2,1)S(1)}, bf16[16,1024]{1,0:T(8,128)(2,1)S(1)}, u32[]{:S(2)}, u32[]{:S(2)}) collective-permute-start(bf16[16,1024]{1,0:T(8,128)(2,1)S(1)} %broadcast_maximum_fusion), channel_id=1, source_target_pairs={{0,8},{4,12},{8,0},{12,4},{1,9},{5,13},{9,1},{13,5},{2,10},{6,14},... | collective-permute-start | bytes 98312 | tf_op jit(solution)/shard_map/ppermute | solution.py:25
  21.8 0.7 pad_add_fusion.where_ref
  22.5 6.7 %pack.1 = (bf16[2,256,1024]{2,1,0:T(8,128)(2,1)}, bf16[2,256,1024]{2,1,0:T(8,128)(2,1)}, bf16[2,256,1024]{2,1,0:T(8,128)(2,1)}, bf16[2,256,1024]{2,1,0:T(8,128)(2,1)}, bf16[8,256,512]{2,1,0:T(8,128)(2,1)}) custom-call(s32[4]{0:T(128)} %pad_add_fusion.where_ref, bf16[256,8192]{1,0:T(8,128)(2,1)} %hidden_ref.5), custom_call_target="tpu_custom_call" | custom-call | tf_op jit(solution)/shard_map/pack/pallas_call | solution.py:64
  29.2 0.6 collective-permute-start.3
  29.8 0.7 collective-permute-start.4
  30.5 2.6 %pad_maximum_fusion.refs_8_ = bf16[768,1024]{1,0:T(8,128)(2,1)} fusion(bf16[256,1024]{1,0:T(8,128)(2,1)} %collective-permute-done.2, bf16[256,1024]{1,0:T(8,128)(2,1)} %collective-permute-done.1, bf16[256,1024]{1,0:T(8,128)(2,1)S(1)} %copy-done.1), kind=kLoop, calls=%fused_computation | loop fusion | flops 4718592 | bytes 3145728 | tf_op jit(solution)/shard_map/concatenate | solution.py:405
  33.1 19.9 %collective-permute-done.3 = bf16[2,256,1024]{2,1,0:T(8,128)(2,1)} collective-permute-done((bf16[2,256,1024]{2,1,0:T(8,128)(2,1)}, bf16[2,256,1024]{2,1,0:T(8,128)(2,1)}, u32[]{:S(2)}, u32[]{:S(2)}) %collective-permute-start.3) | collective-permute-done | bytes 1048608 | tf_op jit(solution)/shard_map/ppermute | solution.py:25
  53.0 0.4 collective-permute-done.4.refs_2_
  53.5 0.3 collective-permute-start.6
  53.8 1.7 collective-permute-start.5
  55.5 3.9 %all-gather.3.cloned.1.call-done = bf16[1024,1024]{1,0:T(8,128)(2,1)} async-done(((bf16[256,1024]{1,0:T(8,128)(2,1)}), bf16[1024,1024]{1,0:T(8,128)(2,1)}) %all-gather.3.cloned.1.call-update) | async-done | bytes 2097168 | tf_op jit(solution)/shard_map/all_gather | solution.py:388
  59.4 2.3 %collective-permute-start.15 = (bf16[256,1024]{1,0:T(8,128)(2,1)}, bf16[256,1024]{1,0:T(8,128)(2,1)}, u32[]{:S(2)}, u32[]{:S(2)}) collective-permute-start(bf16[256,1024]{1,0:T(8,128)(2,1)} %get-tuple-element.124.refs_3_), channel_id=1, source_target_pairs={{0,8},{4,12},{8,0},{12,4},{1,9},{5,13},{9,1},{13,5},{2,10},{6,14},... | collective-permute-start | bytes 1572872 | tf_op jit(solution)/shard_map/ppermute | solution.py:25
  61.7 14.6 %collective-permute-done.6.refs_3_ = bf16[2,256,1024]{2,1,0:T(8,128)(2,1)} collective-permute-done((bf16[2,256,1024]{2,1,0:T(8,128)(2,1)}, bf16[2,256,1024]{2,1,0:T(8,128)(2,1)}, u32[]{:S(2)}, u32[]{:S(2)}) %collective-permute-start.6) | collective-permute-done | bytes 1048608 | tf_op jit(solution)/shard_map/ppermute | solution.py:25
  76.2 7.8 %collective-permute-done.14.refs_5_ = bf16[256,1024]{1,0:T(8,128)(2,1)} collective-permute-done((bf16[256,1024]{1,0:T(8,128)(2,1)}, bf16[256,1024]{1,0:T(8,128)(2,1)}, u32[]{:S(2)}, u32[]{:S(2)}) %collective-permute-start.14) | collective-permute-done | bytes 524320 | tf_op jit(solution)/shard_map/ppermute | solution.py:25
  84.0 1.0 slice.12
  85.0 1.0 slice.13
  86.0 1.6 collective-permute-start.16
  87.6 1.4 collective-permute-start.17
  89.0 5.7 %collective-permute-done.16 = bf16[128,1024]{1,0:T(8,128)(2,1)S(1)} collective-permute-done((bf16[128,1024]{1,0:T(8,128)(2,1)S(1)}, bf16[128,1024]{1,0:T(8,128)(2,1)S(1)}, u32[]{:S(2)}, u32[]{:S(2)}) %collective-permute-start.16) | collective-permute-done | bytes 262176 | tf_op jit(solution)/shard_map/ppermute | solution.py:25
  94.8 1.3 collective-permute-done.17
  96.1 0.8 pad_maximum_fusion.2
  96.9 2.6 %dynamic-slice_bitcast_fusion = (bf16[256,1024]{1,0:T(8,128)(2,1)}, bf16[256,1024]{1,0:T(8,128)(2,1)}, bf16[256,1024]{1,0:T(8,128)(2,1)}) fusion(bf16[4,256,1024]{2,1,0:T(8,128)(2,1)} %bitcast.17, s32[]{:T(128)S(6)} %select_n.20, s32[]{:T(128)S(6)} %select_n.19, s32[]{:T(128)S(6)} %select_n.18), kind=kLoop, calls=%fused_computation.7 | loop fusion | bytes 3145740 | tf_op jit(solution)/shard_map/jit(dynamic_index_in_dim)/squeeze | solution.py:414
  99.5 1.9 %pad_maximum_fusion.1 = bf16[272,1024]{1,0:T(8,128)(2,1)} fusion(bf16[16,1024]{1,0:T(8,128)(2,1)S(1)} %fusion, bf16[256,1024]{1,0:T(8,128)(2,1)} %get-tuple-element.171), kind=kLoop, calls=%fused_computation.5 | loop fusion | flops 1114112 | bytes 1114112 | tf_op jit(solution)/shard_map/concatenate | solution.py:417
  101.4 1.5 collective-permute-start.20
  102.9 0.8 collective-permute-start.19
  103.7 0.1 collective-permute-start.18
  103.8 2.0 %collective-permute-done.18.refs_11_ = bf16[256,1024]{1,0:T(8,128)(2,1)} collective-permute-done((bf16[256,1024]{1,0:T(8,128)(2,1)S(1)}, bf16[256,1024]{1,0:T(8,128)(2,1)}, u32[]{:S(2)}, u32[]{:S(2)}) %collective-permute-start.18) | collective-permute-done | bytes 524320 | tf_op jit(solution)/shard_map/ppermute | solution.py:25
  105.8 8.8 %weight_terms.1 = bf16[1024,1024]{1,0:T(8,128)(2,1)} custom-call(bf16[2,256,1024]{2,1,0:T(8,128)(2,1)} %get-tuple-element.108.refs_0_, bf16[2,256,1024]{2,1,0:T(8,128)(2,1)} %collective-permute-done.5.refs_1_, bf16[2,256,1024]{2,1,0:T(8,128)(2,1)} %collective-permute-done.4.refs_2_, bf16[2,256,1024]{2,1,0:T(8,128)(2,1)} %collective-permute-done.6.refs_3_, ...), custom_call_target="tpu_custom_call" | custom-call | flops 1 | bytes 1 | tf_op jit(solution)/shard_map/weight_terms/pallas_call | solution.py:110
  114.6 2.2 %collective-permute-done.20 = bf16[272,1024]{1,0:T(8,128)(2,1)} collective-permute-done((bf16[272,1024]{1,0:T(8,128)(2,1)}, bf16[272,1024]{1,0:T(8,128)(2,1)}, u32[]{:S(2)}, u32[]{:S(2)}) %collective-permute-start.20) | collective-permute-done | bytes 557088 | tf_op jit(solution)/shard_map/ppermute | solution.py:25
  116.8 1.1 collective-permute-done.19.refs_2_
  118.0 0.7 collective-permute-start.23
  118.7 0.5 collective-permute-start.22
  119.1 0.8 slice_maximum_fusion
  119.9 9.4 %consume.4 = (f32[256,1024]{1,0:T(8,128)}, f32[256,1024]{1,0:T(8,128)}, bf16[256,8192]{1,0:T(8,128)(2,1)}, bf16[4,256,256]{2,1,0:T(8,128)(2,1)}, bf16[1,256,256]{2,1,0:T(8,128)(2,1)}) custom-call(s32[4]{0:T(128)} %pad_add_fusion.where_ref, f32[1]{0:T(128)} %bitcast.5.scale_ref, bf16[256,8192]{1,0:T(8,128)(2,1)} %hidden_ref.5, ...), custom_call_target="tpu_custom_call" | custom-call | flops 1 | bytes 1 | tf_op jit(solution)/shard_map/consume/pallas_call | solution.py:233
  129.3 1.7 collective-permute-start.21
  131.0 0.6 maximum_reduce_fusion
  132.3 1.5 collective-permute-start.25
  133.7 0.5 collective-permute-start.27
  134.2 1.9 slice.14.refs_3_
  136.1 7.5 %consume.5 = (f32[256,1024]{1,0:T(8,128)}, f32[256,1024]{1,0:T(8,128)}, bf16[256,8192]{1,0:T(8,128)(2,1)}, bf16[4,256,256]{2,1,0:T(8,128)(2,1)}) custom-call(s32[4]{0:T(128)} %pad_add_fusion.where_ref, f32[1]{0:T(128)} %bitcast.5.scale_ref, bf16[256,8192]{1,0:T(8,128)(2,1)} %hidden_ref.5, ...), custom_call_target="tpu_custom_call", output_to_operand_aliasing={{0}: (10, {}), {2}: (12, {}), {1}: (11, {})} | custom-call | flops 1 | bytes 1 | tf_op jit(solution)/shard_map/consume/pallas_call | solution.py:233
  143.6 0.7 collective-permute-start.30
  144.4 2.3 %collective-permute-done.25.refs_4_ = bf16[256,1024]{1,0:T(8,128)(2,1)} collective-permute-done((bf16[256,1024]{1,0:T(8,128)(2,1)}, bf16[256,1024]{1,0:T(8,128)(2,1)}, u32[]{:S(2)}, u32[]{:S(2)}) %collective-permute-start.25) | collective-permute-done | bytes 524320 | tf_op jit(solution)/shard_map/ppermute | solution.py:25
  146.6 1.4 collective-permute-start.31
  148.1 0.6 copy-done.8
  148.7 7.6 %consume.6 = (f32[256,1024]{1,0:T(8,128)}, f32[256,1024]{1,0:T(8,128)}, bf16[256,8192]{1,0:T(8,128)(2,1)}, bf16[4,256,256]{2,1,0:T(8,128)(2,1)}) custom-call(s32[4]{0:T(128)} %pad_add_fusion.where_ref, f32[1]{0:T(128)} %bitcast.5.scale_ref, bf16[256,8192]{1,0:T(8,128)(2,1)} %hidden_ref.5, ...), custom_call_target="tpu_custom_call", output_to_operand_aliasing={{0}: (10, {}), {2}: (12, {}), {1}: (11, {})} | custom-call | flops 1 | bytes 1 | tf_op jit(solution)/shard_map/consume/pallas_call | solution.py:233
  156.4 0.6 collective-permute-start.28
  157.0 2.4 %reduce-scatter.2.cloned.1.call-done = bf16[256,1024]{1,0:T(8,128)(2,1)} async-done(((bf16[1024,1024]{1,0:T(8,128)(2,1)}), bf16[256,1024]{1,0:T(8,128)(2,1)}) %reduce-scatter.2.cloned.1.call-update) | async-done | bytes 524304 | tf_op jit(solution)/shard_map/reduce_scatter | solution.py:429
  159.4 1.1 multiply_convert_fusion
  160.6 1.6 collective-permute-start.36
  162.1 5.4 %consume.7 = (f32[256,1024]{1,0:T(8,128)}, bf16[256,1024]{1,0:T(8,128)(2,1)}, bf16[256,8192]{1,0:T(8,128)(2,1)}, bf16[2,256,256]{2,1,0:T(8,128)(2,1)}) custom-call(s32[4]{0:T(128)} %pad_add_fusion.where_ref, f32[1]{0:T(128)} %bitcast.5.scale_ref, bf16[256,8192]{1,0:T(8,128)(2,1)} %hidden_ref.5, ...), custom_call_target="tpu_custom_call", output_to_operand_aliasing={{0}: (8, {}), {2}: (10, {})} | custom-call | flops 1 | bytes 1 | tf_op jit(solution)/shard_map/consume/pallas_call | solution.py:233
  167.5 0.6 collective-permute-start.33
  168.1 1.6 collective-permute-done.28.refs_0_
  169.6 0.5 collective-permute-start.35
  170.2 1.6 collective-permute-done.35.refs_5_
  171.8 0.5 collective-permute-done.29.refs_1_
  172.3 0.3 copy-done.7
  172.5 4.6 %finish.1 = (bf16[256,8192]{1,0:T(8,128)(2,1)}, bf16[256,1024]{1,0:T(8,128)(2,1)}) custom-call(s32[4]{0:T(128)} %pad_add_fusion.where_ref, f32[1]{0:T(128)} %bitcast.5.scale_ref, bf16[256,8192]{1,0:T(8,128)(2,1)} %hidden_ref.5, bf16[256,1024]{1,0:T(8,128)(2,1)} %cot_ref.1, ...), custom_call_target="tpu_custom_call", output_to_operand_aliasing={{0}: (10, {})} | custom-call | flops 1 | bytes 1 | tf_op jit(solution)/shard_map/finish/pallas_call | solution.py:328
  177.2 2.3 %join.1 = bf16[512,1024]{1,0:T(8,128)(2,1)} custom-call(s32[4]{0:T(128)} %pad_add_fusion.where_ref, bf16[272,1024]{1,0:T(8,128)(2,1)} %copy-done.4, bf16[272,1024]{1,0:T(8,128)(2,1)} %collective-permute-done.36.theirs_ref), custom_call_target="tpu_custom_call" | custom-call | tf_op jit(solution)/shard_map/join/pallas_call | solution.py:363
  (61 shorter events, 0.3 us)
Async XLA Ops:
  7.2 7.9 %copy-start.3 = (bf16[512,1024]{1,0:T(8,128)(2,1)S(1)}, bf16[512,1024]{1,0:T(8,128)(2,1)}, u32[]{:S(2)}) copy-start(bf16[512,1024]{1,0:T(8,128)(2,1)} %param.5) | copy-start | bytes 3145732
  7.2 3.4 %copy-start.1 = (bf16[256,1024]{1,0:T(8,128)(2,1)S(1)}, bf16[256,1024]{1,0:T(8,128)(2,1)}, u32[]{:S(2)}) copy-start(bf16[256,1024]{1,0:T(8,128)(2,1)} %cot_ref.1) | copy-start | bytes 1572868
  7.2 52.2 %all-gather.3.cloned.1.call-start = ((), (), s32[]{:S(2)}) async-start(), calls=%async_computation.2 | async-start | bytes 2621440 | tf_op jit(solution)/shard_map/all_gather | solution.py:388
  10.5 148.9 %reduce-scatter.2.cloned.1.call-start = ((), (), s32[]{:S(2)}) async-start(), calls=%async_computation.1 | async-start | bytes 2621440 | tf_op jit(solution)/shard_map/reduce_scatter | solution.py:429
  10.6 18.6 %collective-permute-start.1 = (bf16[256,1024]{1,0:T(8,128)(2,1)S(1)}, bf16[256,1024]{1,0:T(8,128)(2,1)}, u32[]{:S(2)}, u32[]{:S(2)}) collective-permute-start(bf16[256,1024]{1,0:T(8,128)(2,1)S(1)} %copy-done.1), channel_id=1, source_target_pairs={{0,2},{2,0},{1,3},{3,1},{4,6},{6,4},{5,7},{7,5},{8,10},{10,8},{9,1... | collective-permute-start | bytes 1572872 | tf_op jit(solution)/shard_map/ppermute | solution.py:25
  13.6 15.6 %collective-permute-start.2 = (bf16[256,1024]{1,0:T(8,128)(2,1)S(1)}, bf16[256,1024]{1,0:T(8,128)(2,1)}, u32[]{:S(2)}, u32[]{:S(2)}) collective-permute-start(bf16[256,1024]{1,0:T(8,128)(2,1)S(1)} %copy-done.1), channel_id=1, source_target_pairs={{0,16},{16,0},{1,17},{17,1},{2,18},{18,2},{3,19},{19,3},{4,20},{20... | collective-permute-start | bytes 1572872 | tf_op jit(solution)/shard_map/ppermute | solution.py:25
  15.2 4.0 %collective-permute-start.11 = (bf16[16,1024]{1,0:T(8,128)(2,1)S(1)}, bf16[16,1024]{1,0:T(8,128)(2,1)S(1)}, u32[]{:S(2)}, u32[]{:S(2)}) collective-permute-start(bf16[16,1024]{1,0:T(8,128)(2,1)S(1)} %broadcast_in_dim.2), channel_id=1, source_target_pairs={{0,4},{4,0},{8,12},{12,8},{1,5},{5,1},{9,13},{13,9},{2,6},{6,2},{1... | collective-permute-start | bytes 98312 | tf_op jit(solution)/shard_map/ppermute | solution.py:25
  19.2 11.2 %collective-permute-start.12 = (bf16[16,1024]{1,0:T(8,128)(2,1)S(1)}, bf16[16,1024]{1,0:T(8,128)(2,1)S(1)}, u32[]{:S(2)}, u32[]{:S(2)}) collective-permute-start(bf16[16,1024]{1,0:T(8,128)(2,1)S(1)} %broadcast_maximum_fusion), channel_id=1, source_target_pairs={{0,8},{4,12},{8,0},{12,4},{1,9},{5,13},{9,1},{13,5},{2,10},{6,14},... | collective-permute-start | bytes 98312 | tf_op jit(solution)/shard_map/ppermute | solution.py:25
  29.2 23.9 %collective-permute-start.3 = (bf16[2,256,1024]{2,1,0:T(8,128)(2,1)}, bf16[2,256,1024]{2,1,0:T(8,128)(2,1)}, u32[]{:S(2)}, u32[]{:S(2)}) collective-permute-start(bf16[2,256,1024]{2,1,0:T(8,128)(2,1)} %get-tuple-element.102), channel_id=1, source_target_pairs={{0,2},{2,0},{1,3},{3,1},{4,6},{6,4},{5,7},{7,5},{8,10},{10,8},{9,1... | collective-permute-start | bytes 3145736 | tf_op jit(solution)/shard_map/ppermute | solution.py:25
  29.8 23.7 %collective-permute-start.4 = (bf16[2,256,1024]{2,1,0:T(8,128)(2,1)}, bf16[2,256,1024]{2,1,0:T(8,128)(2,1)}, u32[]{:S(2)}, u32[]{:S(2)}) collective-permute-start(bf16[2,256,1024]{2,1,0:T(8,128)(2,1)} %get-tuple-element.103), channel_id=1, source_target_pairs={{0,16},{16,0},{1,17},{17,1},{2,18},{18,2},{3,19},{19,3},{4,20},{20... | collective-permute-start | bytes 3145736 | tf_op jit(solution)/shard_map/ppermute | solution.py:25
  30.5 65.6 %copy-start.2 = (bf16[256,1024]{1,0:T(8,128)(2,1)S(1)}, bf16[256,1024]{1,0:T(8,128)(2,1)}, u32[]{:S(2)}) copy-start(bf16[256,1024]{1,0:T(8,128)(2,1)} %get-tuple-element.119.refs_2_) | copy-start | bytes 1572868
  33.1 26.3 %collective-permute-start.13 = (bf16[768,1024]{1,0:T(8,128)(2,1)}, bf16[768,1024]{1,0:T(8,128)(2,1)S(1)}, u32[]{:S(2)}, u32[]{:S(2)}) collective-permute-start(bf16[768,1024]{1,0:T(8,128)(2,1)} %pad_maximum_fusion.refs_8_), channel_id=1, source_target_pairs={{0,1},{1,0},{2,3},{3,2},{4,5},{5,4},{6,7},{7,6},{8,9},{9,8},{10,11... | collective-permute-start | bytes 4718600 | tf_op jit(solution)/shard_map/ppermute | solution.py:25
  53.5 22.8 %collective-permute-start.6 = (bf16[2,256,1024]{2,1,0:T(8,128)(2,1)}, bf16[2,256,1024]{2,1,0:T(8,128)(2,1)}, u32[]{:S(2)}, u32[]{:S(2)}) collective-permute-start(bf16[2,256,1024]{2,1,0:T(8,128)(2,1)} %collective-permute-done.3), channel_id=1, source_target_pairs={{0,16},{16,0},{1,17},{17,1},{2,18},{18,2},{3,19},{19,3},{4,20},{20... | collective-permute-start | bytes 3145736 | tf_op jit(solution)/shard_map/ppermute | solution.py:25
  53.8 49.1 %collective-permute-start = (bf16[8,256,512]{2,1,0:T(8,128)(2,1)}, bf16[8,256,512]{2,1,0:T(8,128)(2,1)}, u32[]{:S(2)}, u32[]{:S(2)}) collective-permute-start(bf16[8,256,512]{2,1,0:T(8,128)(2,1)} %get-tuple-element.98), channel_id=1, source_target_pairs={{0,1},{1,0},{2,3},{3,2},{4,5},{5,4},{6,7},{7,6},{8,9},{9,8},{10,11... | collective-permute-start | bytes 6291464 | tf_op jit(solution)/shard_map/ppermute | solution.py:25
  53.8 32.2 %collective-permute-start.5 = (bf16[2,256,1024]{2,1,0:T(8,128)(2,1)}, bf16[2,256,1024]{2,1,0:T(8,128)(2,1)}, u32[]{:S(2)}, u32[]{:S(2)}) collective-permute-start(bf16[2,256,1024]{2,1,0:T(8,128)(2,1)} %get-tuple-element.105), channel_id=1, source_target_pairs={{0,2},{2,0},{1,3},{3,1},{4,6},{6,4},{5,7},{7,5},{8,10},{10,8},{9,1... | collective-permute-start | bytes 3145736 | tf_op jit(solution)/shard_map/ppermute | solution.py:25
  59.4 24.7 %collective-permute-start.14 = (bf16[256,1024]{1,0:T(8,128)(2,1)}, bf16[256,1024]{1,0:T(8,128)(2,1)}, u32[]{:S(2)}, u32[]{:S(2)}) collective-permute-start(bf16[256,1024]{1,0:T(8,128)(2,1)} %get-tuple-element.124.refs_3_), channel_id=1, source_target_pairs={{0,4},{4,0},{8,12},{12,8},{1,5},{5,1},{9,13},{13,9},{2,6},{6,2},{1... | collective-permute-start | bytes 1572872 | tf_op jit(solution)/shard_map/ppermute | solution.py:25
  59.4 40.1 %copy-start = (bf16[768,1024]{1,0:T(8,128)(2,1)}, bf16[768,1024]{1,0:T(8,128)(2,1)S(1)}, u32[]{:S(2)}) copy-start(bf16[768,1024]{1,0:T(8,128)(2,1)S(1)} %collective-permute-done.13.refs_9_.refs_1_) | copy-start | bytes 4718596
  59.4 28.3 %collective-permute-start.15 = (bf16[256,1024]{1,0:T(8,128)(2,1)}, bf16[256,1024]{1,0:T(8,128)(2,1)}, u32[]{:S(2)}, u32[]{:S(2)}) collective-permute-start(bf16[256,1024]{1,0:T(8,128)(2,1)} %get-tuple-element.124.refs_3_), channel_id=1, source_target_pairs={{0,8},{4,12},{8,0},{12,4},{1,9},{5,13},{9,1},{13,5},{2,10},{6,14},... | collective-permute-start | bytes 1572872 | tf_op jit(solution)/shard_map/ppermute | solution.py:25
  76.2 25.2 %collective-permute-start.7 = (bf16[2,256,1024]{2,1,0:T(8,128)(2,1)}, bf16[2,256,1024]{2,1,0:T(8,128)(2,1)}, u32[]{:S(2)}, u32[]{:S(2)}) collective-permute-start(bf16[2,256,1024]{2,1,0:T(8,128)(2,1)} %get-tuple-element.108.refs_0_), channel_id=1, source_target_pairs={{0,1},{1,0},{2,3},{3,2},{4,5},{5,4},{6,7},{7,6},{8,9},{9,8},{10,11... | collective-permute-start | bytes 3145736 | tf_op jit(solution)/shard_map/ppermute | solution.py:25
  84.0 19.7 %collective-permute-start.9 = (bf16[2,256,1024]{2,1,0:T(8,128)(2,1)}, bf16[2,256,1024]{2,1,0:T(8,128)(2,1)}, u32[]{:S(2)}, u32[]{:S(2)}) collective-permute-start(bf16[2,256,1024]{2,1,0:T(8,128)(2,1)} %collective-permute-done.4.refs_2_), channel_id=1, source_target_pairs={{0,1},{1,0},{2,3},{3,2},{4,5},{5,4},{6,7},{7,6},{8,9},{9,8},{10,11... | collective-permute-start | bytes 3145736 | tf_op jit(solution)/shard_map/ppermute | solution.py:25
  86.0 8.8 %collective-permute-start.16 = (bf16[128,1024]{1,0:T(8,128)(2,1)S(1)}, bf16[128,1024]{1,0:T(8,128)(2,1)S(1)}, u32[]{:S(2)}, u32[]{:S(2)}) collective-permute-start(bf16[128,1024]{1,0:T(8,128)(2,1)S(1)} %slice.12), channel_id=1, source_target_pairs={{0,2},{2,0},{1,3},{3,1},{4,6},{6,4},{5,7},{7,5},{8,10},{10,8},{9,1... | collective-permute-start | bytes 786440 | tf_op jit(solution)/shard_map/ppermute | solution.py:25
  87.6 8.4 %collective-permute-start.17 = (bf16[128,1024]{1,0:T(8,128)(2,1)S(1)}, bf16[128,1024]{1,0:T(8,128)(2,1)S(1)}, u32[]{:S(2)}, u32[]{:S(2)}) collective-permute-start(bf16[128,1024]{1,0:T(8,128)(2,1)S(1)} %slice.13), channel_id=1, source_target_pairs={{0,16},{16,0},{1,17},{17,1},{2,18},{18,2},{3,19},{19,3},{4,20},{20... | collective-permute-start | bytes 786440 | tf_op jit(solution)/shard_map/ppermute | solution.py:25
  94.8 9.0 %collective-permute-start.10 = (bf16[2,256,1024]{2,1,0:T(8,128)(2,1)}, bf16[2,256,1024]{2,1,0:T(8,128)(2,1)}, u32[]{:S(2)}, u32[]{:S(2)}) collective-permute-start(bf16[2,256,1024]{2,1,0:T(8,128)(2,1)} %collective-permute-done.6.refs_3_), channel_id=1, source_target_pairs={{0,1},{1,0},{2,3},{3,2},{4,5},{5,4},{6,7},{7,6},{8,9},{9,8},{10,11... | collective-permute-start | bytes 3145736 | tf_op jit(solution)/shard_map/ppermute | solution.py:25
  96.1 7.7 %collective-permute-start.8 = (bf16[2,256,1024]{2,1,0:T(8,128)(2,1)}, bf16[2,256,1024]{2,1,0:T(8,128)(2,1)}, u32[]{:S(2)}, u32[]{:S(2)}) collective-permute-start(bf16[2,256,1024]{2,1,0:T(8,128)(2,1)} %collective-permute-done.5.refs_1_), channel_id=1, source_target_pairs={{0,1},{1,0},{2,3},{3,2},{4,5},{5,4},{6,7},{7,6},{8,9},{9,8},{10,11... | collective-permute-start | bytes 3145736 | tf_op jit(solution)/shard_map/ppermute | solution.py:25
  101.4 15.4 %collective-permute-start.20 = (bf16[272,1024]{1,0:T(8,128)(2,1)}, bf16[272,1024]{1,0:T(8,128)(2,1)}, u32[]{:S(2)}, u32[]{:S(2)}) collective-permute-start(bf16[272,1024]{1,0:T(8,128)(2,1)} %pad_maximum_fusion.1), channel_id=1, source_target_pairs={{0,16},{16,0},{1,17},{17,1},{2,18},{18,2},{3,19},{19,3},{4,20},{20... | collective-permute-start | bytes 1671176 | tf_op jit(solution)/shard_map/ppermute | solution.py:25
  102.9 15.1 %collective-permute-start.19 = (bf16[272,1024]{1,0:T(8,128)(2,1)}, bf16[272,1024]{1,0:T(8,128)(2,1)}, u32[]{:S(2)}, u32[]{:S(2)}) collective-permute-start(bf16[272,1024]{1,0:T(8,128)(2,1)} %pad_maximum_fusion.2), channel_id=1, source_target_pairs={{0,2},{2,0},{1,3},{3,1},{4,6},{6,4},{5,7},{7,5},{8,10},{10,8},{9,1... | collective-permute-start | bytes 1671176 | tf_op jit(solution)/shard_map/ppermute | solution.py:25
  103.7 2.1 %copy-start.5 = (bf16[256,1024]{1,0:T(8,128)(2,1)}, bf16[256,1024]{1,0:T(8,128)(2,1)S(1)}, u32[]{:S(2)}) copy-start(bf16[256,1024]{1,0:T(8,128)(2,1)S(1)} %constant_dynamic-update-slice_fusion.refs_10_) | copy-start | bytes 1572868
  103.7 2.1 %collective-permute-start.18 = (bf16[256,1024]{1,0:T(8,128)(2,1)S(1)}, bf16[256,1024]{1,0:T(8,128)(2,1)}, u32[]{:S(2)}, u32[]{:S(2)}) collective-permute-start(bf16[256,1024]{1,0:T(8,128)(2,1)S(1)} %constant_dynamic-update-slice_fusion.refs_10_), channel_id=1, source_target_pairs={{0,1},{1,0},{2,3},{3,2},{4,5},{5,4},{6,7},{7,6},{8,9},{9,8},{10,11... | collective-permute-start | bytes 1572872 | tf_op jit(solution)/shard_map/ppermute | solution.py:25
  118.0 14.2 %collective-permute-start.23 = (bf16[272,1024]{1,0:T(8,128)(2,1)}, bf16[272,1024]{1,0:T(8,128)(2,1)S(1)}, u32[]{:S(2)}, u32[]{:S(2)}) collective-permute-start(bf16[272,1024]{1,0:T(8,128)(2,1)} %collective-permute-done.19.refs_2_), channel_id=1, source_target_pairs={{0,16},{16,0},{1,17},{17,1},{2,18},{18,2},{3,19},{19,3},{4,20},{20... | collective-permute-start | bytes 1671176 | tf_op jit(solution)/shard_map/ppermute | solution.py:25
  118.7 13.6 %collective-permute-start.22 = (bf16[256,1024]{1,0:T(8,128)(2,1)}, bf16[256,1024]{1,0:T(8,128)(2,1)}, u32[]{:S(2)}, u32[]{:S(2)}) collective-permute-start(bf16[256,1024]{1,0:T(8,128)(2,1)} %get-tuple-element.142), channel_id=1, source_target_pairs={{0,2},{2,0},{1,3},{3,1},{4,6},{6,4},{5,7},{7,5},{8,10},{10,8},{9,1... | collective-permute-start | bytes 1572872 | tf_op jit(solution)/shard_map/ppermute | solution.py:25
  119.9 11.1 %collective-permute-start.24 = (bf16[16,1024]{1,0:T(8,128)(2,1)S(1)}, bf16[16,1024]{1,0:T(8,128)(2,1)S(1)}, u32[]{:S(2)}, u32[]{:S(2)}) collective-permute-start(bf16[16,1024]{1,0:T(8,128)(2,1)S(1)} %slice_maximum_fusion), channel_id=1, source_target_pairs={{0,1},{1,0},{2,3},{3,2},{4,5},{5,4},{6,7},{7,6},{8,9},{9,8},{10,11... | collective-permute-start | bytes 98312 | tf_op jit(solution)/shard_map/ppermute | solution.py:25
  129.3 15.1 %collective-permute-start.21 = (bf16[256,1024]{1,0:T(8,128)(2,1)}, bf16[256,1024]{1,0:T(8,128)(2,1)}, u32[]{:S(2)}, u32[]{:S(2)}) collective-permute-start(bf16[256,1024]{1,0:T(8,128)(2,1)} %get-tuple-element.141), channel_id=1, source_target_pairs={{0,2},{2,0},{1,3},{3,1},{4,6},{6,4},{5,7},{7,5},{8,10},{10,8},{9,1... | collective-permute-start | bytes 1572872 | tf_op jit(solution)/shard_map/ppermute | solution.py:25
  132.3 3.9 %copy-start.6 = (bf16[272,1024]{1,0:T(8,128)(2,1)}, bf16[272,1024]{1,0:T(8,128)(2,1)S(1)}, u32[]{:S(2)}) copy-start(bf16[272,1024]{1,0:T(8,128)(2,1)S(1)} %collective-permute-done.23.refs_3_) | copy-start | bytes 1671172
  132.3 14.4 %collective-permute-start.25 = (bf16[256,1024]{1,0:T(8,128)(2,1)}, bf16[256,1024]{1,0:T(8,128)(2,1)}, u32[]{:S(2)}, u32[]{:S(2)}) collective-permute-start(bf16[256,1024]{1,0:T(8,128)(2,1)} %collective-permute-done.22.refs_4_), channel_id=1, source_target_pairs={{0,16},{16,0},{1,17},{17,1},{2,18},{18,2},{3,19},{19,3},{4,20},{20... | collective-permute-start | bytes 1572872 | tf_op jit(solution)/shard_map/ppermute | solution.py:25
  133.7 14.3 %collective-permute-start.26 = (bf16[4,256,256]{2,1,0:T(8,128)(2,1)}, bf16[4,256,256]{2,1,0:T(8,128)(2,1)}, u32[]{:S(2)}, u32[]{:S(2)}) collective-permute-start(bf16[4,256,256]{2,1,0:T(8,128)(2,1)} %get-tuple-element.165), channel_id=1, source_target_pairs={{0,1},{1,0},{2,3},{3,2},{4,5},{5,4},{6,7},{7,6},{8,9},{9,8},{10,11... | collective-permute-start | bytes 1572872 | tf_op jit(solution)/shard_map/ppermute | solution.py:25
  133.7 14.3 %collective-permute-start.27 = (bf16[1,256,256]{2,1,0:T(8,128)(2,1)}, bf16[1,256,256]{2,1,0:T(8,128)(2,1)S(1)}, u32[]{:S(2)}, u32[]{:S(2)}) collective-permute-start(bf16[1,256,256]{2,1,0:T(8,128)(2,1)} %get-tuple-element.166), channel_id=1, source_target_pairs={{0,1},{1,0},{2,3},{3,2},{4,5},{5,4},{6,7},{7,6},{8,9},{9,8},{10,11... | collective-permute-start | bytes 393224 | tf_op jit(solution)/shard_map/ppermute | solution.py:25
  143.6 18.5 %collective-permute-start.30 = (bf16[256,1024]{1,0:T(8,128)(2,1)}, bf16[256,1024]{1,0:T(8,128)(2,1)}, u32[]{:S(2)}, u32[]{:S(2)}) collective-permute-start(bf16[256,1024]{1,0:T(8,128)(2,1)} %get-tuple-element.171), channel_id=1, source_target_pairs={{0,2},{2,0},{1,3},{3,1},{4,6},{6,4},{5,7},{7,5},{8,10},{10,8},{9,1... | collective-permute-start | bytes 1572872 | tf_op jit(solution)/shard_map/ppermute | solution.py:25
  144.4 17.8 %collective-permute-start.32 = (bf16[4,256,256]{2,1,0:T(8,128)(2,1)}, bf16[4,256,256]{2,1,0:T(8,128)(2,1)}, u32[]{:S(2)}, u32[]{:S(2)}) collective-permute-start(bf16[4,256,256]{2,1,0:T(8,128)(2,1)} %get-tuple-element.180), channel_id=1, source_target_pairs={{0,1},{1,0},{2,3},{3,2},{4,5},{5,4},{6,7},{7,6},{8,9},{9,8},{10,11... | collective-permute-start | bytes 1572872 | tf_op jit(solution)/shard_map/ppermute | solution.py:25
  146.6 15.5 %collective-permute-start.31 = (bf16[256,1024]{1,0:T(8,128)(2,1)}, bf16[256,1024]{1,0:T(8,128)(2,1)}, u32[]{:S(2)}, u32[]{:S(2)}) collective-permute-start(bf16[256,1024]{1,0:T(8,128)(2,1)} %collective-permute-done.21.refs_5_), channel_id=1, source_target_pairs={{0,16},{16,0},{1,17},{17,1},{2,18},{18,2},{3,19},{19,3},{4,20},{20... | collective-permute-start | bytes 1572872 | tf_op jit(solution)/shard_map/ppermute | solution.py:25
  148.1 0.7 copy-start.8
  156.4 13.3 %collective-permute-start.28 = (bf16[256,1024]{1,0:T(8,128)(2,1)}, bf16[256,1024]{1,0:T(8,128)(2,1)}, u32[]{:S(2)}, u32[]{:S(2)}) collective-permute-start(bf16[256,1024]{1,0:T(8,128)(2,1)} %slice.14.refs_3_), channel_id=1, source_target_pairs={{0,2},{2,0},{1,3},{3,1},{4,6},{6,4},{5,7},{7,5},{8,10},{10,8},{9,1... | collective-permute-start | bytes 1572872 | tf_op jit(solution)/shard_map/ppermute | solution.py:25
  160.6 7.0 %copy-start.4 = (bf16[272,1024]{1,0:T(8,128)(2,1)}, bf16[272,1024]{1,0:T(8,128)(2,1)S(1)}, u32[]{:S(2)}) copy-start(bf16[272,1024]{1,0:T(8,128)(2,1)S(1)} %pad.4.mine_ref) | copy-start | bytes 1671172
  160.6 16.6 %collective-permute-start.36 = (bf16[272,1024]{1,0:T(8,128)(2,1)S(1)}, bf16[272,1024]{1,0:T(8,128)(2,1)}, u32[]{:S(2)}, u32[]{:S(2)}) collective-permute-start(bf16[272,1024]{1,0:T(8,128)(2,1)S(1)} %pad.4.mine_ref), channel_id=1, source_target_pairs={{0,16},{16,0},{1,17},{17,1},{2,18},{18,2},{3,19},{19,3},{4,20},{20... | collective-permute-start | bytes 1671176 | tf_op jit(solution)/shard_map/ppermute | solution.py:25
  162.1 8.0 %collective-permute-start.34 = (bf16[4,256,256]{2,1,0:T(8,128)(2,1)}, bf16[4,256,256]{2,1,0:T(8,128)(2,1)}, u32[]{:S(2)}, u32[]{:S(2)}) collective-permute-start(bf16[4,256,256]{2,1,0:T(8,128)(2,1)} %get-tuple-element.183), channel_id=1, source_target_pairs={{0,1},{1,0},{2,3},{3,2},{4,5},{5,4},{6,7},{7,6},{8,9},{9,8},{10,11... | collective-permute-start | bytes 1572872 | tf_op jit(solution)/shard_map/ppermute | solution.py:25
  167.5 4.3 %collective-permute-start.33 = (bf16[256,1024]{1,0:T(8,128)(2,1)}, bf16[256,1024]{1,0:T(8,128)(2,1)}, u32[]{:S(2)}, u32[]{:S(2)}) collective-permute-start(bf16[256,1024]{1,0:T(8,128)(2,1)} %get-tuple-element.182), channel_id=1, source_target_pairs={{0,1},{1,0},{2,3},{3,2},{4,5},{5,4},{6,7},{7,6},{8,9},{9,8},{10,11... | collective-permute-start | bytes 1572872 | tf_op jit(solution)/shard_map/ppermute | solution.py:25
  169.6 2.6 %collective-permute-start.29 = (bf16[256,1024]{1,0:T(8,128)(2,1)}, bf16[256,1024]{1,0:T(8,128)(2,1)}, u32[]{:S(2)}, u32[]{:S(2)}) collective-permute-start(bf16[256,1024]{1,0:T(8,128)(2,1)} %collective-permute-done.28.refs_0_), channel_id=1, source_target_pairs={{0,1},{1,0},{2,3},{3,2},{4,5},{5,4},{6,7},{7,6},{8,9},{9,8},{10,11... | collective-permute-start | bytes 1572872 | tf_op jit(solution)/shard_map/ppermute | solution.py:25
  169.6 2.2 %collective-permute-start.35 = (bf16[2,256,256]{2,1,0:T(8,128)(2,1)}, bf16[2,256,256]{2,1,0:T(8,128)(2,1)S(1)}, u32[]{:S(2)}, u32[]{:S(2)}) collective-permute-start(bf16[2,256,256]{2,1,0:T(8,128)(2,1)} %get-tuple-element.184), channel_id=1, source_target_pairs={{0,1},{1,0},{2,3},{3,2},{4,5},{5,4},{6,7},{7,6},{8,9},{9,8},{10,11... | collective-permute-start | bytes 786440 | tf_op jit(solution)/shard_map/ppermute | solution.py:25
  171.8 0.7 copy-start.7
Sparse Core Ops, SparseCore 0:
  10.6 48.6 all-gather.2
  118.1 41.2 reduce-scatter.1

commit v8 on v6

--- a/solution.py
+++ b/solution.py
@@ -455,9 +455,13 @@
 
     rest3, *state = lax.optimization_barrier((rest3, *state))
     other3 = swap(rest3, "x")
-    side3, other2, *state = lax.optimization_barrier((side3, other2, *state))
-    units = [(other2, 0, (2, 1, 1)), (side3, 0, (3, 1, 0))]
-    *state, away = stage(units, state, second, last=True)
+    units = [(side3, 0, (3, 1, 0))]
+    *state, away = stage(units, state, second)
+    late.append(swap(away, "core"))
+    late_units.append(codes_of(units))
+    other2, total, *state = lax.optimization_barrier((other2, total, *state))
+    units = [(other2, 0, (2, 1, 1))]
+    *state, away = stage(units, state, None, last=True)
     late.append(swap(away, "core"))
     late_units.append(codes_of(units))
 

time: 172 us -> 180 us (1.047)
  waiting for transfers between devices: 53.1 us -> 59.4 us
  Pallas kernels: 52.3 us -> 56.8 us
    ppermute x29 -> x30, waiting for transfers between devices: 37.1 us -> 48.1 us  [swap(): return lax.ppermute(block, axis, [(i, i ^ mask) for i in range(size)])]
    reduce_scatter x1, waiting for transfers between devices: 4.72 us -> 0.02 us  [body(): total = lax.psum_scatter(term, 'z', scatter_dimension=0, tiled=True)]
    pallas_call x4 -> x5, Pallas kernels: 29.3 us -> 33.8 us  [consume(): pl.pallas_call(kernel, out_shape=[sums, jax.ShapeDtypeStruct(sums.shape,...]
    ppermute x29 -> x30, starting transfers between devices: 25.7 us -> 24.2 us  [swap(): return lax.ppermute(block, axis, [(i, i ^ mask) for i in range(size)])]
  transfers between devices with their start and end apart: 32 -> 33, of which waited for: 13 -> 14; matrix products, arithmetic and copies ran while one was open for 8% -> 7% of each run, Pallas kernels for 29% -> 30%
where the time goes in v8:
time: 180 us
  waiting for transfers between devices  59.4 us (33%)
  Pallas kernels  56.8 us (32%)
  starting transfers between devices  29 us (16%)
  between operations  16.8 us (9%)
  other arithmetic  9.95 us (6%)
  local copies, waits for them, and re-layouts  7.88 us (4%)
    ppermute x30, waiting for transfers between devices, swap(): return lax.ppermute(block, axis, [(i, i ^ mask) for i in range(size)])  48.1 us
    pallas_call x5, Pallas kernels, consume(): pl.pallas_call(kernel, out_shape=[sums, jax.ShapeDtypeStruct(sums.shape,...  33.8 us
    ppermute x30, starting transfers between devices, swap(): return lax.ppermute(block, axis, [(i, i ^ mask) for i in range(size)])  24.2 us
    all_gather x1, waiting for transfers between devices, body(): mine = lax.all_gather(own, 'z', axis=0)  11.2 us
    pallas_call x1, Pallas kernels, weight_terms(): pl.pallas_call(kernel, out_shape=jax.ShapeDtypeStruct((width, features),...  9.5 us
    pallas_call x1, Pallas kernels, pack(): pl.pallas_call(kernel, out_shape=[jax.ShapeDtypeStruct((group, tokens, nz...  6.65 us
    all_to_all x1, starting transfers between devices, body(): lax.all_to_all(for_group, ('replica', 'x', 'core'), 0, 0, tiled=True)  4.7 us
    pallas_call x1, Pallas kernels, finish(): pl.pallas_call(kernel, out_shape=[jax.ShapeDtypeStruct(gradient.shape, BF...  4.61 us
  transfers between devices with their start and end apart: 33, of which 14 were waited for; matrix products, arithmetic and copies ran while one was open for 7% of the time, Pallas kernels for 30%

profile of v8, /device:TPU:0, one launch (start us, length us, event | category | flops | bytes accessed | tf_op | source)
XLA Modules:
  0.0 179.8 jit_solution(5330474229403507019)
XLA Ops:
  8.0 2.4 %clamp_convert_fusion = (bf16[256,1024]{1,0:T(8,128)(2,1)}, bf16[256,1024]{1,0:T(8,128)(2,1)}) fusion(bf16[512,1024]{1,0:T(8,128)(2,1)} %param.5, s32[]{:T(128)S(6)} %select_n.17, f32[]{:T(128)S(6)} %div.11, s32[]{:T(128)S(6)} %select_n.16), kind=kLoop, calls=%fused_computation.3 | loop fusion | flops 2097152 | bytes 2097164 | tf_op jit(solution)/shard_map/convert_element_type | solution.py:20
  10.4 3.0 %collective-permute-start.1 = (bf16[256,1024]{1,0:T(8,128)(2,1)S(1)}, bf16[256,1024]{1,0:T(8,128)(2,1)}, u32[]{:S(2)}, u32[]{:S(2)}) collective-permute-start(bf16[256,1024]{1,0:T(8,128)(2,1)S(1)} %copy-done.1), channel_id=1, source_target_pairs={{0,16},{16,0},{1,17},{17,1},{2,18},{18,2},{3,19},{19,3},{4,20},{20... | collective-permute-start | bytes 1572872 | tf_op jit(solution)/shard_map/ppermute | solution.py:25
  13.4 1.5 collective-permute-start
  14.9 0.6 pad_add_fusion.core_ref.where_ref
  15.6 6.7 %pack.1 = (bf16[8,256,1024]{2,1,0:T(8,128)(2,1)}, bf16[8,256,512]{2,1,0:T(8,128)(2,1)}) custom-call(s32[4]{0:T(128)} %pad_add_fusion.core_ref.where_ref, bf16[256,8192]{1,0:T(8,128)(2,1)} %hidden_ref.6), custom_call_target="tpu_custom_call" | custom-call | tf_op jit(solution)/shard_map/pack/pallas_call | solution.py:61
  22.2 3.3 %collective-permute-done.1 = bf16[256,1024]{1,0:T(8,128)(2,1)} collective-permute-done((bf16[256,1024]{1,0:T(8,128)(2,1)S(1)}, bf16[256,1024]{1,0:T(8,128)(2,1)}, u32[]{:S(2)}, u32[]{:S(2)}) %collective-permute-start.1) | collective-permute-done | bytes 524320 | tf_op jit(solution)/shard_map/ppermute | solution.py:25
  25.5 1.5 collective-permute-done
  26.9 4.7 %all-to-all-start = ((bf16[8,256,1024]{2,1,0:T(8,128)(2,1)}), bf16[8,256,1024]{2,1,0:T(8,128)(2,1)}, u32[]{:S(2)}, u32[]{:S(2)}) async-start(bf16[8,256,1024]{2,1,0:T(8,128)(2,1)} %get-tuple-element.86), calls=%async_computation | async-start | bytes 8388608 | tf_op jit(solution)/shard_map/all_to_all | solution.py:397
  31.7 0.1 abs_reduce_fusion
  31.8 1.6 collective-permute-start.3
  33.5 5.1 %collective-permute-done.3 = bf16[16,1024]{1,0:T(8,128)(2,1)S(1)} collective-permute-done((bf16[16,1024]{1,0:T(8,128)(2,1)S(1)}, bf16[16,1024]{1,0:T(8,128)(2,1)S(1)}, u32[]{:S(2)}, u32[]{:S(2)}) %collective-permute-start.3) | collective-permute-done | bytes 32800 | tf_op jit(solution)/shard_map/ppermute | solution.py:25
  38.6 1.6 collective-permute-start.4
  40.2 6.0 %collective-permute-done.4 = bf16[16,1024]{1,0:T(8,128)(2,1)S(1)} collective-permute-done((bf16[16,1024]{1,0:T(8,128)(2,1)S(1)}, bf16[16,1024]{1,0:T(8,128)(2,1)S(1)}, u32[]{:S(2)}, u32[]{:S(2)}) %collective-permute-start.4) | collective-permute-done | bytes 32800 | tf_op jit(solution)/shard_map/ppermute | solution.py:25
  46.3 2.6 %pad_maximum_fusion.refs_0_ = bf16[768,1024]{1,0:T(8,128)(2,1)} fusion(bf16[256,1024]{1,0:T(8,128)(2,1)} %collective-permute-done.1, bf16[256,1024]{1,0:T(8,128)(2,1)} %collective-permute-done, bf16[256,1024]{1,0:T(8,128)(2,1)S(1)} %copy-done.1), kind=kLoop, calls=%fused_computation | loop fusion | flops 4718592 | bytes 3145728 | tf_op jit(solution)/shard_map/concatenate | solution.py:404
  48.8 0.5 collective-permute-start.2
  49.3 11.2 %all-gather.3.cloned.1.call-done = bf16[1024,1024]{1,0:T(8,128)(2,1)} async-done(((bf16[256,1024]{1,0:T(8,128)(2,1)}), bf16[1024,1024]{1,0:T(8,128)(2,1)}) %all-gather.3.cloned.1.call-update) | async-done | bytes 2097168 | tf_op jit(solution)/shard_map/all_gather | solution.py:390
  60.6 1.1 collective-permute-start.7
  61.7 0.5 collective-permute-start.6
  62.2 1.1 slice.13
  63.3 1.0 slice.12
  64.3 1.5 collective-permute-start.8
  65.8 0.9 pad_maximum_fusion.2
  66.7 1.5 collective-permute-start.9
  68.2 1.1 dynamic-slice_bitcast_fusion
  69.3 0.8 pad_maximum_fusion.1
  70.2 15.2 %collective-permute-done.8 = bf16[128,1024]{1,0:T(8,128)(2,1)S(1)} collective-permute-done((bf16[128,1024]{1,0:T(8,128)(2,1)S(1)}, bf16[128,1024]{1,0:T(8,128)(2,1)S(1)}, u32[]{:S(2)}, u32[]{:S(2)}) %collective-permute-start.8) | collective-permute-done | bytes 262176 | tf_op jit(solution)/shard_map/ppermute | solution.py:25
  85.4 1.5 collective-permute-start.12
  86.9 0.5 collective-permute-start.11
  87.5 0.8 copy-done.6
  88.3 0.6 stack.55.slots_ref
  88.9 1.4 collective-permute-done.10.refs_3_
  90.3 9.5 %weight_terms.1 = bf16[1024,1024]{1,0:T(8,128)(2,1)} custom-call(s32[8]{0:T(128)} %stack.55.slots_ref, bf16[8,256,1024]{2,1,0:T(8,128)(2,1)} %all-to-all-done.swapped_ref, bf16[768,1024]{1,0:T(8,128)(2,1)} %pad_maximum_fusion.refs_0_, bf16[768,1024]{1,0:T(8,128)(2,1)} %copy-done, bf16[256,1024]{1,0:T(8,128)(2,1)} %copy-done.6, ...), custom_call_target="tpu_custom_call" | custom-call | flops 1 | bytes 1 | tf_op jit(solution)/shard_map/weight_terms/pallas_call | solution.py:111
  99.8 0.2 collective-permute-done.12
  100.0 1.2 collective-permute-done.11.refs_2_
  101.2 0.6 collective-permute-start.15
  101.8 0.6 collective-permute-start.14
  102.4 0.8 slice_maximum_fusion
  103.2 8.9 %consume.5 = (f32[256,1024]{1,0:T(8,128)}, f32[256,1024]{1,0:T(8,128)}, bf16[256,8192]{1,0:T(8,128)(2,1)}, bf16[4,256,256]{2,1,0:T(8,128)(2,1)}, bf16[1,256,256]{2,1,0:T(8,128)(2,1)}) custom-call(s32[4]{0:T(128)} %pad_add_fusion.core_ref.where_ref, f32[1]{0:T(128)} %bitcast.5.scale_ref, bf16[256,8192]{1,0:T(8,128)(2,1)} %hidden_ref.6, ...), custom_call_target="tpu_custom_call" | custom-call | flops 1 | bytes 1 | tf_op jit(solution)/shard_map/consume/pallas_call | solution.py:235
  112.1 1.5 collective-permute-start.13
  113.6 0.6 maximum_reduce_fusion
  114.9 1.6 collective-permute-start.17
  116.5 7.6 %consume.6 = (f32[256,1024]{1,0:T(8,128)}, f32[256,1024]{1,0:T(8,128)}, bf16[256,8192]{1,0:T(8,128)(2,1)}, bf16[4,256,256]{2,1,0:T(8,128)(2,1)}) custom-call(s32[4]{0:T(128)} %pad_add_fusion.core_ref.where_ref, f32[1]{0:T(128)} %bitcast.5.scale_ref, bf16[256,8192]{1,0:T(8,128)(2,1)} %hidden_ref.6, ...), custom_call_target="tpu_custom_call", output_to_operand_aliasing={{0}: (10, {}), {2}: (12, {}), {1}: (11, {})} | custom-call | flops 1 | bytes 1 | tf_op jit(solution)/shard_map/consume/pallas_call | solution.py:235
  124.1 1.1 collective-permute-start.23
  125.1 0.1 collective-permute-start.24
  125.2 1.6 collective-permute-done.13.refs_5_
  126.8 2.5 %collective-permute-done.17.refs_4_ = bf16[256,1024]{1,0:T(8,128)(2,1)} collective-permute-done((bf16[256,1024]{1,0:T(8,128)(2,1)}, bf16[256,1024]{1,0:T(8,128)(2,1)}, u32[]{:S(2)}, u32[]{:S(2)}) %collective-permute-start.17) | collective-permute-done | bytes 524320 | tf_op jit(solution)/shard_map/ppermute | solution.py:25
  129.4 1.5 collective-permute-start.22
  130.9 1.9 %slice.14.refs_3_ = bf16[256,1024]{1,0:T(8,128)(2,1)} slice(bf16[272,1024]{1,0:T(8,128)(2,1)} %collective-permute-done.12), slice={[0:256], [0:1024]} | slice | bytes 1048576 | tf_op jit(solution)/shard_map/slice | solution.py:429
  132.8 0.7 copy-done.9
  133.4 7.6 %consume.7 = (f32[256,1024]{1,0:T(8,128)}, f32[256,1024]{1,0:T(8,128)}, bf16[256,8192]{1,0:T(8,128)(2,1)}, bf16[4,256,256]{2,1,0:T(8,128)(2,1)}) custom-call(s32[4]{0:T(128)} %pad_add_fusion.core_ref.where_ref, f32[1]{0:T(128)} %bitcast.5.scale_ref, bf16[256,8192]{1,0:T(8,128)(2,1)} %hidden_ref.6, ...), custom_call_target="tpu_custom_call", output_to_operand_aliasing={{0}: (10, {}), {2}: (12, {}), {1}: (11, {})} | custom-call | flops 1 | bytes 1 | tf_op jit(solution)/shard_map/consume/pallas_call | solution.py:235
  141.0 0.7 collective-permute-start.20
  141.7 5.1 %consume.8 = (f32[256,1024]{1,0:T(8,128)}, f32[256,1024]{1,0:T(8,128)}, bf16[256,8192]{1,0:T(8,128)(2,1)}, bf16[1,256,256]{2,1,0:T(8,128)(2,1)}) custom-call(s32[4]{0:T(128)} %pad_add_fusion.core_ref.where_ref, f32[1]{0:T(128)} %bitcast.5.scale_ref, bf16[256,8192]{1,0:T(8,128)(2,1)} %hidden_ref.6, ...), custom_call_target="tpu_custom_call", output_to_operand_aliasing={{0}: (7, {}), {2}: (9, {}), {1}: (8, {})} | custom-call | flops 1 | bytes 1 | tf_op jit(solution)/shard_map/consume/pallas_call | solution.py:235
  146.8 1.1 multiply_convert_fusion
  148.0 0.6 collective-permute-start.29
  148.6 7.1 %collective-permute-done.20.refs_0_ = bf16[256,1024]{1,0:T(8,128)(2,1)} collective-permute-done((bf16[256,1024]{1,0:T(8,128)(2,1)}, bf16[256,1024]{1,0:T(8,128)(2,1)}, u32[]{:S(2)}, u32[]{:S(2)}) %collective-permute-start.20) | collective-permute-done | bytes 524320 | tf_op jit(solution)/shard_map/ppermute | solution.py:25
  155.8 4.6 %consume.9 = (f32[256,1024]{1,0:T(8,128)}, bf16[256,1024]{1,0:T(8,128)(2,1)}, bf16[256,8192]{1,0:T(8,128)(2,1)}, bf16[1,256,256]{2,1,0:T(8,128)(2,1)}) custom-call(s32[4]{0:T(128)} %pad_add_fusion.core_ref.where_ref, f32[1]{0:T(128)} %bitcast.5.scale_ref, bf16[256,8192]{1,0:T(8,128)(2,1)} %hidden_ref.6, ...), custom_call_target="tpu_custom_call", output_to_operand_aliasing={{0}: (7, {}), {2}: (9, {})} | custom-call | flops 1 | bytes 1 | tf_op jit(solution)/shard_map/consume/pallas_call | solution.py:235
  160.4 0.6 collective-permute-start.25
  161.0 0.1 collective-permute-start.27
  161.0 1.6 collective-permute-done.27.refs_5_
  162.7 0.4 collective-permute-start.28
  163.1 1.2 collective-permute-done.28.refs_6_
  164.3 0.7 copy-done.8
  164.9 4.6 %finish.1 = (bf16[256,8192]{1,0:T(8,128)(2,1)}, bf16[256,1024]{1,0:T(8,128)(2,1)}) custom-call(s32[4]{0:T(128)} %pad_add_fusion.core_ref.where_ref, f32[1]{0:T(128)} %bitcast.5.scale_ref, bf16[256,8192]{1,0:T(8,128)(2,1)} %hidden_ref.6, bf16[256,1024]{1,0:T(8,128)(2,1)} %cot_ref.1, ...), custom_call_target="tpu_custom_call", output_to_operand_aliasing={{0}: (11, {})} | custom-call | flops 1 | bytes 1 | tf_op jit(solution)/shard_map/finish/pallas_call | solution.py:330
  169.6 2.3 %join.1 = bf16[512,1024]{1,0:T(8,128)(2,1)} custom-call(s32[4]{0:T(128)} %pad_add_fusion.core_ref.where_ref, bf16[272,1024]{1,0:T(8,128)(2,1)} %copy-done.5, bf16[272,1024]{1,0:T(8,128)(2,1)} %collective-permute-done.29.theirs_ref), custom_call_target="tpu_custom_call" | custom-call | tf_op jit(solution)/shard_map/join/pallas_call | solution.py:365
  (57 shorter events, 0.3 us)
Async XLA Ops:
  7.2 3.2 %copy-start.1 = (bf16[256,1024]{1,0:T(8,128)(2,1)S(1)}, bf16[256,1024]{1,0:T(8,128)(2,1)}, u32[]{:S(2)}) copy-start(bf16[256,1024]{1,0:T(8,128)(2,1)} %cot_ref.1) | copy-start | bytes 1572868
  7.2 53.4 %all-gather.3.cloned.1.call-start = ((), (), s32[]{:S(2)}) async-start(), calls=%async_computation.3 | async-start | bytes 2621440 | tf_op jit(solution)/shard_map/all_gather | solution.py:390
  10.4 15.1 %collective-permute-start.1 = (bf16[256,1024]{1,0:T(8,128)(2,1)S(1)}, bf16[256,1024]{1,0:T(8,128)(2,1)}, u32[]{:S(2)}, u32[]{:S(2)}) collective-permute-start(bf16[256,1024]{1,0:T(8,128)(2,1)S(1)} %copy-done.1), channel_id=1, source_target_pairs={{0,16},{16,0},{1,17},{17,1},{2,18},{18,2},{3,19},{19,3},{4,20},{20... | collective-permute-start | bytes 1572872 | tf_op jit(solution)/shard_map/ppermute | solution.py:25
  13.4 13.5 %collective-permute-start = (bf16[256,1024]{1,0:T(8,128)(2,1)S(1)}, bf16[256,1024]{1,0:T(8,128)(2,1)}, u32[]{:S(2)}, u32[]{:S(2)}) collective-permute-start(bf16[256,1024]{1,0:T(8,128)(2,1)S(1)} %copy-done.1), channel_id=1, source_target_pairs={{0,2},{2,0},{1,3},{3,1},{4,6},{6,4},{5,7},{7,5},{8,10},{10,8},{9,1... | collective-permute-start | bytes 1572872 | tf_op jit(solution)/shard_map/ppermute | solution.py:25
  26.9 4.8 %copy-start.4 = (bf16[512,1024]{1,0:T(8,128)(2,1)S(1)}, bf16[512,1024]{1,0:T(8,128)(2,1)}, u32[]{:S(2)}) copy-start(bf16[512,1024]{1,0:T(8,128)(2,1)} %param.5) | copy-start | bytes 3145732
  26.9 62.0 %all-to-all-start = ((bf16[8,256,1024]{2,1,0:T(8,128)(2,1)}), bf16[8,256,1024]{2,1,0:T(8,128)(2,1)}, u32[]{:S(2)}, u32[]{:S(2)}) async-start(bf16[8,256,1024]{2,1,0:T(8,128)(2,1)} %get-tuple-element.86), calls=%async_computation | async-start | bytes 8388608 | tf_op jit(solution)/shard_map/all_to_all | solution.py:397
  31.6 115.2 %reduce-scatter.2.cloned.1.call-start = ((), (), s32[]{:S(2)}) async-start(), calls=%async_computation.2 | async-start | bytes 2621440 | tf_op jit(solution)/shard_map/reduce_scatter | solution.py:430
  31.8 6.7 %collective-permute-start.3 = (bf16[16,1024]{1,0:T(8,128)(2,1)S(1)}, bf16[16,1024]{1,0:T(8,128)(2,1)S(1)}, u32[]{:S(2)}, u32[]{:S(2)}) collective-permute-start(bf16[16,1024]{1,0:T(8,128)(2,1)S(1)} %broadcast_in_dim.2), channel_id=1, source_target_pairs={{0,4},{4,0},{8,12},{12,8},{1,5},{5,1},{9,13},{13,9},{2,6},{6,2},{1... | collective-permute-start | bytes 98312 | tf_op jit(solution)/shard_map/ppermute | solution.py:25
  38.6 7.7 %collective-permute-start.4 = (bf16[16,1024]{1,0:T(8,128)(2,1)S(1)}, bf16[16,1024]{1,0:T(8,128)(2,1)S(1)}, u32[]{:S(2)}, u32[]{:S(2)}) collective-permute-start(bf16[16,1024]{1,0:T(8,128)(2,1)S(1)} %broadcast_maximum_fusion), channel_id=1, source_target_pairs={{0,8},{4,12},{8,0},{12,4},{1,9},{5,13},{9,1},{13,5},{2,10},{6,14},... | collective-permute-start | bytes 98312 | tf_op jit(solution)/shard_map/ppermute | solution.py:25
  46.3 19.6 %copy-start.2 = (bf16[256,1024]{1,0:T(8,128)(2,1)S(1)}, bf16[256,1024]{1,0:T(8,128)(2,1)}, u32[]{:S(2)}) copy-start(bf16[256,1024]{1,0:T(8,128)(2,1)} %get-tuple-element.92.refs_2_) | copy-start | bytes 1572868
  48.8 17.9 %collective-permute-start.5 = (bf16[768,1024]{1,0:T(8,128)(2,1)}, bf16[768,1024]{1,0:T(8,128)(2,1)S(1)}, u32[]{:S(2)}, u32[]{:S(2)}) collective-permute-start(bf16[768,1024]{1,0:T(8,128)(2,1)} %pad_maximum_fusion.refs_0_), channel_id=1, source_target_pairs={{0,1},{1,0},{2,3},{3,2},{4,5},{5,4},{6,7},{7,6},{8,9},{9,8},{10,11... | collective-permute-start | bytes 4718600 | tf_op jit(solution)/shard_map/ppermute | solution.py:25
  48.8 40.1 %collective-permute-start.2 = (bf16[8,256,512]{2,1,0:T(8,128)(2,1)}, bf16[8,256,512]{2,1,0:T(8,128)(2,1)}, u32[]{:S(2)}, u32[]{:S(2)}) collective-permute-start(bf16[8,256,512]{2,1,0:T(8,128)(2,1)} %get-tuple-element.87), channel_id=1, source_target_pairs={{0,1},{1,0},{2,3},{3,2},{4,5},{5,4},{6,7},{7,6},{8,9},{9,8},{10,11... | collective-permute-start | bytes 6291464 | tf_op jit(solution)/shard_map/ppermute | solution.py:25
  60.6 26.9 %collective-permute-start.7 = (bf16[256,1024]{1,0:T(8,128)(2,1)}, bf16[256,1024]{1,0:T(8,128)(2,1)}, u32[]{:S(2)}, u32[]{:S(2)}) collective-permute-start(bf16[256,1024]{1,0:T(8,128)(2,1)} %get-tuple-element.97.refs_3_), channel_id=1, source_target_pairs={{0,8},{4,12},{8,0},{12,4},{1,9},{5,13},{9,1},{13,5},{2,10},{6,14},... | collective-permute-start | bytes 1572872 | tf_op jit(solution)/shard_map/ppermute | solution.py:25
  61.7 25.8 %collective-permute-start.6 = (bf16[256,1024]{1,0:T(8,128)(2,1)}, bf16[256,1024]{1,0:T(8,128)(2,1)}, u32[]{:S(2)}, u32[]{:S(2)}) collective-permute-start(bf16[256,1024]{1,0:T(8,128)(2,1)} %get-tuple-element.97.refs_3_), channel_id=1, source_target_pairs={{0,4},{4,0},{8,12},{12,8},{1,5},{5,1},{9,13},{13,9},{2,6},{6,2},{1... | collective-permute-start | bytes 1572872 | tf_op jit(solution)/shard_map/ppermute | solution.py:25
  62.2 6.0 %copy-start.3 = (bf16[1024,1024]{1,0:T(8,128)(2,1)S(1)}, bf16[1024,1024]{1,0:T(8,128)(2,1)}, u32[]{:S(2)}) copy-start(bf16[1024,1024]{1,0:T(8,128)(2,1)} %all-gather.3.cloned.1.call-done) | copy-start | bytes 6291460
  64.3 21.1 %collective-permute-start.8 = (bf16[128,1024]{1,0:T(8,128)(2,1)S(1)}, bf16[128,1024]{1,0:T(8,128)(2,1)S(1)}, u32[]{:S(2)}, u32[]{:S(2)}) collective-permute-start(bf16[128,1024]{1,0:T(8,128)(2,1)S(1)} %slice.12), channel_id=1, source_target_pairs={{0,2},{2,0},{1,3},{3,1},{4,6},{6,4},{5,7},{7,5},{8,10},{10,8},{9,1... | collective-permute-start | bytes 786440 | tf_op jit(solution)/shard_map/ppermute | solution.py:25
  66.7 3.5 %copy-start = (bf16[768,1024]{1,0:T(8,128)(2,1)}, bf16[768,1024]{1,0:T(8,128)(2,1)S(1)}, u32[]{:S(2)}) copy-start(bf16[768,1024]{1,0:T(8,128)(2,1)S(1)} %collective-permute-done.5.refs_1_) | copy-start | bytes 4718596
  66.7 20.2 %collective-permute-start.9 = (bf16[128,1024]{1,0:T(8,128)(2,1)S(1)}, bf16[128,1024]{1,0:T(8,128)(2,1)S(1)}, u32[]{:S(2)}, u32[]{:S(2)}) collective-permute-start(bf16[128,1024]{1,0:T(8,128)(2,1)S(1)} %slice.13), channel_id=1, source_target_pairs={{0,16},{16,0},{1,17},{17,1},{2,18},{18,2},{3,19},{19,3},{4,20},{20... | collective-permute-start | bytes 786440 | tf_op jit(solution)/shard_map/ppermute | solution.py:25
  85.4 14.6 %collective-permute-start.12 = (bf16[272,1024]{1,0:T(8,128)(2,1)}, bf16[272,1024]{1,0:T(8,128)(2,1)}, u32[]{:S(2)}, u32[]{:S(2)}) collective-permute-start(bf16[272,1024]{1,0:T(8,128)(2,1)} %pad_maximum_fusion.1), channel_id=1, source_target_pairs={{0,16},{16,0},{1,17},{17,1},{2,18},{18,2},{3,19},{19,3},{4,20},{20... | collective-permute-start | bytes 1671176 | tf_op jit(solution)/shard_map/ppermute | solution.py:25
  86.9 14.3 %collective-permute-start.11 = (bf16[272,1024]{1,0:T(8,128)(2,1)}, bf16[272,1024]{1,0:T(8,128)(2,1)}, u32[]{:S(2)}, u32[]{:S(2)}) collective-permute-start(bf16[272,1024]{1,0:T(8,128)(2,1)} %pad_maximum_fusion.2), channel_id=1, source_target_pairs={{0,2},{2,0},{1,3},{3,1},{4,6},{6,4},{5,7},{7,5},{8,10},{10,8},{9,1... | collective-permute-start | bytes 1671176 | tf_op jit(solution)/shard_map/ppermute | solution.py:25
  87.5 0.8 copy-start.6
  88.3 2.0 %collective-permute-start.10 = (bf16[256,1024]{1,0:T(8,128)(2,1)S(1)}, bf16[256,1024]{1,0:T(8,128)(2,1)}, u32[]{:S(2)}, u32[]{:S(2)}) collective-permute-start(bf16[256,1024]{1,0:T(8,128)(2,1)S(1)} %constant_dynamic-update-slice_fusion.refs_2_), channel_id=1, source_target_pairs={{0,1},{1,0},{2,3},{3,2},{4,5},{5,4},{6,7},{7,6},{8,9},{9,8},{10,11... | collective-permute-start | bytes 1572872 | tf_op jit(solution)/shard_map/ppermute | solution.py:25
  101.2 13.7 %collective-permute-start.15 = (bf16[272,1024]{1,0:T(8,128)(2,1)}, bf16[272,1024]{1,0:T(8,128)(2,1)}, u32[]{:S(2)}, u32[]{:S(2)}) collective-permute-start(bf16[272,1024]{1,0:T(8,128)(2,1)} %collective-permute-done.11.refs_2_), channel_id=1, source_target_pairs={{0,16},{16,0},{1,17},{17,1},{2,18},{18,2},{3,19},{19,3},{4,20},{20... | collective-permute-start | bytes 1671176 | tf_op jit(solution)/shard_map/ppermute | solution.py:25
  101.8 13.1 %collective-permute-start.14 = (bf16[256,1024]{1,0:T(8,128)(2,1)}, bf16[256,1024]{1,0:T(8,128)(2,1)}, u32[]{:S(2)}, u32[]{:S(2)}) collective-permute-start(bf16[256,1024]{1,0:T(8,128)(2,1)} %get-tuple-element.112), channel_id=1, source_target_pairs={{0,2},{2,0},{1,3},{3,1},{4,6},{6,4},{5,7},{7,5},{8,10},{10,8},{9,1... | collective-permute-start | bytes 1572872 | tf_op jit(solution)/shard_map/ppermute | solution.py:25
  103.2 10.5 %collective-permute-start.16 = (bf16[16,1024]{1,0:T(8,128)(2,1)S(1)}, bf16[16,1024]{1,0:T(8,128)(2,1)S(1)}, u32[]{:S(2)}, u32[]{:S(2)}) collective-permute-start(bf16[16,1024]{1,0:T(8,128)(2,1)S(1)} %slice_maximum_fusion), channel_id=1, source_target_pairs={{0,1},{1,0},{2,3},{3,2},{4,5},{5,4},{6,7},{7,6},{8,9},{9,8},{10,11... | collective-permute-start | bytes 98312 | tf_op jit(solution)/shard_map/ppermute | solution.py:25
  112.1 14.7 %collective-permute-start.13 = (bf16[256,1024]{1,0:T(8,128)(2,1)}, bf16[256,1024]{1,0:T(8,128)(2,1)}, u32[]{:S(2)}, u32[]{:S(2)}) collective-permute-start(bf16[256,1024]{1,0:T(8,128)(2,1)} %get-tuple-element.111), channel_id=1, source_target_pairs={{0,2},{2,0},{1,3},{3,1},{4,6},{6,4},{5,7},{7,5},{8,10},{10,8},{9,1... | collective-permute-start | bytes 1572872 | tf_op jit(solution)/shard_map/ppermute | solution.py:25
  114.9 14.4 %collective-permute-start.17 = (bf16[256,1024]{1,0:T(8,128)(2,1)}, bf16[256,1024]{1,0:T(8,128)(2,1)}, u32[]{:S(2)}, u32[]{:S(2)}) collective-permute-start(bf16[256,1024]{1,0:T(8,128)(2,1)} %collective-permute-done.14.refs_4_), channel_id=1, source_target_pairs={{0,16},{16,0},{1,17},{17,1},{2,18},{18,2},{3,19},{19,3},{4,20},{20... | collective-permute-start | bytes 1572872 | tf_op jit(solution)/shard_map/ppermute | solution.py:25
  116.5 14.4 %copy-start.10 = (bf16[1,256,256]{2,1,0:T(8,128)(2,1)S(1)}, bf16[1,256,256]{2,1,0:T(8,128)(2,1)}, u32[]{:S(2)}) copy-start(bf16[1,256,256]{2,1,0:T(8,128)(2,1)} %get-tuple-element.136) | copy-start | bytes 393220
  116.5 16.3 %collective-permute-start.18 = (bf16[4,256,256]{2,1,0:T(8,128)(2,1)}, bf16[4,256,256]{2,1,0:T(8,128)(2,1)}, u32[]{:S(2)}, u32[]{:S(2)}) collective-permute-start(bf16[4,256,256]{2,1,0:T(8,128)(2,1)} %get-tuple-element.135), channel_id=1, source_target_pairs={{0,1},{1,0},{2,3},{3,2},{4,5},{5,4},{6,7},{7,6},{8,9},{9,8},{10,11... | collective-permute-start | bytes 1572872 | tf_op jit(solution)/shard_map/ppermute | solution.py:25
  124.1 17.6 %collective-permute-start.23 = (bf16[256,1024]{1,0:T(8,128)(2,1)S(1)}, bf16[256,1024]{1,0:T(8,128)(2,1)}, u32[]{:S(2)}, u32[]{:S(2)}) collective-permute-start(bf16[256,1024]{1,0:T(8,128)(2,1)S(1)} %get-tuple-element.142), channel_id=1, source_target_pairs={{0,2},{2,0},{1,3},{3,1},{4,6},{6,4},{5,7},{7,5},{8,10},{10,8},{9,1... | collective-permute-start | bytes 1572872 | tf_op jit(solution)/shard_map/ppermute | solution.py:25
  125.1 16.6 %collective-permute-start.24 = (bf16[4,256,256]{2,1,0:T(8,128)(2,1)}, bf16[4,256,256]{2,1,0:T(8,128)(2,1)}, u32[]{:S(2)}, u32[]{:S(2)}) collective-permute-start(bf16[4,256,256]{2,1,0:T(8,128)(2,1)} %get-tuple-element.146), channel_id=1, source_target_pairs={{0,1},{1,0},{2,3},{3,2},{4,5},{5,4},{6,7},{7,6},{8,9},{9,8},{10,11... | collective-permute-start | bytes 1572872 | tf_op jit(solution)/shard_map/ppermute | solution.py:25
  129.4 17.4 %collective-permute-start.22 = (bf16[256,1024]{1,0:T(8,128)(2,1)}, bf16[256,1024]{1,0:T(8,128)(2,1)}, u32[]{:S(2)}, u32[]{:S(2)}) collective-permute-start(bf16[256,1024]{1,0:T(8,128)(2,1)} %collective-permute-done.13.refs_5_), channel_id=1, source_target_pairs={{0,16},{16,0},{1,17},{17,1},{2,18},{18,2},{3,19},{19,3},{4,20},{20... | collective-permute-start | bytes 1572872 | tf_op jit(solution)/shard_map/ppermute | solution.py:25
  130.9 1.9 %collective-permute-start.19 = (bf16[1,256,256]{2,1,0:T(8,128)(2,1)S(1)}, bf16[1,256,256]{2,1,0:T(8,128)(2,1)S(1)}, u32[]{:S(2)}, u32[]{:S(2)}) collective-permute-start(bf16[1,256,256]{2,1,0:T(8,128)(2,1)S(1)} %copy-done.10), channel_id=1, source_target_pairs={{0,1},{1,0},{2,3},{3,2},{4,5},{5,4},{6,7},{7,6},{8,9},{9,8},{10,11... | collective-permute-start | bytes 393224 | tf_op jit(solution)/shard_map/ppermute | solution.py:25
  132.7 0.7 copy-start.9
  141.0 14.8 %collective-permute-start.20 = (bf16[256,1024]{1,0:T(8,128)(2,1)}, bf16[256,1024]{1,0:T(8,128)(2,1)}, u32[]{:S(2)}, u32[]{:S(2)}) collective-permute-start(bf16[256,1024]{1,0:T(8,128)(2,1)} %slice.14.refs_3_), channel_id=1, source_target_pairs={{0,2},{2,0},{1,3},{3,1},{4,6},{6,4},{5,7},{7,5},{8,10},{10,8},{9,1... | collective-permute-start | bytes 1572872 | tf_op jit(solution)/shard_map/ppermute | solution.py:25
  148.0 12.3 %copy-start.5 = (bf16[272,1024]{1,0:T(8,128)(2,1)}, bf16[272,1024]{1,0:T(8,128)(2,1)S(1)}, u32[]{:S(2)}) copy-start(bf16[272,1024]{1,0:T(8,128)(2,1)S(1)} %pad.4.mine_ref) | copy-start | bytes 1671172
  148.0 21.5 %collective-permute-start.29 = (bf16[272,1024]{1,0:T(8,128)(2,1)S(1)}, bf16[272,1024]{1,0:T(8,128)(2,1)}, u32[]{:S(2)}, u32[]{:S(2)}) collective-permute-start(bf16[272,1024]{1,0:T(8,128)(2,1)S(1)} %pad.4.mine_ref), channel_id=1, source_target_pairs={{0,16},{16,0},{1,17},{17,1},{2,18},{18,2},{3,19},{19,3},{4,20},{20... | collective-permute-start | bytes 1671176 | tf_op jit(solution)/shard_map/ppermute | solution.py:25
  148.6 12.3 %copy-start.11 = (bf16[1,256,256]{2,1,0:T(8,128)(2,1)S(1)}, bf16[1,256,256]{2,1,0:T(8,128)(2,1)}, u32[]{:S(2)}) copy-start(bf16[1,256,256]{2,1,0:T(8,128)(2,1)} %get-tuple-element.157) | copy-start | bytes 393220
  148.6 14.4 %collective-permute-start.26 = (bf16[4,256,256]{2,1,0:T(8,128)(2,1)}, bf16[4,256,256]{2,1,0:T(8,128)(2,1)}, u32[]{:S(2)}, u32[]{:S(2)}) collective-permute-start(bf16[4,256,256]{2,1,0:T(8,128)(2,1)} %get-tuple-element.156), channel_id=1, source_target_pairs={{0,1},{1,0},{2,3},{3,2},{4,5},{5,4},{6,7},{7,6},{8,9},{9,8},{10,11... | collective-permute-start | bytes 1572872 | tf_op jit(solution)/shard_map/ppermute | solution.py:25
  155.8 7.3 %collective-permute-start.21 = (bf16[256,1024]{1,0:T(8,128)(2,1)}, bf16[256,1024]{1,0:T(8,128)(2,1)}, u32[]{:S(2)}, u32[]{:S(2)}) collective-permute-start(bf16[256,1024]{1,0:T(8,128)(2,1)} %collective-permute-done.20.refs_0_), channel_id=1, source_target_pairs={{0,1},{1,0},{2,3},{3,2},{4,5},{5,4},{6,7},{7,6},{8,9},{9,8},{10,11... | collective-permute-start | bytes 1572872 | tf_op jit(solution)/shard_map/ppermute | solution.py:25
  160.4 3.9 %collective-permute-start.25 = (bf16[256,1024]{1,0:T(8,128)(2,1)}, bf16[256,1024]{1,0:T(8,128)(2,1)}, u32[]{:S(2)}, u32[]{:S(2)}) collective-permute-start(bf16[256,1024]{1,0:T(8,128)(2,1)} %get-tuple-element.155), channel_id=1, source_target_pairs={{0,1},{1,0},{2,3},{3,2},{4,5},{5,4},{6,7},{7,6},{8,9},{9,8},{10,11... | collective-permute-start | bytes 1572872 | tf_op jit(solution)/shard_map/ppermute | solution.py:25
  161.0 1.7 collective-permute-start.27
  162.7 1.6 copy-start.7
  162.7 1.6 collective-permute-start.28
  164.3 0.7 copy-start.8
Sparse Core Ops, SparseCore 0:
  10.5 49.9 all-gather.2
  101.4 43.2 reduce-scatter.1
